TPU v7x, 128 devices: a whole 4x4x4 slice. The times are simulated.
128 devices in a mesh: row: 8 (over y, core), col: 16 (over x, z).
Axes of the slice: x: 4, y: 4, z: 4, core: 2. Of those that a mesh axis runs over, the one named last changes fastest.
Arguments:
- amplitudes: bfloat16 [8192, 32768], P('row', 'col'), may hold values from -6 to 6
- t2_mask: int32 [128, 512], P('row', 'col'), may hold values 0 or 1
- eri_tiles: bfloat16 [40960, 4096], P(('row', 'col')), may hold values from -0.046875 to 0.046875
- eri_slot: int32 [32768], replicated, may hold values from -1 to 40959, as said below
Outputs:
- cycle_term: float32 [4096, 8192], P('col', 'row')
Inputs may be any that keep to these rules, and one draw needn't show every extreme that they name: `eri_slot`: different tiles have different slots. For each col index g, of the tiles whose virtual tile c lies in [g * 2, (g + 1) * 2), at most 20 have slots on one device (slots s with s // 320 equal), and exactly 20 on some device.
All inputs are finite; a program needn't handle non-finite values. No bound on the sum of `t2_mask` on one device may be relied on, other than what follows from the above.
Results may differ from a plain program's by a relative error of at most 0.0003.
Values may be sent and summed in bfloat16 or wider, within the bound.
No kernel may reach another device: no remote copies, remote signals or barrier semaphores. Data moves between devices by JAX's collectives and lax.ppermute only.
A program may use at most 192 MiB of HBM per device.

v0:
```python
import jax
import jax.numpy as jnp
from jax import lax
from jax.sharding import PartitionSpec as P

TILE = 64
VTILES = 32
KOCC = 16
JOCC = 2


def shards(amplitudes, t2_mask, eri_tiles, eri_slot):
    n_row = lax.axis_size("row")
    n_col = lax.axis_size("col")
    devices = n_row * n_col
    col_index = lax.axis_index("col")
    myself = lax.axis_index("row") * n_col + col_index
    rows_dev, depth_dev = amplitudes.shape
    slots_dev = eri_tiles.shape[0]
    capacity = slots_dev // n_col
    ct_dev = VTILES // n_col
    need = ct_dev * KOCC * VTILES * JOCC
    blocks = amplitudes.reshape(rows_dev // TILE, TILE, depth_dev // TILE, TILE)
    masked = (blocks * t2_mask[:, None, :, None].astype(jnp.bfloat16)).reshape(
        rows_dev, ct_dev * KOCC, TILE
    )
    owner_all = jnp.where(eri_slot >= 0, eri_slot // slots_dev, -1).reshape(n_col, need)
    mine = (owner_all == myself).astype(jnp.int32)
    send_rank = jnp.cumsum(mine, axis=1) - 1
    group_ids = jnp.arange(n_col, dtype=jnp.int32)[:, None]
    target = jnp.where(mine > 0, group_ids * capacity + send_rank, n_col * capacity).reshape(-1)
    local_slot = jnp.clip(eri_slot - myself * slots_dev, 0, slots_dev - 1)
    send_index = (
        jnp.full((n_col * capacity,), slots_dev, jnp.int32).at[target].set(local_slot, mode="drop")
    )
    stored = jnp.concatenate([eri_tiles, jnp.zeros((1, TILE * TILE), eri_tiles.dtype)], axis=0)
    outgoing = stored[send_index].reshape(n_col, capacity, TILE * TILE)
    spread = jnp.broadcast_to(outgoing[None], (n_row, n_col, capacity, TILE * TILE)).reshape(
        devices, capacity, TILE * TILE
    )
    received = lax.all_to_all(spread, ("row", "col"), split_axis=0, concat_axis=0, tiled=True)
    wanted = lax.dynamic_slice_in_dim(eri_slot, col_index * need, need)
    wanted_owner = jnp.where(wanted >= 0, wanted // slots_dev, -1)
    owner_onehot = (wanted_owner[:, None] == jnp.arange(devices, dtype=jnp.int32)[None, :]).astype(
        jnp.int32
    )
    recv_rank = jnp.sum((jnp.cumsum(owner_onehot, axis=0) - 1) * owner_onehot, axis=1)
    pool_index = jnp.where(
        wanted < 0, devices * capacity, jnp.maximum(wanted_owner, 0) * capacity + recv_rank
    )
    tile_index = pool_index.reshape(ct_dev * KOCC, VTILES * JOCC)
    tile_pool = jnp.concatenate(
        [
            received.reshape(devices * capacity, TILE * TILE),
            jnp.zeros((1, TILE * TILE), received.dtype),
        ],
        axis=0,
    )
    tiles = tile_pool[tile_index].reshape(
        ct_dev * KOCC, VTILES * JOCC * TILE // n_col * lax.axis_size("col") // TILE, TILE, TILE
    )
    product = lax.dot_general(
        tiles, masked, (((0, 2), (1, 2)), ((), ())), preferred_element_type=jnp.float32
    )
    return lax.psum_scatter(
        product.reshape(VTILES * JOCC * TILE // n_col * lax.axis_size("col"), rows_dev),
        "col",
        scatter_dimension=0,
        tiled=True,
    )


def solution(mesh):
    in_specs = (P("row", "col"), P("row", "col"), P(("row", "col"), None), P())
    out_specs = P("col", "row")
    return jax.shard_map(shards, mesh=mesh, in_specs=in_specs, out_specs=out_specs, check_vma=False)
```

profile of v0, /device:TPU:6, one launch (start us, length us, event | category | flops | bytes accessed | tf_op | source)
XLA Modules:
  0.0 888.3 jit_solution(5275527552177851328)
XLA Ops:
  6.5 1.0 fusion.7
  7.6 4.5 reduce-window.14
  12.9 1.1 compare_select_fusion
  14.0 120.0 %scatter_custom_fusion = s32[320]{0:T(512)S(1)} fusion(s32[32768]{0:T(1024)S(1)} %get-tuple-element.5, s32[32768]{0:T(1024)S(1)} %get-tuple-element.6, s32[]{:T(128)} %constant.18.clone.1), kind=kCustom, calls=%fused_computation.36 | custom fusion | bytes 1284 | tf_op jit(solution)/shard_map/scatter | solution.py:34
  134.0 2.0 concatenate.6
  136.0 3.9 gather_fusion
  139.9 2.7 broadcast_in_dim.34
  142.6 8.5 broadcast_in_dim.35
  151.1 10.9 %all-to-all-start = ((bf16[128,20,4096]{2,1,0:T(8,128)(2,1)}), bf16[128,20,4096]{2,1,0:T(8,128)(2,1)}, u32[]{:S(2)}, u32[]{:S(2)}) async-start(bf16[128,20,4096]{2,1,0:T(8,128)(2,1)} %bitcast.34), calls=%async_computation | async-start | bytes 50331648 | tf_op jit(solution)/shard_map/all_to_all | solution.py:41
  162.2 0.7 fusion.14
  163.9 0.7 fusion.8
  164.6 0.6 fusion
  165.2 0.7 add_select_fusion.2
  166.1 6.4 copy.11
  172.9 4.4 bitcast_multiply_fusion
  177.3 351.1 %all-to-all-done = bf16[128,20,4096]{2,1,0:T(8,128)(2,1)} async-done(((bf16[128,20,4096]{2,1,0:T(8,128)(2,1)}), bf16[128,20,4096]{2,1,0:T(8,128)(2,1)}, u32[]{:S(2)}, u32[]{:S(2)}) %all-to-all-start) | async-done | bytes 20971552 | tf_op jit(solution)/shard_map/all_to_all | solution.py:41
  528.4 26.5 %reshape.97 = bf16[2560,4096]{1,0:T(8,128)(2,1)} reshape(bf16[128,20,4096]{2,1,0:T(8,128)(2,1)} %all-to-all-done) | data formatting | bytes 41943040 | tf_op jit(solution)/shard_map/reshape | solution.py:54
  554.9 17.7 %concatenate.7 = bf16[2561,4096]{1,0:T(8,128)(2,1)} pad(bf16[2560,4096]{1,0:T(8,128)(2,1)} %reshape.97, bf16[]{:T(256)} %constant.17.clone.1), padding=0_1x0_0 | pad | bytes 41951232 | tf_op jit(solution)/shard_map/concatenate | solution.py:52
  572.6 38.3 %gather_fusion.1 = bf16[2048,4096]{1,0:T(8,128)(2,1)} fusion(bf16[2561,4096]{1,0:T(8,128)(2,1)} %concatenate.7, s32[2048]{0:T(1024)S(1)} %broadcast_clamp_fusion), kind=kCustom, calls=%fused_computation.1 | custom fusion | bytes 33562624 | tf_op jit(solution)/shard_map/gather | solution.py:59
  610.9 46.0 %reshape.100 = bf16[32,64,64,64]{3,2,1,0:T(8,128)(2,1)} reshape(bf16[2048,4096]{1,0:T(8,128)(2,1)} %gather_fusion.1) | data formatting | bytes 33554432 | tf_op jit(solution)/shard_map/reshape | solution.py:59
  656.9 29.2 %copy.9 = bf16[64,64,32,64]{1,0,3,2:T(8,128)(2,1)} copy(bf16[64,64,32,64]{1,3,0,2:T(8,128)(2,1)} %bitcast.33) | data formatting | bytes 33554432 | tf_op jit(solution)/shard_map/dot_general | solution.py:62
  686.2 44.1 %dot_general.8 = bf16[4096,32,64]{0,2,1:T(8,128)(2,1)} reshape(bf16[64,64,32,64]{1,0,3,2:T(8,128)(2,1)} %copy.9) | data formatting | bytes 33554432 | tf_op jit(solution)/shard_map/dot_general | solution.py:62
  730.2 23.7 %convolution_bitcast_fusion = f32[4096,1024]{1,0:T(8,128)} fusion(bf16[4096,32,64]{0,2,1:T(8,128)(2,1)} %dot_general.8, bf16[1024,32,64]{0,2,1:T(8,128)(2,1)} %bitcast.35), kind=kOutput, calls=%fused_computation.3 | convolution fusion | flops 17179869184 | bytes 37748736 | tf_op jit(solution)/shard_map/dot_general | solution.py:62
  754.0 127.5 %reduce-scatter.2.cloned.1.call-done = f32[256,1024]{1,0:T(8,128)} async-done(((f32[4096,1024]{1,0:T(8,128)}), f32[256,1024]{1,0:T(8,128)}) %reduce-scatter.2.cloned.1.call-update) | async-done | bytes 1048592 | tf_op jit(solution)/shard_map/reduce_scatter | solution.py:65
  (27 shorter events, 2.5 us)
Async XLA Ops:
  151.1 21.4 %copy-start = (s32[16,32]{1,0:T(8,128)S(1)}, s32[16,32]{1,0:T(8,128)}, u32[]{:S(2)}) copy-start(s32[16,32]{1,0:T(8,128)} %param.5) | copy-start | bytes 6148
  151.1 377.3 %all-to-all-start = ((bf16[128,20,4096]{2,1,0:T(8,128)(2,1)}), bf16[128,20,4096]{2,1,0:T(8,128)(2,1)}, u32[]{:S(2)}, u32[]{:S(2)}) async-start(bf16[128,20,4096]{2,1,0:T(8,128)(2,1)} %bitcast.34), calls=%async_computation | async-start | bytes 50331648 | tf_op jit(solution)/shard_map/all_to_all | solution.py:41
  162.0 719.5 %reduce-scatter.2.cloned.1.call-start = ((), (), s32[]{:S(2)}) async-start(), calls=%async_computation.2 | async-start | bytes 17825792 | tf_op jit(solution)/shard_map/reduce_scatter | solution.py:65
Sparse Core Ops, SparseCore 0:
  754.1 127.2 reduce-scatter.1
where the time goes:
time: 893 us; the launch traced here: 888 us
  waiting for transfers between devices  479 us (54%)
  local copies, waits for them, and re-layouts  347 us (39%)
  matrix products  23.7 us (3%)
  other arithmetic  14.6 us (2%)
  between operations  13.5 us (2%)
  starting transfers between devices  11.1 us (1%)
    all_to_all x1, waiting for transfers between devices, shards(): lax.all_to_all(spread, ('row', 'col'), split_axis=0, concat_axis=0, tiled...  351 us
    reduce_scatter x1, waiting for transfers between devices, shards(): lax.psum_scatter(product.reshape(VTILES * JOCC * TILE // n_col * lax.axis...  127 us
    scatter x1, local copies, waits for them, and re-layouts, shards(): jnp.full((n_col * capacity,), slots_dev, jnp.int32).at[target]  120 us
    dot_general x2, local copies, waits for them, and re-layouts, shards(): lax.dot_general(tiles, masked, (((0, 2), (1, 2)), ((), ())), preferred_el...  73.3 us
    reshape x1, local copies, waits for them, and re-layouts, shards(): tile_pool[tile_index]  46 us
    gather x1, local copies, waits for them, and re-layouts, shards(): tile_pool[tile_index]  38.3 us
    reshape x1, local copies, waits for them, and re-layouts, shards(): received.reshape(devices * capacity, TILE * TILE)  26.5 us
    dot_general x1, matrix products, shards(): lax.dot_general(tiles, masked, (((0, 2), (1, 2)), ((), ())), preferred_el...  23.7 us
  transfers between devices with their start and end apart: 2, of which 2 were waited for; matrix products, arithmetic and copies ran while one was open for 2% of the time, Pallas kernels for 0%

commit v1 on v0

v1 whole, which is shorter than its diff:
```python
import functools

import jax
import jax.numpy as jnp
from jax import lax
from jax.experimental import pallas as pl
from jax.experimental.pallas import tpu as pltpu
from jax.sharding import Mesh
from jax.sharding import PartitionSpec as P

TILE = 64
VTILES = 32
KOCC = 16
JOCC = 2
CAP = 20
COLS = 16
ROWS = 8
DEVS = 128
GROUP = VTILES * KOCC * VTILES * JOCC // COLS
KB = GROUP // (VTILES * JOCC)
NB = VTILES * JOCC
SUB = TILE * TILE // 128
BATCH = CAP // 2
EXTRA = 48
CORE = 4 * COLS * BATCH + 4 * EXTRA
THIRD = ROWS * (COLS * BATCH - EXTRA)
POOL = 2 * CORE + THIRD
FAR, NEAR = (2,), (1, 3)
PARTS = 12
HALF = 512
PACKED = HALF + HALF // 16
VMEM_GRANT = 16 * 1024 * 1024


def route_kernel(slots_dev, me_ref, slot_ref, out_ref):
    base = me_ref[0] * slots_dev
    slot = slot_ref[...]
    rows = slot.shape[0]
    per = rows // COLS
    local = slot - base
    mine = jnp.logical_and(local >= 0, local < slots_dev)
    ones = jnp.where(mine, 1.0, 0.0).astype(jnp.bfloat16)
    r = lax.broadcasted_iota(jnp.int32, (128, 128), 0)
    c = lax.broadcasted_iota(jnp.int32, (128, 128), 1)
    before = jnp.where(r < c, 1.0, 0.0).astype(jnp.bfloat16)
    within = jnp.dot(ones, before, preferred_element_type=jnp.float32)
    r = lax.broadcasted_iota(jnp.int32, (rows, rows), 0)
    c = lax.broadcasted_iota(jnp.int32, (rows, rows), 1)
    above = jnp.where(jnp.logical_and(r // per == c // per, c < r), 1.0, 0.0).astype(jnp.bfloat16)
    upto = jnp.dot(above, ones, preferred_element_type=jnp.float32)
    rank = within + jnp.sum(upto, axis=1, keepdims=True)
    rank = jnp.where(mine, rank, -1.0).reshape(COLS, per, 128)
    parity = lax.broadcasted_iota(jnp.int32, (rows, 128), 1) % 2
    local = jnp.where(mine, 2 * local + parity, 0).astype(jnp.float32).reshape(COLS, per, 128)
    lane = lax.broadcasted_iota(jnp.int32, (COLS, 128), 1)
    out = jnp.zeros((COLS, 128), jnp.float32)
    for j in range(CAP):
        picked = jnp.sum(jnp.where(rank == float(j), local, 0.0), axis=1)
        out = jnp.where(lane == j, jnp.sum(picked, axis=1, keepdims=True), out)
    out_ref[...] = out.astype(jnp.int32)


def fill_kernel(index_ref, tiles_ref, first_ref, second_ref):
    def group(g, carry):
        codes = [index_ref[g, j] for j in range(CAP)]
        tiles = [tiles_ref[code // 2] for code in codes]
        for j in range(CAP):
            turned = jnp.concatenate([tiles[j][:, TILE:], tiles[j][:, :TILE]], axis=1)
            tiles[j] = jnp.where(codes[j] % 2 == 1, turned, tiles[j])
        for j in range(CAP):
            out_ref = first_ref if j < BATCH else second_ref
            out_ref[g * BATCH + j % BATCH] = tiles[j]
        return carry

    lax.fori_loop(0, COLS, group, 0)


def compact_kernel(index_ref, tiles_ref, first_ref, second_ref):
    def place(out_ref, base):
        def body(i, carry):
            tiles = [tiles_ref[index_ref[base + i * 16 + k]] for k in range(16)]
            for k in range(16):
                out_ref[i * 16 + k] = tiles[k]
            return carry

        lax.fori_loop(0, out_ref.shape[0] // 16, body, 0)

    place(first_ref, 0)
    place(second_ref, EXTRA)


def prep_kernel(mask_ref, amp_ref, even_ref, odd_ref):
    blk = pl.program_id(0)
    rows = amp_ref.shape[0]
    r = lax.broadcasted_iota(jnp.int32, (256, 256), 0)
    c = lax.broadcasted_iota(jnp.int32, (256, 256), 1)
    source = (c % 128 // SUB) * TILE + 2 * (c % SUB) + c // 128
    shuffle = jnp.where(r == source, 1.0, 0.0).astype(jnp.bfloat16)
    moved = jnp.dot(amp_ref[...], shuffle, preferred_element_type=jnp.float32)
    mask = mask_ref[...].astype(jnp.bfloat16)
    r = lax.broadcasted_iota(jnp.int32, (mask.shape[1], 128), 0)
    c = lax.broadcasted_iota(jnp.int32, (mask.shape[1], 128), 1)
    spread = jnp.where(r == 4 * blk + c // SUB, 1.0, 0.0).astype(jnp.bfloat16)
    wide = jnp.dot(mask, spread, preferred_element_type=jnp.float32).astype(jnp.bfloat16)
    r = lax.broadcasted_iota(jnp.int32, (rows, mask.shape[0]), 0)
    c = lax.broadcasted_iota(jnp.int32, (rows, mask.shape[0]), 1)
    tall = jnp.where(r // TILE == c, 1.0, 0.0).astype(jnp.bfloat16)
    full = jnp.dot(tall, wide, preferred_element_type=jnp.float32)
    even_ref[...] = (moved[:, :128] * full).astype(jnp.bfloat16)
    odd_ref[...] = (moved[:, 128:] * full).astype(jnp.bfloat16)


def pack(out_ref, value):
    value = value.reshape(HALF // 16, 16, 128)
    top = jnp.maximum(jnp.max(jnp.abs(value), axis=1), 1e-30)
    exponent = jnp.ceil(jnp.log2(top * 1.0001))
    scaled = jnp.round(value * jnp.exp2(15.0 - exponent)[:, None, :]).reshape(HALF, 128)
    out_ref[pl.ds(0, HALF)] = scaled.astype(jnp.int32).astype(jnp.int16)
    out_ref[pl.ds(HALF, HALF // 16)] = exponent.astype(jnp.int32).astype(jnp.int16)


def unpack(ref):
    mantissa = ref[pl.ds(0, HALF)].astype(jnp.int32).astype(jnp.float32)
    exponent = ref[pl.ds(HALF, HALF // 16)].astype(jnp.int32).astype(jnp.float32)
    value = mantissa.reshape(HALF // 16, 16, 128) * jnp.exp2(exponent - 15.0)[:, None, :]
    return value.reshape(HALF, 128)


def collect_kernel(misc_ref, *refs):
    parts, third_ref, tiles, sems = refs[:PARTS], refs[PARTS], refs[PARTS + 1], refs[PARTS + 2]
    copies, base = [], 0
    for k, part in enumerate(parts):
        size = part.shape[0]
        copies.append(pltpu.make_async_copy(part, tiles.at[pl.ds(base, size)], sems.at[k]))
        base += size
    for copy in copies:
        copy.start()
    tiles[pl.ds(POOL, 1)] = jnp.zeros((1, SUB, 128), jnp.bfloat16)

    @pl.when(misc_ref[2] > 0)
    def _():
        copy = pltpu.make_async_copy(third_ref, tiles.at[pl.ds(base, THIRD)], sems.at[PARTS])
        copy.start()
        copy.wait()

    for copy in copies:
        copy.wait()


def collect_call(misc, parts, third):
    return pl.pallas_call(
        collect_kernel,
        in_specs=[pl.BlockSpec(memory_space=pltpu.SMEM)] + [pl.BlockSpec(memory_space=pl.ANY)] * (PARTS + 1),
        out_specs=pl.BlockSpec(memory_space=pltpu.VMEM),
        out_shape=jax.ShapeDtypeStruct((POOL + 1, SUB, 128), jnp.bfloat16),
        scratch_shapes=[pltpu.SemaphoreType.DMA((PARTS + 1,))],
        compiler_params=pltpu.CompilerParams(vmem_limit_bytes=VMEM_GRANT),
        cost_estimate=pl.CostEstimate(flops=0, bytes_accessed=POOL * 8192, transcendentals=0),
        name="collect",
    )(misc, *parts, third)


def build(hop, unit, index_ref, misc_ref, tiles, weight):
    at = [((misc_ref[0] + hop) % 4 * 4 + unit) * 4, (unit * 4 + (misc_ref[1] + hop) % 4) * 4 + 2]
    left = lax.broadcasted_iota(jnp.int32, (SUB, 128), 1) < TILE
    for kb in range(KB):
        picked = [tiles[index_ref[kb * NB + at[pair] + k]] for pair in range(2) for k in range(2)]
        rows = slice(kb * SUB, (kb + 1) * SUB)
        for pair in range(2):
            one, two = picked[2 * pair : 2 * pair + 2]
            columns = slice(128 * pair, 128 * pair + 128)
            weight[0][rows, columns] = jnp.where(left, one, two)
            weight[1][rows, columns] = jnp.where(left, two, one)


def product_kernel(hops, index_ref, misc_ref, even_ref, odd_ref, tiles, *refs):
    outs, weights = refs[:-4], (refs[-4:-2], refs[-2:])
    build(hops[0], 0, index_ref, misc_ref, tiles, weights[0])

    def emit(at, unit, weight):
        straight = jnp.dot(even_ref[...], weight[0][...], preferred_element_type=jnp.float32)
        crossed = jnp.dot(odd_ref[...], weight[1][...], preferred_element_type=jnp.float32)
        for way in range(2):
            columns = slice(way * 128, way * 128 + 128)
            value = straight[:, columns] + pltpu.roll(crossed[:, columns], TILE, 1)
            if hops == (0,):
                outs[way][unit] = value
                continue
            for half in range(2):
                out_ref = outs[2 * way + half] if hops == FAR else outs[2 * way + at].at[half]
                pack(out_ref.at[unit], value[half * HALF : (half + 1) * HALF])

    for at, hop in enumerate(hops):
        after = hops[min(at + 1, len(hops) - 1)]

        def two_units(i, carry, at=at, hop=hop, after=after):
            build(hop, 2 * i + 1, index_ref, misc_ref, tiles, weights[1])
            emit(at, 2 * i, weights[0])
            build(jnp.where(i == 0, hop, after), 2 - 2 * i, index_ref, misc_ref, tiles, weights[0])
            emit(at, 2 * i + 1, weights[1])
            return carry

        lax.fori_loop(0, 2, two_units, 0)


def product_call(name, hops, scalars, even, odd, tiles):
    rows_dev, depth_half = even.shape
    vmem = pl.BlockSpec(memory_space=pltpu.VMEM)
    if hops == FAR:
        outs = [jax.ShapeDtypeStruct((4, PACKED, 128), jnp.int16)] * 4
    elif hops == NEAR:
        outs = [jax.ShapeDtypeStruct((2, 4, PACKED, 128), jnp.int16)] * 4
    else:
        outs = [jax.ShapeDtypeStruct((4, rows_dev, 128), jnp.float32)] * 2
    return pl.pallas_call(
        functools.partial(product_kernel, hops),
        grid_spec=pltpu.PrefetchScalarGridSpec(
            num_scalar_prefetch=2,
            grid=(),
            in_specs=[vmem] * 3,
            out_specs=[vmem] * len(outs),
            scratch_shapes=[pltpu.VMEM((depth_half, 256), jnp.bfloat16)] * 4,
        ),
        out_shape=outs,
        compiler_params=pltpu.CompilerParams(vmem_limit_bytes=VMEM_GRANT),
        cost_estimate=pl.CostEstimate(
            flops=8 * len(hops) * rows_dev * depth_half * 512, bytes_accessed=POOL * 8192, transcendentals=0
        ),
        name=name,
    )(*scalars, even, odd, tiles)


def ahead(axis, value):
    return lax.ppermute(value, axis, [(i, (i + 1) % 4) for i in range(4)])


def behind(axis, value):
    return lax.ppermute(value, axis, [(i, (i + 3) % 4) for i in range(4)])


def reach(tiles):
    return ahead("y", tiles), behind("y", tiles)


def swap(parts):
    return [lax.ppermute(part, "core", [(0, 1), (1, 0)]) for part in parts]


def add_first_kernel(*refs):
    def body(i, carry):
        for way in range(2):
            ahead_in, behind_in, came_a, came_b = refs[4 * way : 4 * way + 4]
            ahead_out, behind_out = refs[8 + 2 * way : 10 + 2 * way]
            pack(ahead_out.at[0, i], unpack(ahead_in.at[0, i]) + unpack(came_a.at[i]))
            ahead_out[1, i] = ahead_in[1, i]
            behind_out[0, i] = behind_in[0, i]
            pack(behind_out.at[1, i], unpack(behind_in.at[1, i]) + unpack(came_b.at[i]))
        return carry

    lax.fori_loop(0, 4, body, 0)


def add_second_kernel(*refs):
    for way in range(2):
        ahead_in, behind_in, came_a, came_b = refs[4 * way : 4 * way + 4]
        ahead_out, behind_out = refs[8 + 2 * way : 10 + 2 * way]
        pack(ahead_out.at[0], unpack(ahead_in.at[0]) + unpack(came_a.at[0]))
        ahead_out[1] = ahead_in[1]
        behind_out[0] = behind_in[0]
        pack(behind_out.at[1], unpack(behind_in.at[1]) + unpack(came_b.at[0]))


def whole_call(body, name, outs, *arrays, scalars=()):
    vmem = pl.BlockSpec(memory_space=pltpu.VMEM)
    size = sum(a.size * a.dtype.itemsize for a in [*arrays, *outs])
    return pl.pallas_call(
        body,
        in_specs=[pl.BlockSpec(memory_space=pltpu.SMEM)] * len(scalars) + [vmem] * len(arrays),
        out_specs=[vmem] * len(outs),
        out_shape=outs,
        compiler_params=pltpu.CompilerParams(vmem_limit_bytes=VMEM_GRANT),
        cost_estimate=pl.CostEstimate(flops=10 * size, bytes_accessed=size, transcendentals=0),
        name=name,
    )(*scalars, *arrays)


def middle_kernel(misc_ref, one_ref, two_ref, *refs):
    came, outs, own_ref = refs[:4], refs[4:12], refs[12]
    for way, own in enumerate((one_ref, two_ref)):
        right, left = came[2 * way : 2 * way + 2]
        far_a, far_b, ahead_ref, behind_ref = outs[4 * way : 4 * way + 4]
        for hop, ahead_by in enumerate((2, 1, 3, 0)):
            at = (misc_ref[1 - way] + ahead_by) % 4
            total = [
                own[at, pl.ds(half * HALF, HALF)] + unpack(right.at[half, at]) + unpack(left.at[half, at])
                for half in range(2)
            ]
            for half in range(2):
                if hop == 0:
                    pack((far_a, far_b)[half].at[0], total[half])
                elif hop < 3:
                    pack((ahead_ref, behind_ref)[hop - 1].at[half], total[half])
                else:
                    own_ref[pl.ds(half * HALF, HALF), pl.ds(way * 128, 128)] = total[half]


def last_kernel(own_ref, *refs):
    came, out_ref = refs[:4], refs[4]
    for way in range(2):
        right, left = came[2 * way : 2 * way + 2]
        columns = pl.ds(way * 128, 128)
        for half in range(2):
            rows = pl.ds(half * HALF, HALF)
            total = own_ref[rows, columns] + unpack(right.at[half]) + unpack(left.at[half])
            out_ref[columns, rows] = total.T


def shards(amplitudes, t2_mask, eri_tiles, eri_slot):
    y, core, x, z = (lax.axis_index(name) for name in ("y", "core", "x", "z"))
    group = x * 4 + z
    myself = (y * 2 + core) * COLS + group
    rows_dev, depth_dev = amplitudes.shape
    slots_dev = eri_tiles.shape[0]

    send_index = pl.pallas_call(
        lambda *refs: route_kernel(slots_dev, *refs),
        out_shape=jax.ShapeDtypeStruct((COLS, 128), jnp.int32),
        in_specs=[
            pl.BlockSpec(memory_space=pltpu.SMEM),
            pl.BlockSpec(memory_space=pltpu.VMEM),
        ],
        out_specs=pl.BlockSpec(memory_space=pltpu.VMEM),
        compiler_params=pltpu.CompilerParams(vmem_limit_bytes=VMEM_GRANT),
        name="route",
    )(myself.reshape(1).astype(jnp.int32), eri_slot.reshape(-1, 128))
    vmem = pl.BlockSpec(memory_space=pltpu.VMEM)
    batch = jax.ShapeDtypeStruct((COLS * BATCH, SUB, 128), jnp.bfloat16)
    outgoing = pl.pallas_call(
        fill_kernel,
        grid_spec=pltpu.PrefetchScalarGridSpec(
            num_scalar_prefetch=1, grid=(), in_specs=[vmem], out_specs=[vmem] * 2
        ),
        out_shape=[batch] * 2,
        compiler_params=pltpu.CompilerParams(vmem_limit_bytes=VMEM_GRANT),
        name="fill",
    )(send_index, eri_tiles.reshape(slots_dev, SUB, 128))
    def send(part):
        part = part.reshape(COLS, BATCH, SUB, 128)
        part = lax.all_to_all(part, ("x", "z"), split_axis=0, concat_axis=0, tiled=True)
        return part.reshape(COLS * BATCH, SUB, 128)

    first = send(outgoing[0])
    first, second, eri_slot = lax.optimization_barrier((first, outgoing[1], eri_slot))
    up, down = reach(first)
    second = send(second)

    devices = jnp.arange(DEVS, dtype=jnp.int32)
    owner_all = jnp.where(eri_slot >= 0, eri_slot // slots_dev, -1).reshape(COLS, 1, GROUP)
    held = jnp.sum((owner_all == devices[None, :, None]).astype(jnp.int32), axis=2)
    tail = jnp.maximum(held - BATCH, 0).reshape(COLS, ROWS, COLS)
    spill = jnp.any(jnp.sum(tail, axis=2) > EXTRA)
    tail = lax.dynamic_index_in_dim(tail, group, 0, keepdims=False)
    upto = jnp.sum(jnp.where(jnp.arange(COLS)[:, None] >= jnp.arange(COLS)[None, :], tail[:, None, :], 0), axis=2)
    start = upto - tail
    mine_upto = lax.dynamic_index_in_dim(upto, y * 2 + core, 0, keepdims=False)
    mine_start = lax.dynamic_index_in_dim(start, y * 2 + core, 0, keepdims=False)
    spot = jnp.arange(COLS * BATCH, dtype=jnp.int32)
    inside = jnp.logical_and(spot[:, None] >= mine_start[None, :], spot[:, None] < mine_upto[None, :])
    source = jnp.arange(COLS, dtype=jnp.int32)[None, :] * BATCH + spot[:, None] - mine_start[None, :]
    source = jnp.sum(jnp.where(inside, source, 0), axis=1).astype(jnp.int32)
    some, rest = pl.pallas_call(
        compact_kernel,
        grid_spec=pltpu.PrefetchScalarGridSpec(
            num_scalar_prefetch=1, grid=(), in_specs=[vmem], out_specs=[vmem] * 2
        ),
        out_shape=[
            jax.ShapeDtypeStruct((EXTRA, SUB, 128), jnp.bfloat16),
            jax.ShapeDtypeStruct((COLS * BATCH - EXTRA, SUB, 128), jnp.bfloat16),
        ],
        compiler_params=pltpu.CompilerParams(vmem_limit_bytes=VMEM_GRANT),
        name="compact",
    )(source, second)
    wanted = lax.dynamic_slice_in_dim(eri_slot, group * GROUP, GROUP)
    up, down, amplitudes, wanted = lax.optimization_barrier((up, down, amplitudes, wanted))
    half = COLS * BATCH // 2
    from_up = ahead("y", jnp.concatenate([up[:half], some]))
    from_down = behind("y", jnp.concatenate([down[half:], some]))
    parted = jax.ShapeDtypeStruct((rows_dev, depth_dev // 2), jnp.bfloat16)
    even, odd = pl.pallas_call(
        prep_kernel,
        grid=(depth_dev // 256,),
        out_shape=[parted] * 2,
        in_specs=[
            pl.BlockSpec(t2_mask.shape, lambda i: (0, 0)),
            pl.BlockSpec((rows_dev, 256), lambda i: (0, i)),
        ],
        out_specs=[pl.BlockSpec((rows_dev, 128), lambda i: (0, i))] * 2,
        compiler_params=pltpu.CompilerParams(vmem_limit_bytes=VMEM_GRANT),
        name="prep",
    )(t2_mask, amplitudes)

    owner = jnp.where(wanted >= 0, wanted // slots_dev, -1)
    mine = owner[:, None] == devices[None, :]
    spot = jnp.arange(GROUP, dtype=jnp.int32)
    before = (spot[:, None] > spot[None, :]).astype(jnp.bfloat16)
    counts = jnp.dot(before, mine.astype(jnp.bfloat16), preferred_element_type=jnp.float32)
    rank = jnp.sum(jnp.where(mine, counts, 0.0), axis=1).astype(jnp.int32)
    begin = jnp.sum(jnp.where(mine, start.reshape(1, DEVS), 0), axis=1)
    behind_first = begin + rank - BATCH
    owner_row = owner // COLS
    turn = (owner_row // 2 - y) % 4
    turn = jnp.where(turn == 1, 2, jnp.where(turn == 2, 3, jnp.where(turn == 3, 1, 0)))
    size = COLS * BATCH
    slot = owner % COLS * BATCH + rank
    early = turn * size + slot + jnp.where(jnp.logical_and(turn == 3, slot >= half), EXTRA, 0)
    begins = (4 * size + 2 * EXTRA, 3 * size + half, 4 * size + EXTRA, 4 * size + 3 * EXTRA)
    late = behind_first + sum(jnp.where(turn == k, begin_late, 0) for k, begin_late in enumerate(begins))
    tile_index = jnp.where(rank < BATCH, early, late) + CORE * (owner_row % 2 != core)
    spilled = 2 * CORE + owner_row * (size - EXTRA) + behind_first - EXTRA
    tile_index = jnp.where(jnp.logical_or(rank < BATCH, behind_first < EXTRA), tile_index, spilled)
    tile_index = jnp.where(wanted < 0, POOL, tile_index)
    misc = jnp.stack([x, z, spill.astype(jnp.int32)]).astype(jnp.int32)
    third = lax.cond(
        misc[2] > 0,
        lambda value: lax.all_gather(value, ("y", "core"), axis=0, tiled=True),
        lambda value: jnp.zeros((THIRD, SUB, 128), jnp.bfloat16),
        rest,
    )
    from_up, from_down, even, odd, tile_index, misc, third = lax.optimization_barrier(
        (from_up, from_down, even, odd, tile_index, misc, third)
    )
    tail = jnp.concatenate(
        [
            some,
            ahead("y", from_up[half : half + EXTRA // 2]),
            behind("y", from_down[half + EXTRA // 2 :]),
        ]
    )
    same = [first, up, down, from_up, from_down, tail]
    tiles = collect_call(misc, same + swap(same), third)

    scalars, arrays = (tile_index, misc), (even, odd, tiles)
    far = product_call("far", FAR, scalars, *arrays)
    near = product_call("near", NEAR, scalars, *arrays)
    axes = ("x", "z")
    inputs = []
    for way, axis in enumerate(axes):
        inputs += [*near[2 * way : 2 * way + 2], ahead(axis, far[2 * way]), behind(axis, far[2 * way + 1])]
    packed = jax.ShapeDtypeStruct((2, 4, PACKED, 128), jnp.int16)
    added = whole_call(add_first_kernel, "add_first", [packed] * 4, *inputs)
    came = []
    for way, axis in enumerate(axes):
        came += [ahead(axis, added[2 * way]), behind(axis, added[2 * way + 1])]
    one, two = product_call("own", (0,), scalars, *arrays)
    single = jax.ShapeDtypeStruct((1, PACKED, 128), jnp.int16)
    double = jax.ShapeDtypeStruct((2, PACKED, 128), jnp.int16)
    *outs, own = whole_call(
        middle_kernel,
        "middle",
        [single, single, double, double] * 2 + [jax.ShapeDtypeStruct((rows_dev, 256), jnp.float32)],
        one,
        two,
        *came,
        scalars=(misc,),
    )
    axes = ("z", "x")
    inputs = []
    for way, axis in enumerate(axes):
        far_a, far_b, next_ab, prev_ab = outs[4 * way : 4 * way + 4]
        inputs += [next_ab, prev_ab, ahead(axis, far_a), behind(axis, far_b)]
    added = whole_call(add_second_kernel, "add_second", [double] * 4, *inputs)
    came = []
    for way, axis in enumerate(axes):
        came += [ahead(axis, added[2 * way]), behind(axis, added[2 * way + 1])]
    return whole_call(
        last_kernel, "last", [jax.ShapeDtypeStruct((256, rows_dev), jnp.float32)], own, *came
    )[0]


def solution(mesh):
    axes = ("y", "core", "x", "z")
    fine = Mesh(mesh.devices.reshape(4, 2, 4, 4), axes)
    row, col = ("y", "core"), ("x", "z")
    in_specs = (P(row, col), P(row, col), P(axes, None), P())
    out_specs = P(col, row)
    return jax.shard_map(shards, mesh=fine, in_specs=in_specs, out_specs=out_specs, check_vma=False)
```

time: 893 us -> 231 us (0.26)
  waiting for transfers between devices: 479 us -> 78.4 us
  local copies, waits for them, and re-layouts: 347 us -> 32.6 us
  Pallas kernels: 0 us -> 50.8 us
  starting transfers between devices: 11.1 us -> 46.7 us
  matrix products: 23.7 us -> 1.97 us
  other arithmetic: 14.6 us -> 5.35 us
    all_to_all x1 -> x2, waiting for transfers between devices: 351 us -> 34.7 us  [send(): lax.all_to_all(part, ('x', 'z'), split_axis=0, concat_axis=0, tiled=True)]
    reduce_scatter x1 -> x0, waiting for transfers between devices: 127 us -> none  [shards(): lax.psum_scatter(product.reshape(VTILES * JOCC * TILE // n_col * lax.axis...]
    scatter x1 -> x0, local copies, waits for them, and re-layouts: 120 us -> none  [shards(): jnp.full((n_col * capacity,), slots_dev, jnp.int32).at[target]]
    dot_general x2 -> x0, local copies, waits for them, and re-layouts: 73.3 us -> none  [shards(): lax.dot_general(tiles, masked, (((0, 2), (1, 2)), ((), ())), preferred_el...]
    reshape x3 -> x0, local copies, waits for them, and re-layouts: 72.6 us -> none  [the longest x1 46 us: shards(): tile_pool[tile_index]]
    pallas_call x0 -> x12, Pallas kernels: none -> 50.8 us  [the longest x3 27.2 us: product_call(): pl.pallas_call(functools.partial(product_kernel, hops), grid_spec=pltpu.P...]
    ppermute x0 -> x28, waiting for transfers between devices: none -> 43.7 us  [the longest x11 21.4 us: ahead(): return lax.ppermute(value, axis, [(i, (i + 1) % 4) for i in range(4)])]
    gather x2 -> x0, local copies, waits for them, and re-layouts: 42.2 us -> none  [the longest x1 38.3 us: shards(): tile_pool[tile_index]]
  transfers between devices with their start and end apart: 2 -> 30, of which waited for: 2 -> 17; matrix products, arithmetic and copies ran while one was open for 2% -> 6% of each run, Pallas kernels for 0% -> 12%
where the time goes in v1:
time: 231 us; the launch traced here: 230 us
  waiting for transfers between devices  78.4 us (34%)
  Pallas kernels  50.8 us (22%)
  starting transfers between devices  46.7 us (20%)
  local copies, waits for them, and re-layouts  32.6 us (14%)
  between operations  14.4 us (6%)
  other arithmetic  5.35 us (2%)
    all_to_all x2, waiting for transfers between devices, send(): lax.all_to_all(part, ('x', 'z'), split_axis=0, concat_axis=0, tiled=True)  34.7 us
    pallas_call x3, Pallas kernels, product_call(): pl.pallas_call(functools.partial(product_kernel, hops), grid_spec=pltpu.P...  27.2 us
    unnamed x39, local copies, waits for them, and re-layouts  25.2 us
    ppermute x11, waiting for transfers between devices, ahead(): return lax.ppermute(value, axis, [(i, (i + 1) % 4) for i in range(4)])  21.4 us
    ppermute x11, waiting for transfers between devices, behind(): return lax.ppermute(value, axis, [(i, (i + 3) % 4) for i in range(4)])  19 us
    ppermute x11, starting transfers between devices, behind(): return lax.ppermute(value, axis, [(i, (i + 3) % 4) for i in range(4)])  17.9 us
    all_to_all x2, starting transfers between devices, send(): lax.all_to_all(part, ('x', 'z'), split_axis=0, concat_axis=0, tiled=True)  14.3 us
    ppermute x11, starting transfers between devices, ahead(): return lax.ppermute(value, axis, [(i, (i + 1) % 4) for i in range(4)])  13.4 us
  transfers between devices with their start and end apart: 30, of which 17 were waited for; matrix products, arithmetic and copies ran while one was open for 6% of the time, Pallas kernels for 12%

profile of v1, /device:TPU:6, one launch (start us, length us, event | category | flops | bytes accessed | tf_op | source)
XLA Modules:
  0.0 230.3 jit_solution(16886574190333760615)
XLA Ops:
  9.8 3.5 %fill.1 = (bf16[160,32,128]{2,1,0:T(8,128)(2,1)S(1)}, bf16[160,32,128]{2,1,0:T(8,128)(2,1)S(1)}) custom-call(s32[16,128]{1,0:T(8,128)S(1)} %route.1.index_ref, bf16[320,32,128]{2,1,0:T(8,128)(2,1)S(1)} %bitcast.18), custom_call_target="tpu_custom_call" | custom-call | tf_op jit(solution)/shard_map/fill/pallas_call | solution.py:338
  15.5 8.3 %all-to-all-start = ((bf16[16,10,32,128]{3,2,1,0:T(8,128)(2,1)}), bf16[16,10,32,128]{3,2,1,0:T(8,128)(2,1)S(1)}, u32[]{:S(2)}, u32[]{:S(2)}) async-start(bf16[16,10,32,128]{3,2,1,0:T(8,128)(2,1)} %bitcast.25), calls=%async_computation | async-start | bytes 2621440 | tf_op jit(solution)/shard_map/all_to_all | solution.py:349
  23.7 18.4 %all-to-all-done = bf16[16,10,32,128]{3,2,1,0:T(8,128)(2,1)S(1)} async-done(((bf16[16,10,32,128]{3,2,1,0:T(8,128)(2,1)}), bf16[16,10,32,128]{3,2,1,0:T(8,128)(2,1)S(1)}, u32[]{:S(2)}, u32[]{:S(2)}) %all-to-all-start) | async-done | bytes 1310752 | tf_op jit(solution)/shard_map/all_to_all | solution.py:349
  45.3 6.1 %all-to-all-start.1 = ((bf16[16,10,32,128]{3,2,1,0:T(8,128)(2,1)}), bf16[16,10,32,128]{3,2,1,0:T(8,128)(2,1)S(1)}, u32[]{:S(2)}, u32[]{:S(2)}) async-start(bf16[16,10,32,128]{3,2,1,0:T(8,128)(2,1)} %bitcast.24), calls=%async_computation.1 | async-start | bytes 2621440 | tf_op jit(solution)/shard_map/all_to_all | solution.py:349
  54.3 16.3 %all-to-all-done.1 = bf16[16,10,32,128]{3,2,1,0:T(8,128)(2,1)S(1)} async-done(((bf16[16,10,32,128]{3,2,1,0:T(8,128)(2,1)}), bf16[16,10,32,128]{3,2,1,0:T(8,128)(2,1)S(1)}, u32[]{:S(2)}, u32[]{:S(2)}) %all-to-all-start.1) | async-done | bytes 1310752 | tf_op jit(solution)/shard_map/all_to_all | solution.py:349
  73.9 3.5 %collective-permute-done.refs_1_ = bf16[160,32,128]{2,1,0:T(8,128)(2,1)} collective-permute-done((bf16[160,32,128]{2,1,0:T(8,128)(2,1)S(1)}, bf16[160,32,128]{2,1,0:T(8,128)(2,1)}, u32[]{:S(2)}, u32[]{:S(2)}) %collective-permute-start) | collective-permute-done | bytes 1310752 | tf_op jit(solution)/shard_map/ppermute | solution.py:234
  84.7 3.9 %conditional.1 = (bf16[896,32,128]{2,1,0:T(8,128)(2,1)}) conditional(s32[]{:T(128)} %convert_element_type.18, () %tuple.16, bf16[112,32,128]{2,1,0:T(8,128)(2,1)} %get-tuple-element.68), branch_computations={%region_7.8_spmd, %region_8.9_spmd} | conditional | bytes 24772656 | solution.py:423
  84.7 3.9 %broadcast.56 = bf16[896,32,128]{2,1,0:T(8,128)(2,1)} broadcast(bf16[]{:T(256)} %constant.115.clone), dimensions={} | broadcast | bytes 7340034 | tf_op jit(solution)/shard_map/broadcast.10
  90.8 5.7 %prep.1 = (bf16[1024,1024]{1,0:T(8,128)(2,1)S(1)}, bf16[1024,1024]{1,0:T(8,128)(2,1)S(1)}) custom-call(s32[16,32]{1,0:T(8,128)S(1)} %copy-done.15, bf16[1024,2048]{1,0:T(8,128)(2,1)S(1)} %copy-done.9), custom_call_target="tpu_custom_call" | custom-call | tf_op jit(solution)/shard_map/prep/pallas_call | solution.py:389
  98.8 7.0 %collective-permute-done.3.refs_4_ = bf16[128,32,128]{2,1,0:T(8,128)(2,1)S(1)} collective-permute-done((bf16[128,32,128]{2,1,0:T(8,128)(2,1)}, bf16[128,32,128]{2,1,0:T(8,128)(2,1)S(1)}, u32[]{:S(2)}, u32[]{:S(2)}) %collective-permute-start.3) | collective-permute-done | bytes 1048608 | tf_op jit(solution)/shard_map/ppermute | solution.py:238
  116.4 3.3 %collective-permute-done.11.refs_11_ = bf16[96,32,128]{2,1,0:T(8,128)(2,1)S(1)} collective-permute-done((bf16[96,32,128]{2,1,0:T(8,128)(2,1)S(1)}, bf16[96,32,128]{2,1,0:T(8,128)(2,1)S(1)}, u32[]{:S(2)}, u32[]{:S(2)}) %collective-permute-start.11) | collective-permute-done | bytes 786464 | tf_op jit(solution)/shard_map/ppermute | solution.py:246
  124.2 7.9 %far.1 = (s16[4,544,128]{2,1,0:T(8,128)(2,1)}, s16[4,544,128]{2,1,0:T(8,128)(2,1)S(1)}, s16[4,544,128]{2,1,0:T(8,128)(2,1)S(1)}, s16[4,544,128]{2,1,0:T(8,128)(2,1)S(1)}) custom-call(s32[2048]{0:T(1024)S(1)} %select_select_fusion.index_ref, s32[3]{0:T(128)S(1)} %pad_add_fusion.misc_ref, bf16[1024,1024]{1,0:T(8,128)(2,1)S(1)} %get-tuple-element.71.even_ref, ...), custom_call_target="tpu_custom_call" | custom-call | flops 4294967296 | bytes 20971520 | tf_op jit(solution)/shard_map/far/pallas_call | solution.py:215
  137.7 7.0 %copy-done.1 = bf16[2561,32,128]{2,1,0:T(8,128)(2,1)S(1)} copy-done((bf16[2561,32,128]{2,1,0:T(8,128)(2,1)S(1)}, bf16[2561,32,128]{2,1,0:T(8,128)(2,1)}, u32[]{:S(2)}) %copy-start.1) | copy-done | bytes 20979736
  147.9 13.2 %near.1 = (s16[2,4,544,128]{3,2,1,0:T(8,128)(2,1)S(1)}, s16[2,4,544,128]{3,2,1,0:T(8,128)(2,1)S(1)}, s16[2,4,544,128]{3,2,1,0:T(8,128)(2,1)S(1)}, s16[2,4,544,128]{3,2,1,0:T(8,128)(2,1)S(1)}) custom-call(s32[2048]{0:T(1024)S(1)} %select_select_fusion.index_ref, s32[3]{0:T(128)S(1)} %pad_add_fusion.misc_ref, bf16[1024,1024]{1,0:T(8,128)(2,1)S(1)} %copy-done.4, ...), custom_call_target="tpu_custom_call" | custom-call | flops 8589934592 | bytes 20971520 | tf_op jit(solution)/shard_map/near/pallas_call | solution.py:215
  164.3 3.5 %collective-permute-start.16 = (s16[2,4,544,128]{3,2,1,0:T(8,128)(2,1)S(1)}, s16[2,4,544,128]{3,2,1,0:T(8,128)(2,1)S(1)}, u32[]{:S(2)}, u32[]{:S(2)}) collective-permute-start(s16[2,4,544,128]{3,2,1,0:T(8,128)(2,1)S(1)} %get-tuple-element.86), channel_id=1, source_target_pairs={{0,4},{4,8},{8,12},{12,0},{1,5},{5,9},{9,13},{13,1},{2,6},{6,10},{... | collective-permute-start | bytes 3342344 | tf_op jit(solution)/shard_map/ppermute | solution.py:234
  167.8 3.2 %collective-permute-start.19 = (s16[2,4,544,128]{3,2,1,0:T(8,128)(2,1)S(1)}, s16[2,4,544,128]{3,2,1,0:T(8,128)(2,1)S(1)}, u32[]{:S(2)}, u32[]{:S(2)}) collective-permute-start(s16[2,4,544,128]{3,2,1,0:T(8,128)(2,1)S(1)} %get-tuple-element.89), channel_id=1, source_target_pairs={{0,3},{1,0},{2,1},{3,2},{4,7},{5,4},{6,5},{7,6},{8,11},{9,8},{10,9... | collective-permute-start | bytes 3342344 | tf_op jit(solution)/shard_map/ppermute | solution.py:238
  171.0 7.0 %copy-done.2 = bf16[2561,32,128]{2,1,0:T(8,128)(2,1)S(1)} copy-done((bf16[2561,32,128]{2,1,0:T(8,128)(2,1)S(1)}, bf16[2561,32,128]{2,1,0:T(8,128)(2,1)}, u32[]{:S(2)}) %copy-start.2) | copy-done | bytes 20979736
  178.0 6.1 %own.1 = (f32[4,1024,128]{2,1,0:T(8,128)S(1)}, f32[4,1024,128]{2,1,0:T(8,128)S(1)}) custom-call(s32[2048]{0:T(1024)S(1)} %select_select_fusion.index_ref, s32[3]{0:T(128)S(1)} %pad_add_fusion.misc_ref, bf16[1024,1024]{1,0:T(8,128)(2,1)S(1)} %copy-done.5, bf16[1024,1024]{1,0:T(8,128)(2,1)S(1)} %copy-done.8, bf16[2561,32,128]{2,1,0:T(8,128)(2,1)S(1)} %copy-done.2), custom_call_target="tpu_custom_call" | custom-call | flops 4294967296 | bytes 20971520 | tf_op jit(solution)/shard_map/own/pallas_call | solution.py:215
  184.1 6.7 %collective-permute-done.16.refs_0_ = s16[2,4,544,128]{3,2,1,0:T(8,128)(2,1)S(1)} collective-permute-done((s16[2,4,544,128]{3,2,1,0:T(8,128)(2,1)S(1)}, s16[2,4,544,128]{3,2,1,0:T(8,128)(2,1)S(1)}, u32[]{:S(2)}, u32[]{:S(2)}) %collective-permute-start.16) | collective-permute-done | bytes 1114144 | tf_op jit(solution)/shard_map/ppermute | solution.py:234
  190.8 3.4 %collective-permute-done.17.refs_1_ = s16[2,4,544,128]{3,2,1,0:T(8,128)(2,1)S(1)} collective-permute-done((s16[2,4,544,128]{3,2,1,0:T(8,128)(2,1)S(1)}, s16[2,4,544,128]{3,2,1,0:T(8,128)(2,1)S(1)}, u32[]{:S(2)}, u32[]{:S(2)}) %collective-permute-start.17) | collective-permute-done | bytes 1114144 | tf_op jit(solution)/shard_map/ppermute | solution.py:238
  194.2 3.5 %middle.1 = (s16[1,544,128]{2,1,0:T(8,128)(2,1)S(1)}, s16[1,544,128]{2,1,0:T(8,128)(2,1)S(1)}, s16[2,544,128]{2,1,0:T(8,128)(2,1)S(1)}, s16[2,544,128]{2,1,0:T(8...) custom-call(s32[3]{0:T(128)S(1)} %pad_add_fusion.misc_ref, ...), custom_call_target="tpu_custom_call" | custom-call | flops 113704960 | bytes 11370496 | tf_op jit(solution)/shard_map/middle/pallas_call | solution.py:276
  197.8 3.2 %collective-permute-start.21 = (s16[1,544,128]{2,1,0:T(8,128)(2,1)S(1)}, s16[1,544,128]{2,1,0:T(8,128)(2,1)S(1)}, u32[]{:S(2)}, u32[]{:S(2)}) collective-permute-start(s16[1,544,128]{2,1,0:T(8,128)(2,1)S(1)} %get-tuple-element.94), channel_id=1, source_target_pairs={{0,3},{1,0},{2,1},{3,2},{4,7},{5,4},{6,5},{7,6},{8,11},{9,8},{10,9... | collective-permute-start | bytes 417800 | tf_op jit(solution)/shard_map/ppermute | solution.py:238
  206.6 3.7 %collective-permute-done.23.refs_7_ = s16[1,544,128]{2,1,0:T(8,128)(2,1)S(1)} collective-permute-done((s16[1,544,128]{2,1,0:T(8,128)(2,1)S(1)}, s16[1,544,128]{2,1,0:T(8,128)(2,1)S(1)}, u32[]{:S(2)}, u32[]{:S(2)}) %collective-permute-start.23) | collective-permute-done | bytes 139296 | tf_op jit(solution)/shard_map/ppermute | solution.py:238
  211.1 3.2 %collective-permute-start.25 = (s16[2,544,128]{2,1,0:T(8,128)(2,1)S(1)}, s16[2,544,128]{2,1,0:T(8,128)(2,1)S(1)}, u32[]{:S(2)}, u32[]{:S(2)}) collective-permute-start(s16[2,544,128]{2,1,0:T(8,128)(2,1)S(1)} %get-tuple-element.100), channel_id=1, source_target_pairs={{0,3},{1,0},{2,1},{3,2},{4,7},{5,4},{6,5},{7,6},{8,11},{9,8},{10,9... | collective-permute-start | bytes 835592 | tf_op jit(solution)/shard_map/ppermute | solution.py:238
  (121 shorter events, 68.4 us)
Async XLA Ops:
  15.5 26.7 %all-to-all-start = ((bf16[16,10,32,128]{3,2,1,0:T(8,128)(2,1)}), bf16[16,10,32,128]{3,2,1,0:T(8,128)(2,1)S(1)}, u32[]{:S(2)}, u32[]{:S(2)}) async-start(bf16[16,10,32,128]{3,2,1,0:T(8,128)(2,1)} %bitcast.25), calls=%async_computation | async-start | bytes 2621440 | tf_op jit(solution)/shard_map/all_to_all | solution.py:349
  42.1 73.6 %collective-permute-start.6 = (bf16[160,32,128]{2,1,0:T(8,128)(2,1)S(1)}, bf16[160,32,128]{2,1,0:T(8,128)(2,1)}, u32[]{:S(2)}, u32[]{:S(2)}) collective-permute-start(bf16[160,32,128]{2,1,0:T(8,128)(2,1)S(1)} %bitcast.19), channel_id=1, source_target_pairs={{0,16},{16,0},{1,17},{17,1},{2,18},{18,2},{3,19},{19,3},{4,20},{20... | collective-permute-start | bytes 3932168 | tf_op jit(solution)/shard_map/ppermute | solution.py:246
  42.1 31.7 %collective-permute-start.1 = (bf16[160,32,128]{2,1,0:T(8,128)(2,1)S(1)}, bf16[160,32,128]{2,1,0:T(8,128)(2,1)}, u32[]{:S(2)}, u32[]{:S(2)}) collective-permute-start(bf16[160,32,128]{2,1,0:T(8,128)(2,1)S(1)} %bitcast.20), channel_id=1, source_target_pairs={{0,96},{32,0},{64,32},{96,64},{1,97},{33,1},{65,33},{97,65},{2,98}... | collective-permute-start | bytes 3932168 | tf_op jit(solution)/shard_map/ppermute | solution.py:238
  45.2 32.2 %collective-permute-start = (bf16[160,32,128]{2,1,0:T(8,128)(2,1)S(1)}, bf16[160,32,128]{2,1,0:T(8,128)(2,1)}, u32[]{:S(2)}, u32[]{:S(2)}) collective-permute-start(bf16[160,32,128]{2,1,0:T(8,128)(2,1)S(1)} %bitcast.21), channel_id=1, source_target_pairs={{0,32},{32,64},{64,96},{96,0},{1,33},{33,65},{65,97},{97,1},{2,34}... | collective-permute-start | bytes 3932168 | tf_op jit(solution)/shard_map/ppermute | solution.py:234
  45.3 25.3 %all-to-all-start.1 = ((bf16[16,10,32,128]{3,2,1,0:T(8,128)(2,1)}), bf16[16,10,32,128]{3,2,1,0:T(8,128)(2,1)S(1)}, u32[]{:S(2)}, u32[]{:S(2)}) async-start(bf16[16,10,32,128]{3,2,1,0:T(8,128)(2,1)} %bitcast.24), calls=%async_computation.1 | async-start | bytes 2621440 | tf_op jit(solution)/shard_map/all_to_all | solution.py:349
  81.2 24.7 %collective-permute-start.3 = (bf16[128,32,128]{2,1,0:T(8,128)(2,1)}, bf16[128,32,128]{2,1,0:T(8,128)(2,1)S(1)}, u32[]{:S(2)}, u32[]{:S(2)}) collective-permute-start(bf16[128,32,128]{2,1,0:T(8,128)(2,1)} %get-tuple-element.103), channel_id=1, source_target_pairs={{0,96},{32,0},{64,32},{96,64},{1,97},{33,1},{65,33},{97,65},{2,98}... | collective-permute-start | bytes 3145736 | tf_op jit(solution)/shard_map/ppermute | solution.py:238
  81.5 26.0 %collective-permute-start.2 = (bf16[128,32,128]{2,1,0:T(8,128)(2,1)}, bf16[128,32,128]{2,1,0:T(8,128)(2,1)}, u32[]{:S(2)}, u32[]{:S(2)}) collective-permute-start(bf16[128,32,128]{2,1,0:T(8,128)(2,1)} %get-tuple-element.104), channel_id=1, source_target_pairs={{0,32},{32,64},{64,96},{96,0},{1,33},{33,65},{65,97},{97,1},{2,34}... | collective-permute-start | bytes 3145736 | tf_op jit(solution)/shard_map/ppermute | solution.py:234
  108.7 6.9 %collective-permute-start.4 = (bf16[24,32,128]{2,1,0:T(8,128)(2,1)S(1)}, bf16[24,32,128]{2,1,0:T(8,128)(2,1)S(1)}, u32[]{:S(2)}, u32[]{:S(2)}) collective-permute-start(bf16[24,32,128]{2,1,0:T(8,128)(2,1)S(1)} %slice.14), channel_id=1, source_target_pairs={{0,32},{32,64},{64,96},{96,0},{1,33},{33,65},{65,97},{97,1},{2,34}... | collective-permute-start | bytes 589832 | tf_op jit(solution)/shard_map/ppermute | solution.py:234
  113.3 6.4 %collective-permute-start.9 = (bf16[128,32,128]{2,1,0:T(8,128)(2,1)}, bf16[128,32,128]{2,1,0:T(8,128)(2,1)S(1)}, u32[]{:S(2)}, u32[]{:S(2)}) collective-permute-start(bf16[128,32,128]{2,1,0:T(8,128)(2,1)} %collective-permute-done.2.refs_3_), channel_id=1, source_target_pairs={{0,16},{16,0},{1,17},{17,1},{2,18},{18,2},{3,19},{19,3},{4,20},{20... | collective-permute-start | bytes 3145736 | tf_op jit(solution)/shard_map/ppermute | solution.py:246
  132.0 29.1 %collective-permute-start.12 = (s16[4,544,128]{2,1,0:T(8,128)(2,1)}, s16[4,544,128]{2,1,0:T(8,128)(2,1)S(1)}, u32[]{:S(2)}, u32[]{:S(2)}) collective-permute-start(s16[4,544,128]{2,1,0:T(8,128)(2,1)} %get-tuple-element.80), channel_id=1, source_target_pairs={{0,4},{4,8},{8,12},{12,0},{1,5},{5,9},{9,13},{13,1},{2,6},{6,10},{... | collective-permute-start | bytes 1671176 | tf_op jit(solution)/shard_map/ppermute | solution.py:234
  134.5 26.6 %collective-permute-start.13 = (s16[4,544,128]{2,1,0:T(8,128)(2,1)S(1)}, s16[4,544,128]{2,1,0:T(8,128)(2,1)S(1)}, u32[]{:S(2)}, u32[]{:S(2)}) collective-permute-start(s16[4,544,128]{2,1,0:T(8,128)(2,1)S(1)} %get-tuple-element.81), channel_id=1, source_target_pairs={{0,12},{4,0},{8,4},{12,8},{1,13},{5,1},{9,5},{13,9},{2,14},{6,2},{... | collective-permute-start | bytes 1671176 | tf_op jit(solution)/shard_map/ppermute | solution.py:238
  134.5 26.6 %collective-permute-start.14 = (s16[4,544,128]{2,1,0:T(8,128)(2,1)S(1)}, s16[4,544,128]{2,1,0:T(8,128)(2,1)S(1)}, u32[]{:S(2)}, u32[]{:S(2)}) collective-permute-start(s16[4,544,128]{2,1,0:T(8,128)(2,1)S(1)} %get-tuple-element.84), channel_id=1, source_target_pairs={{0,1},{1,2},{2,3},{3,0},{4,5},{5,6},{6,7},{7,4},{8,9},{9,10},{10,1... | collective-permute-start | bytes 1671176 | tf_op jit(solution)/shard_map/ppermute | solution.py:234
  135.1 26.1 %collective-permute-start.15 = (s16[4,544,128]{2,1,0:T(8,128)(2,1)S(1)}, s16[4,544,128]{2,1,0:T(8,128)(2,1)S(1)}, u32[]{:S(2)}, u32[]{:S(2)}) collective-permute-start(s16[4,544,128]{2,1,0:T(8,128)(2,1)S(1)} %get-tuple-element.85), channel_id=1, source_target_pairs={{0,3},{1,0},{2,1},{3,2},{4,7},{5,4},{6,5},{7,6},{8,11},{9,8},{10,9... | collective-permute-start | bytes 1671176 | tf_op jit(solution)/shard_map/ppermute | solution.py:238
  164.3 26.6 %collective-permute-start.16 = (s16[2,4,544,128]{3,2,1,0:T(8,128)(2,1)S(1)}, s16[2,4,544,128]{3,2,1,0:T(8,128)(2,1)S(1)}, u32[]{:S(2)}, u32[]{:S(2)}) collective-permute-start(s16[2,4,544,128]{3,2,1,0:T(8,128)(2,1)S(1)} %get-tuple-element.86), channel_id=1, source_target_pairs={{0,4},{4,8},{8,12},{12,0},{1,5},{5,9},{9,13},{13,1},{2,6},{6,10},{... | collective-permute-start | bytes 3342344 | tf_op jit(solution)/shard_map/ppermute | solution.py:234
  167.8 26.4 %collective-permute-start.17 = (s16[2,4,544,128]{3,2,1,0:T(8,128)(2,1)S(1)}, s16[2,4,544,128]{3,2,1,0:T(8,128)(2,1)S(1)}, u32[]{:S(2)}, u32[]{:S(2)}) collective-permute-start(s16[2,4,544,128]{3,2,1,0:T(8,128)(2,1)S(1)} %get-tuple-element.87), channel_id=1, source_target_pairs={{0,12},{4,0},{8,4},{12,8},{1,13},{5,1},{9,5},{13,9},{2,14},{6,2},{... | collective-permute-start | bytes 3342344 | tf_op jit(solution)/shard_map/ppermute | solution.py:238
  167.8 26.4 %collective-permute-start.18 = (s16[2,4,544,128]{3,2,1,0:T(8,128)(2,1)S(1)}, s16[2,4,544,128]{3,2,1,0:T(8,128)(2,1)S(1)}, u32[]{:S(2)}, u32[]{:S(2)}) collective-permute-start(s16[2,4,544,128]{3,2,1,0:T(8,128)(2,1)S(1)} %get-tuple-element.88), channel_id=1, source_target_pairs={{0,1},{1,2},{2,3},{3,0},{4,5},{5,6},{6,7},{7,4},{8,9},{9,10},{10,1... | collective-permute-start | bytes 3342344 | tf_op jit(solution)/shard_map/ppermute | solution.py:234
  167.8 26.4 %collective-permute-start.19 = (s16[2,4,544,128]{3,2,1,0:T(8,128)(2,1)S(1)}, s16[2,4,544,128]{3,2,1,0:T(8,128)(2,1)S(1)}, u32[]{:S(2)}, u32[]{:S(2)}) collective-permute-start(s16[2,4,544,128]{3,2,1,0:T(8,128)(2,1)S(1)} %get-tuple-element.89), channel_id=1, source_target_pairs={{0,3},{1,0},{2,1},{3,2},{4,7},{5,4},{6,5},{7,6},{8,11},{9,8},{10,9... | collective-permute-start | bytes 3342344 | tf_op jit(solution)/shard_map/ppermute | solution.py:238
  197.7 6.3 %collective-permute-start.20 = (s16[1,544,128]{2,1,0:T(8,128)(2,1)S(1)}, s16[1,544,128]{2,1,0:T(8,128)(2,1)S(1)}, u32[]{:S(2)}, u32[]{:S(2)}) collective-permute-start(s16[1,544,128]{2,1,0:T(8,128)(2,1)S(1)} %get-tuple-element.93), channel_id=1, source_target_pairs={{0,1},{1,2},{2,3},{3,0},{4,5},{5,6},{6,7},{7,4},{8,9},{9,10},{10,1... | collective-permute-start | bytes 417800 | tf_op jit(solution)/shard_map/ppermute | solution.py:234
  197.8 6.3 %collective-permute-start.21 = (s16[1,544,128]{2,1,0:T(8,128)(2,1)S(1)}, s16[1,544,128]{2,1,0:T(8,128)(2,1)S(1)}, u32[]{:S(2)}, u32[]{:S(2)}) collective-permute-start(s16[1,544,128]{2,1,0:T(8,128)(2,1)S(1)} %get-tuple-element.94), channel_id=1, source_target_pairs={{0,3},{1,0},{2,1},{3,2},{4,7},{5,4},{6,5},{7,6},{8,11},{9,8},{10,9... | collective-permute-start | bytes 417800 | tf_op jit(solution)/shard_map/ppermute | solution.py:238
  204.0 6.3 %collective-permute-start.23 = (s16[1,544,128]{2,1,0:T(8,128)(2,1)S(1)}, s16[1,544,128]{2,1,0:T(8,128)(2,1)S(1)}, u32[]{:S(2)}, u32[]{:S(2)}) collective-permute-start(s16[1,544,128]{2,1,0:T(8,128)(2,1)S(1)} %get-tuple-element.98), channel_id=1, source_target_pairs={{0,12},{4,0},{8,4},{12,8},{1,13},{5,1},{9,5},{13,9},{2,14},{6,2},{... | collective-permute-start | bytes 417800 | tf_op jit(solution)/shard_map/ppermute | solution.py:238
  211.0 7.8 %collective-permute-start.24 = (s16[2,544,128]{2,1,0:T(8,128)(2,1)S(1)}, s16[2,544,128]{2,1,0:T(8,128)(2,1)S(1)}, u32[]{:S(2)}, u32[]{:S(2)}) collective-permute-start(s16[2,544,128]{2,1,0:T(8,128)(2,1)S(1)} %get-tuple-element.99), channel_id=1, source_target_pairs={{0,1},{1,2},{2,3},{3,0},{4,5},{5,6},{6,7},{7,4},{8,9},{9,10},{10,1... | collective-permute-start | bytes 835592 | tf_op jit(solution)/shard_map/ppermute | solution.py:234
  211.1 7.7 %collective-permute-start.25 = (s16[2,544,128]{2,1,0:T(8,128)(2,1)S(1)}, s16[2,544,128]{2,1,0:T(8,128)(2,1)S(1)}, u32[]{:S(2)}, u32[]{:S(2)}) collective-permute-start(s16[2,544,128]{2,1,0:T(8,128)(2,1)S(1)} %get-tuple-element.100), channel_id=1, source_target_pairs={{0,3},{1,0},{2,1},{3,2},{4,7},{5,4},{6,5},{7,6},{8,11},{9,8},{10,9... | collective-permute-start | bytes 835592 | tf_op jit(solution)/shard_map/ppermute | solution.py:238
  214.3 6.5 %collective-permute-start.26 = (s16[2,544,128]{2,1,0:T(8,128)(2,1)S(1)}, s16[2,544,128]{2,1,0:T(8,128)(2,1)S(1)}, u32[]{:S(2)}, u32[]{:S(2)}) collective-permute-start(s16[2,544,128]{2,1,0:T(8,128)(2,1)S(1)} %get-tuple-element.101), channel_id=1, source_target_pairs={{0,4},{4,8},{8,12},{12,0},{1,5},{5,9},{9,13},{13,1},{2,6},{6,10},{... | collective-permute-start | bytes 835592 | tf_op jit(solution)/shard_map/ppermute | solution.py:234
  214.3 7.8 %collective-permute-start.27 = (s16[2,544,128]{2,1,0:T(8,128)(2,1)S(1)}, s16[2,544,128]{2,1,0:T(8,128)(2,1)S(1)}, u32[]{:S(2)}, u32[]{:S(2)}) collective-permute-start(s16[2,544,128]{2,1,0:T(8,128)(2,1)S(1)} %get-tuple-element.102), channel_id=1, source_target_pairs={{0,12},{4,0},{8,4},{12,8},{1,13},{5,1},{9,5},{13,9},{2,14},{6,2},{... | collective-permute-start | bytes 835592 | tf_op jit(solution)/shard_map/ppermute | solution.py:238
  (24 other events, 202.4 us)

commit v2 on v1

--- a/solution.py
+++ b/solution.py
@@ -25,11 +25,10 @@
 CORE = 4 * COLS * BATCH + 4 * EXTRA
 THIRD = ROWS * (COLS * BATCH - EXTRA)
 POOL = 2 * CORE + THIRD
-FAR, NEAR = (2,), (1, 3)
 PARTS = 12
 HALF = 512
 PACKED = HALF + HALF // 16
-VMEM_GRANT = 16 * 1024 * 1024
+VMEM_GRANT = 10 * 1024 * 1024
 
 
 def route_kernel(slots_dev, me_ref, slot_ref, out_ref):
@@ -60,33 +59,57 @@
     out_ref[...] = out.astype(jnp.int32)
 
 
-def fill_kernel(index_ref, tiles_ref, first_ref, second_ref):
-    def group(g, carry):
-        codes = [index_ref[g, j] for j in range(CAP)]
-        tiles = [tiles_ref[code // 2] for code in codes]
-        for j in range(CAP):
-            turned = jnp.concatenate([tiles[j][:, TILE:], tiles[j][:, :TILE]], axis=1)
-            tiles[j] = jnp.where(codes[j] % 2 == 1, turned, tiles[j])
-        for j in range(CAP):
-            out_ref = first_ref if j < BATCH else second_ref
-            out_ref[g * BATCH + j % BATCH] = tiles[j]
+def fill_kernel(index_ref, tiles_ref, first_ref, second_ref, filled, sems):
+    copies = []
+    for k, out_ref in enumerate((first_ref, second_ref)):
+
+        def group(g, carry, k=k):
+            codes = [index_ref[g, k * BATCH + j] for j in range(BATCH)]
+            tiles = [tiles_ref[code // 2] for code in codes]
+            for j in range(BATCH):
+                turned = jnp.concatenate([tiles[j][:, TILE:], tiles[j][:, :TILE]], axis=1)
+                filled[k, g * BATCH + j] = jnp.where(codes[j] % 2 == 1, turned, tiles[j])
+            return carry
+
+        lax.fori_loop(0, COLS, group, 0)
+        copies.append(pltpu.make_async_copy(filled.at[k], out_ref, sems.at[k]))
+        copies[k].start()
+    for copy in copies:
+        copy.wait()
+
+
+def mix_kernel(index_ref, second_ref, up_ref, down_ref, up_out, down_out, some_out, rest_out, sems):
+    half = COLS * BATCH // 2
+    copies = [
+        pltpu.make_async_copy(up_ref.at[pl.ds(0, half)], up_out.at[pl.ds(0, half)], sems.at[0]),
+        pltpu.make_async_copy(down_ref.at[pl.ds(half, half)], down_out.at[pl.ds(0, half)], sems.at[1]),
+    ]
+    for copy in copies:
+        copy.start()
+
+    def body(i, carry):
+        tiles = [second_ref[index_ref[i * 16 + k]] for k in range(16)]
+        for k in range(16):
+            some_out[i * 16 + k] = tiles[k]
         return carry
 
-    lax.fori_loop(0, COLS, group, 0)
-
-
-def compact_kernel(index_ref, tiles_ref, first_ref, second_ref):
-    def place(out_ref, base):
-        def body(i, carry):
-            tiles = [tiles_ref[index_ref[base + i * 16 + k]] for k in range(16)]
-            for k in range(16):
-                out_ref[i * 16 + k] = tiles[k]
-            return carry
-
-        lax.fori_loop(0, out_ref.shape[0] // 16, body, 0)
-
-    place(first_ref, 0)
-    place(second_ref, EXTRA)
+    lax.fori_loop(0, EXTRA // 16, body, 0)
+    copies += [
+        pltpu.make_async_copy(some_out, up_out.at[pl.ds(half, EXTRA)], sems.at[2]),
+        pltpu.make_async_copy(some_out, down_out.at[pl.ds(half, EXTRA)], sems.at[3]),
+    ]
+    for copy in copies[2:]:
+        copy.start()
+
+    def body_rest(i, carry):
+        tiles = [second_ref[index_ref[EXTRA + i * 16 + k]] for k in range(16)]
+        for k in range(16):
+            rest_out[i * 16 + k] = tiles[k]
+        return carry
+
+    lax.fori_loop(0, (COLS * BATCH - EXTRA) // 16, body_rest, 0)
+    for copy in copies:
+        copy.wait()
 
 
 def prep_kernel(mask_ref, amp_ref, even_ref, odd_ref):
@@ -187,7 +210,7 @@
                 outs[way][unit] = value
                 continue
             for half in range(2):
-                out_ref = outs[2 * way + half] if hops == FAR else outs[2 * way + at].at[half]
+                out_ref = outs[2 * way + half] if len(hops) == 1 else outs[2 * way + at].at[half]
                 pack(out_ref.at[unit], value[half * HALF : (half + 1) * HALF])
 
     for at, hop in enumerate(hops):
@@ -203,31 +226,34 @@
         lax.fori_loop(0, 2, two_units, 0)
 
 
-def product_call(name, hops, scalars, even, odd, tiles):
-    rows_dev, depth_half = even.shape
+def product_call(name, hops, scalars, arrays):
+    rows_dev, depth_half = arrays[0].shape
     vmem = pl.BlockSpec(memory_space=pltpu.VMEM)
-    if hops == FAR:
+    if hops == (0,):
+        outs = [jax.ShapeDtypeStruct((4, rows_dev, 128), jnp.float32)] * 2
+    elif len(hops) == 1:
         outs = [jax.ShapeDtypeStruct((4, PACKED, 128), jnp.int16)] * 4
-    elif hops == NEAR:
+    else:
         outs = [jax.ShapeDtypeStruct((2, 4, PACKED, 128), jnp.int16)] * 4
-    else:
-        outs = [jax.ShapeDtypeStruct((4, rows_dev, 128), jnp.float32)] * 2
-    return pl.pallas_call(
+    handed = [] if hops == (0,) else [jax.ShapeDtypeStruct(a.shape, a.dtype) for a in arrays]
+    result = pl.pallas_call(
         functools.partial(product_kernel, hops),
         grid_spec=pltpu.PrefetchScalarGridSpec(
             num_scalar_prefetch=2,
             grid=(),
             in_specs=[vmem] * 3,
-            out_specs=[vmem] * len(outs),
+            out_specs=[vmem] * (len(outs) + len(handed)),
             scratch_shapes=[pltpu.VMEM((depth_half, 256), jnp.bfloat16)] * 4,
         ),
-        out_shape=outs,
+        out_shape=outs + handed,
+        input_output_aliases={2 + k: len(outs) + k for k in range(len(handed))},
         compiler_params=pltpu.CompilerParams(vmem_limit_bytes=VMEM_GRANT),
         cost_estimate=pl.CostEstimate(
             flops=8 * len(hops) * rows_dev * depth_half * 512, bytes_accessed=POOL * 8192, transcendentals=0
         ),
         name=name,
-    )(*scalars, even, odd, tiles)
+    )(*scalars, *arrays)
+    return result[: len(outs)], result[len(outs) :]
 
 
 def ahead(axis, value):
@@ -338,12 +364,20 @@
     outgoing = pl.pallas_call(
         fill_kernel,
         grid_spec=pltpu.PrefetchScalarGridSpec(
-            num_scalar_prefetch=1, grid=(), in_specs=[vmem], out_specs=[vmem] * 2
+            num_scalar_prefetch=1,
+            grid=(),
+            in_specs=[vmem],
+            out_specs=[pl.BlockSpec(memory_space=pl.ANY)] * 2,
+            scratch_shapes=[
+                pltpu.VMEM((2, COLS * BATCH, SUB, 128), jnp.bfloat16),
+                pltpu.SemaphoreType.DMA((2,)),
+            ],
         ),
         out_shape=[batch] * 2,
         compiler_params=pltpu.CompilerParams(vmem_limit_bytes=VMEM_GRANT),
         name="fill",
     )(send_index, eri_tiles.reshape(slots_dev, SUB, 128))
+
     def send(part):
         part = part.reshape(COLS, BATCH, SUB, 128)
         part = lax.all_to_all(part, ("x", "z"), split_axis=0, concat_axis=0, tiled=True)
@@ -353,7 +387,6 @@
     first, second, eri_slot = lax.optimization_barrier((first, outgoing[1], eri_slot))
     up, down = reach(first)
     second = send(second)
-
     devices = jnp.arange(DEVS, dtype=jnp.int32)
     owner_all = jnp.where(eri_slot >= 0, eri_slot // slots_dev, -1).reshape(COLS, 1, GROUP)
     held = jnp.sum((owner_all == devices[None, :, None]).astype(jnp.int32), axis=2)
@@ -368,23 +401,31 @@
     inside = jnp.logical_and(spot[:, None] >= mine_start[None, :], spot[:, None] < mine_upto[None, :])
     source = jnp.arange(COLS, dtype=jnp.int32)[None, :] * BATCH + spot[:, None] - mine_start[None, :]
     source = jnp.sum(jnp.where(inside, source, 0), axis=1).astype(jnp.int32)
-    some, rest = pl.pallas_call(
-        compact_kernel,
+    second, up, down, source, spill = lax.optimization_barrier((second, up, down, source, spill))
+    half = COLS * BATCH // 2
+    mixed = jax.ShapeDtypeStruct((half + EXTRA, SUB, 128), jnp.bfloat16)
+    from_up, from_down, some, rest = pl.pallas_call(
+        mix_kernel,
         grid_spec=pltpu.PrefetchScalarGridSpec(
-            num_scalar_prefetch=1, grid=(), in_specs=[vmem], out_specs=[vmem] * 2
+            num_scalar_prefetch=1,
+            grid=(),
+            in_specs=[vmem] * 3,
+            out_specs=[vmem] * 4,
+            scratch_shapes=[pltpu.SemaphoreType.DMA((4,))],
         ),
-        out_shape=[
+        out_shape=[mixed] * 2
+        + [
             jax.ShapeDtypeStruct((EXTRA, SUB, 128), jnp.bfloat16),
             jax.ShapeDtypeStruct((COLS * BATCH - EXTRA, SUB, 128), jnp.bfloat16),
         ],
         compiler_params=pltpu.CompilerParams(vmem_limit_bytes=VMEM_GRANT),
-        name="compact",
-    )(source, second)
+        name="mix",
+    )(source, second, up, down)
+    from_up, from_down = ahead("y", from_up), behind("y", from_down)
     wanted = lax.dynamic_slice_in_dim(eri_slot, group * GROUP, GROUP)
-    up, down, amplitudes, wanted = lax.optimization_barrier((up, down, amplitudes, wanted))
-    half = COLS * BATCH // 2
-    from_up = ahead("y", jnp.concatenate([up[:half], some]))
-    from_down = behind("y", jnp.concatenate([down[half:], some]))
+    some, up, down, amplitudes, wanted = lax.optimization_barrier((some, up, down, amplitudes, wanted))
+    swapped = swap([first, up, down])
+
     parted = jax.ShapeDtypeStruct((rows_dev, depth_dev // 2), jnp.bfloat16)
     even, odd = pl.pallas_call(
         prep_kernel,
@@ -436,13 +477,13 @@
             behind("y", from_down[half + EXTRA // 2 :]),
         ]
     )
-    same = [first, up, down, from_up, from_down, tail]
-    tiles = collect_call(misc, same + swap(same), third)
-
-    scalars, arrays = (tile_index, misc), (even, odd, tiles)
-    far = product_call("far", FAR, scalars, *arrays)
-    near = product_call("near", NEAR, scalars, *arrays)
+    late_parts = [from_up, from_down, tail]
+    tiles = collect_call(misc, [first, up, down, *late_parts, *swapped, *swap(late_parts)], third)
+
+    scalars = (tile_index, misc)
+    far, arrays = product_call("far", (2,), scalars, (even, odd, tiles))
     axes = ("x", "z")
+    near, arrays = product_call("near", (1, 3), scalars, arrays)
     inputs = []
     for way, axis in enumerate(axes):
         inputs += [*near[2 * way : 2 * way + 2], ahead(axis, far[2 * way]), behind(axis, far[2 * way + 1])]
@@ -451,7 +492,7 @@
     came = []
     for way, axis in enumerate(axes):
         came += [ahead(axis, added[2 * way]), behind(axis, added[2 * way + 1])]
-    one, two = product_call("own", (0,), scalars, *arrays)
+    (one, two), _ = product_call("own", (0,), scalars, arrays)
     single = jax.ShapeDtypeStruct((1, PACKED, 128), jnp.int16)
     double = jax.ShapeDtypeStruct((2, PACKED, 128), jnp.int16)
     *outs, own = whole_call(

time: 231 us -> 217 us (0.939)
  local copies, waits for them, and re-layouts: 32.6 us -> 15 us
  Pallas kernels: 50.8 us -> 54.1 us
    unnamed x39 -> x27, local copies, waits for them, and re-layouts: 25.2 us -> 8.92 us
    ppermute x11, waiting for transfers between devices: 21.4 us -> 33.2 us  [ahead(): return lax.ppermute(value, axis, [(i, (i + 1) % 4) for i in range(4)])]
    ppermute x11, starting transfers between devices: 17.9 us -> 25.8 us  [behind(): return lax.ppermute(value, axis, [(i, (i + 3) % 4) for i in range(4)])]
    ppermute x11, starting transfers between devices: 13.4 us -> 6.01 us  [ahead(): return lax.ppermute(value, axis, [(i, (i + 1) % 4) for i in range(4)])]
    ppermute x11, waiting for transfers between devices: 19 us -> 13.1 us  [behind(): return lax.ppermute(value, axis, [(i, (i + 3) % 4) for i in range(4)])]
    all_to_all x2, waiting for transfers between devices: 34.7 us -> 30.3 us  [send(): lax.all_to_all(part, ('x', 'z'), split_axis=0, concat_axis=0, tiled=True)]
    pallas_call x1, Pallas kernels: 1.71 us -> 4.92 us  [shards(): pl.pallas_call(mix_kernel, grid_spec=pltpu.PrefetchScalarGridSpec(num_sca...]
  transfers between devices with their start and end apart: 30 -> 30, of which waited for: 17 -> 16; matrix products, arithmetic and copies ran while one was open for 6% -> 6% of each run, Pallas kernels for 12% -> 11%
where the time goes in v2:
time: 217 us
  waiting for transfers between devices  79.6 us (37%)
  Pallas kernels  54.1 us (25%)
  starting transfers between devices  47.9 us (22%)
  local copies, waits for them, and re-layouts  15 us (7%)
  between operations  14.5 us (7%)
  other arithmetic  3.86 us (2%)
    ppermute x11, waiting for transfers between devices, ahead(): return lax.ppermute(value, axis, [(i, (i + 1) % 4) for i in range(4)])  33.2 us
    all_to_all x2, waiting for transfers between devices, send(): lax.all_to_all(part, ('x', 'z'), split_axis=0, concat_axis=0, tiled=True)  30.3 us
    pallas_call x3, Pallas kernels, product_call(): pl.pallas_call(functools.partial(product_kernel, hops), grid_spec=pltpu.P...  26.1 us
    ppermute x11, starting transfers between devices, behind(): return lax.ppermute(value, axis, [(i, (i + 3) % 4) for i in range(4)])  25.8 us
    all_to_all x2, starting transfers between devices, send(): lax.all_to_all(part, ('x', 'z'), split_axis=0, concat_axis=0, tiled=True)  14.9 us
    ppermute x11, waiting for transfers between devices, behind(): return lax.ppermute(value, axis, [(i, (i + 3) % 4) for i in range(4)])  13.1 us
    unnamed x27, local copies, waits for them, and re-layouts  8.92 us
    pallas_call x4, Pallas kernels, whole_call(): pl.pallas_call(body, in_specs=[pl.BlockSpec(memory_space=pltpu.SMEM)] * l...  8.74 us
  transfers between devices with their start and end apart: 30, of which 16 were waited for; matrix products, arithmetic and copies ran while one was open for 6% of the time, Pallas kernels for 11%

profile of v2, /device:TPU:6, one launch (start us, length us, event | category | flops | bytes accessed | tf_op | source)
XLA Modules:
  0.0 217.0 jit_solution(8359198433881825160)
XLA Ops:
  9.8 4.6 %fill.1 = (bf16[160,32,128]{2,1,0:T(8,128)(2,1)S(1)}, bf16[160,32,128]{2,1,0:T(8,128)(2,1)S(1)}) custom-call(s32[16,128]{1,0:T(8,128)S(1)} %route.1.index_ref, bf16[320,32,128]{2,1,0:T(8,128)(2,1)S(1)} %bitcast.18), custom_call_target="tpu_custom_call" | custom-call | tf_op jit(solution)/shard_map/fill/pallas_call | solution.py:364
  16.6 8.3 %all-to-all-start = ((bf16[16,10,32,128]{3,2,1,0:T(8,128)(2,1)}), bf16[16,10,32,128]{3,2,1,0:T(8,128)(2,1)S(1)}, u32[]{:S(2)}, u32[]{:S(2)}) async-start(bf16[16,10,32,128]{3,2,1,0:T(8,128)(2,1)} %bitcast.24), calls=%async_computation | async-start | bytes 2621440 | tf_op jit(solution)/shard_map/all_to_all | solution.py:383
  24.9 18.4 %all-to-all-done = bf16[16,10,32,128]{3,2,1,0:T(8,128)(2,1)S(1)} async-done(((bf16[16,10,32,128]{3,2,1,0:T(8,128)(2,1)}), bf16[16,10,32,128]{3,2,1,0:T(8,128)(2,1)S(1)}, u32[]{:S(2)}, u32[]{:S(2)}) %all-to-all-start) | async-done | bytes 1310752 | tf_op jit(solution)/shard_map/all_to_all | solution.py:383
  46.3 6.7 %all-to-all-start.1 = ((bf16[16,10,32,128]{3,2,1,0:T(8,128)(2,1)}), bf16[16,10,32,128]{3,2,1,0:T(8,128)(2,1)}, u32[]{:S(2)}, u32[]{:S(2)}) async-start(bf16[16,10,32,128]{3,2,1,0:T(8,128)(2,1)} %bitcast.23), calls=%async_computation.1 | async-start | bytes 2621440 | tf_op jit(solution)/shard_map/all_to_all | solution.py:383
  56.7 11.9 %all-to-all-done.1 = bf16[16,10,32,128]{3,2,1,0:T(8,128)(2,1)} async-done(((bf16[16,10,32,128]{3,2,1,0:T(8,128)(2,1)}), bf16[16,10,32,128]{3,2,1,0:T(8,128)(2,1)}, u32[]{:S(2)}, u32[]{:S(2)}) %all-to-all-start.1) | async-done | bytes 1310752 | tf_op jit(solution)/shard_map/all_to_all | solution.py:383
  68.5 4.0 %collective-permute-done.1.down_ref.refs_2_ = bf16[160,32,128]{2,1,0:T(8,128)(2,1)S(1)} collective-permute-done((bf16[160,32,128]{2,1,0:T(8,128)(2,1)S(1)}, bf16[160,32,128]{2,1,0:T(8,128)(2,1)S(1)}, u32[]{:S(2)}, u32[]{:S(2)}) %collective-permute-start.1) | collective-permute-done | bytes 1310752 | tf_op jit(solution)/shard_map/ppermute | solution.py:264
  72.5 3.5 %collective-permute-done.up_ref.refs_1_ = bf16[160,32,128]{2,1,0:T(8,128)(2,1)} collective-permute-done((bf16[160,32,128]{2,1,0:T(8,128)(2,1)S(1)}, bf16[160,32,128]{2,1,0:T(8,128)(2,1)}, u32[]{:S(2)}, u32[]{:S(2)}) %collective-permute-start) | collective-permute-done | bytes 1310752 | tf_op jit(solution)/shard_map/ppermute | solution.py:260
  76.0 4.9 %mix.1 = (bf16[128,32,128]{2,1,0:T(8,128)(2,1)}, bf16[128,32,128]{2,1,0:T(8,128)(2,1)}, bf16[48,32,128]{2,1,0:T(8,128)(2,1)S(1)}, bf16[112,32,128]{2,1,0:T(8,128)(2,1)}) custom-call(s32[160]{0:T(256)S(1)} %select_reduce_fusion.2.index_ref, bf16[160,32,128]{2,1,0:T(8,128)(2,1)} %bitcast.5.second_ref, ...), custom_call_target="tpu_custom_call" | custom-call | tf_op jit(solution)/shard_map/mix/pallas_call | solution.py:407
  81.7 3.2 %collective-permute-start.3 = (bf16[128,32,128]{2,1,0:T(8,128)(2,1)}, bf16[128,32,128]{2,1,0:T(8,128)(2,1)}, u32[]{:S(2)}, u32[]{:S(2)}) collective-permute-start(bf16[128,32,128]{2,1,0:T(8,128)(2,1)} %get-tuple-element.80), channel_id=1, source_target_pairs={{0,96},{32,0},{64,32},{96,64},{1,97},{33,1},{65,33},{97,65},{2,98}... | collective-permute-start | bytes 3145736 | tf_op jit(solution)/shard_map/ppermute | solution.py:264
  88.1 5.7 %prep.1 = (bf16[1024,1024]{1,0:T(8,128)(2,1)S(1)}, bf16[1024,1024]{1,0:T(8,128)(2,1)S(1)}) custom-call(s32[16,32]{1,0:T(8,128)S(1)} %copy-done.10, bf16[1024,2048]{1,0:T(8,128)(2,1)S(1)} %copy-done.4), custom_call_target="tpu_custom_call" | custom-call | tf_op jit(solution)/shard_map/prep/pallas_call | solution.py:430
  95.2 3.9 %conditional.1 = (bf16[896,32,128]{2,1,0:T(8,128)(2,1)}) conditional(s32[]{:T(128)} %convert_element_type.18, () %tuple.18, bf16[112,32,128]{2,1,0:T(8,128)(2,1)} %get-tuple-element.87), branch_computations={%region_7.8_spmd, %region_8.9_spmd} | conditional | bytes 24772656 | solution.py:464
  95.2 3.9 %broadcast.56 = bf16[896,32,128]{2,1,0:T(8,128)(2,1)} broadcast(bf16[]{:T(256)} %constant.115.clone), dimensions={} | broadcast | bytes 7340034 | tf_op jit(solution)/shard_map/broadcast.10
  101.5 3.6 %collective-permute-done.2.refs_3_ = bf16[128,32,128]{2,1,0:T(8,128)(2,1)} collective-permute-done((bf16[128,32,128]{2,1,0:T(8,128)(2,1)}, bf16[128,32,128]{2,1,0:T(8,128)(2,1)}, u32[]{:S(2)}, u32[]{:S(2)}) %collective-permute-start.2) | collective-permute-done | bytes 1048608 | tf_op jit(solution)/shard_map/ppermute | solution.py:260
  112.3 4.7 %collective-permute-done.4 = bf16[24,32,128]{2,1,0:T(8,128)(2,1)S(1)} collective-permute-done((bf16[24,32,128]{2,1,0:T(8,128)(2,1)S(1)}, bf16[24,32,128]{2,1,0:T(8,128)(2,1)S(1)}, u32[]{:S(2)}, u32[]{:S(2)}) %collective-permute-start.4) | collective-permute-done | bytes 196640 | tf_op jit(solution)/shard_map/ppermute | solution.py:260
  120.8 3.1 %collect.1.tiles = bf16[2561,32,128]{2,1,0:T(8,128)(2,1)S(1)} custom-call(s32[3]{0:T(128)S(1)} %pad_add_fusion.misc_ref, bf16[160,32,128]{2,1,0:T(8,128)(2,1)S(1)} %bitcast.22, bf16[160,32,128]{2,1,0:T(8,128)(2,1)} %collective-permute-done.up_ref.refs_1_, bf16[160,32,128]{2,1,0:T(8,128)(2,1)S(1)} %copy-done.3, ...), custom_call_target="tpu_custom_call" | custom-call | bytes 20971520 | tf_op jit(solution)/shard_map/collect/pallas_call | solution.py:174
  123.9 7.0 %far.1 = (s16[4,544,128]{2,1,0:T(8,128)(2,1)S(1)}, s16[4,544,128]{2,1,0:T(8,128)(2,1)S(1)}, s16[4,544,128]{2,1,0:T(8,128)(2,1)S(1)}, s16[4,544,128]{2,1,0:T(8,12...) custom-call(s32[2048]{0:T(1024)S(1)} %select_select_fusion.index_ref, ...), custom_call_target="tpu_custom_call", output_to_operand_aliasing={{4}: (2, {}), {5}: (3, {}), {6}: (4, {})} | custom-call | flops 4294967296 | bytes 20971520 | tf_op jit(solution)/shard_map/far/pallas_call | solution.py:239
  136.2 13.1 %near.1 = (s16[2,4,544,128]{3,2,1,0:T(8,128)(2,1)S(1)}, s16[2,4,544,128]{3,2,1,0:T(8,128)(2,1)S(1)}, s16[2,4,544,128]{3,2,1,0:T(8,128)(2,1)S(1)}, s16[2,4,544,12...) custom-call(s32[2048]{0:T(1024)S(1)} %select_select_fusion.index_ref, ...), custom_call_target="tpu_custom_call", output_to_operand_aliasing={{4}: (2, {}), {5}: (3, {}), {6}: (4, {})} | custom-call | flops 8589934592 | bytes 20971520 | tf_op jit(solution)/shard_map/near/pallas_call | solution.py:239
  149.3 3.1 %add_first.1 = (s16[2,4,544,128]{3,2,1,0:T(8,128)(2,1)S(1)}, s16[2,4,544,128]{3,2,1,0:T(8,128)(2,1)S(1)}, s16[2,4,544,128]{3,2,1,0:T(8,128)(2,1)S(1)}, s16[2,4,544,128]{3,2,1,0:T(8,128)(2,1)S(1)}) custom-call(s16[2,4,544,128]{3,2,1,0:T(8,128)(2,1)S(1)} %get-tuple-element.106.refs_0_, s16[2,4,544,128]{3,2,1,0:T(8,128)(2,1)S(1)} %get-tuple-element.107.refs_1_, ...), custom_call_target="tpu_custom_call" | custom-call | flops 111411200 | bytes 11141120 | tf_op jit(solution)/shard_map/add_first/pallas_call | solution.py:302
  154.8 3.2 %collective-permute-start.19 = (s16[2,4,544,128]{3,2,1,0:T(8,128)(2,1)S(1)}, s16[2,4,544,128]{3,2,1,0:T(8,128)(2,1)S(1)}, u32[]{:S(2)}, u32[]{:S(2)}) collective-permute-start(s16[2,4,544,128]{3,2,1,0:T(8,128)(2,1)S(1)} %get-tuple-element.117), channel_id=1, source_target_pairs={{0,3},{1,0},{2,1},{3,2},{4,7},{5,4},{6,5},{7,6},{8,11},{9,8},{10,9... | collective-permute-start | bytes 3342344 | tf_op jit(solution)/shard_map/ppermute | solution.py:264
  158.0 6.0 %own.1 = (f32[4,1024,128]{2,1,0:T(8,128)S(1)}, f32[4,1024,128]{2,1,0:T(8,128)S(1)}) custom-call(s32[2048]{0:T(1024)S(1)} %select_select_fusion.index_ref, s32[3]{0:T(128)S(1)} %pad_add_fusion.misc_ref, bf16[1024,1024]{1,0:T(8,128)(2,1)S(1)} %get-tuple-element.101.even_ref, bf16[1024,1024]{1,0:T(8,128)(2,1)S(1)} %get-tuple-element.102.odd_ref, ...), custom_call_target="tpu_custom_call" | custom-call | flops 4294967296 | bytes 20971520 | tf_op jit(solution)/shard_map/own/pallas_call | solution.py:239
  164.0 14.2 %collective-permute-done.16.refs_0_ = s16[2,4,544,128]{3,2,1,0:T(8,128)(2,1)S(1)} collective-permute-done((s16[2,4,544,128]{3,2,1,0:T(8,128)(2,1)S(1)}, s16[2,4,544,128]{3,2,1,0:T(8,128)(2,1)S(1)}, u32[]{:S(2)}, u32[]{:S(2)}) %collective-permute-start.16) | collective-permute-done | bytes 1114144 | tf_op jit(solution)/shard_map/ppermute | solution.py:260
  180.9 3.5 %middle.1 = (s16[1,544,128]{2,1,0:T(8,128)(2,1)S(1)}, s16[1,544,128]{2,1,0:T(8,128)(2,1)S(1)}, s16[2,544,128]{2,1,0:T(8,128)(2,1)S(1)}, s16[2,544,128]{2,1,0:T(8...) custom-call(s32[3]{0:T(128)S(1)} %pad_add_fusion.misc_ref, ...), custom_call_target="tpu_custom_call" | custom-call | flops 113704960 | bytes 11370496 | tf_op jit(solution)/shard_map/middle/pallas_call | solution.py:302
  193.2 3.7 %collective-permute-done.23.refs_7_ = s16[1,544,128]{2,1,0:T(8,128)(2,1)S(1)} collective-permute-done((s16[1,544,128]{2,1,0:T(8,128)(2,1)S(1)}, s16[1,544,128]{2,1,0:T(8,128)(2,1)S(1)}, u32[]{:S(2)}, u32[]{:S(2)}) %collective-permute-start.23) | collective-permute-done | bytes 139296 | tf_op jit(solution)/shard_map/ppermute | solution.py:264
  197.7 3.2 %collective-permute-start.25 = (s16[2,544,128]{2,1,0:T(8,128)(2,1)S(1)}, s16[2,544,128]{2,1,0:T(8,128)(2,1)S(1)}, u32[]{:S(2)}, u32[]{:S(2)}) collective-permute-start(s16[2,544,128]{2,1,0:T(8,128)(2,1)S(1)} %get-tuple-element.128), channel_id=1, source_target_pairs={{0,3},{1,0},{2,1},{3,2},{4,7},{5,4},{6,5},{7,6},{8,11},{9,8},{10,9... | collective-permute-start | bytes 835592 | tf_op jit(solution)/shard_map/ppermute | solution.py:264
  (105 shorter events, 59.1 us)
Async XLA Ops:
  16.6 26.7 %all-to-all-start = ((bf16[16,10,32,128]{3,2,1,0:T(8,128)(2,1)}), bf16[16,10,32,128]{3,2,1,0:T(8,128)(2,1)S(1)}, u32[]{:S(2)}, u32[]{:S(2)}) async-start(bf16[16,10,32,128]{3,2,1,0:T(8,128)(2,1)} %bitcast.24), calls=%async_computation | async-start | bytes 2621440 | tf_op jit(solution)/shard_map/all_to_all | solution.py:383
  43.3 29.2 %collective-permute-start.1 = (bf16[160,32,128]{2,1,0:T(8,128)(2,1)S(1)}, bf16[160,32,128]{2,1,0:T(8,128)(2,1)S(1)}, u32[]{:S(2)}, u32[]{:S(2)}) collective-permute-start(bf16[160,32,128]{2,1,0:T(8,128)(2,1)S(1)} %bitcast.19), channel_id=1, source_target_pairs={{0,96},{32,0},{64,32},{96,64},{1,97},{33,1},{65,33},{97,65},{2,98}... | collective-permute-start | bytes 3932168 | tf_op jit(solution)/shard_map/ppermute | solution.py:264
  46.3 29.7 %collective-permute-start = (bf16[160,32,128]{2,1,0:T(8,128)(2,1)S(1)}, bf16[160,32,128]{2,1,0:T(8,128)(2,1)}, u32[]{:S(2)}, u32[]{:S(2)}) collective-permute-start(bf16[160,32,128]{2,1,0:T(8,128)(2,1)S(1)} %bitcast.20), channel_id=1, source_target_pairs={{0,32},{32,64},{64,96},{96,0},{1,33},{33,65},{65,97},{97,1},{2,34}... | collective-permute-start | bytes 3932168 | tf_op jit(solution)/shard_map/ppermute | solution.py:260
  46.3 22.2 %all-to-all-start.1 = ((bf16[16,10,32,128]{3,2,1,0:T(8,128)(2,1)}), bf16[16,10,32,128]{3,2,1,0:T(8,128)(2,1)}, u32[]{:S(2)}, u32[]{:S(2)}) async-start(bf16[16,10,32,128]{3,2,1,0:T(8,128)(2,1)} %bitcast.23), calls=%async_computation.1 | async-start | bytes 2621440 | tf_op jit(solution)/shard_map/all_to_all | solution.py:383
  81.7 23.4 %collective-permute-start.2 = (bf16[128,32,128]{2,1,0:T(8,128)(2,1)}, bf16[128,32,128]{2,1,0:T(8,128)(2,1)}, u32[]{:S(2)}, u32[]{:S(2)}) collective-permute-start(bf16[128,32,128]{2,1,0:T(8,128)(2,1)} %get-tuple-element.79), channel_id=1, source_target_pairs={{0,32},{32,64},{64,96},{96,0},{1,33},{33,65},{65,97},{97,1},{2,34}... | collective-permute-start | bytes 3145736 | tf_op jit(solution)/shard_map/ppermute | solution.py:260
  81.7 23.4 %collective-permute-start.3 = (bf16[128,32,128]{2,1,0:T(8,128)(2,1)}, bf16[128,32,128]{2,1,0:T(8,128)(2,1)}, u32[]{:S(2)}, u32[]{:S(2)}) collective-permute-start(bf16[128,32,128]{2,1,0:T(8,128)(2,1)} %get-tuple-element.80), channel_id=1, source_target_pairs={{0,96},{32,0},{64,32},{96,64},{1,97},{33,1},{65,33},{97,65},{2,98}... | collective-permute-start | bytes 3145736 | tf_op jit(solution)/shard_map/ppermute | solution.py:264
  85.0 32.1 %collective-permute-start.6 = (bf16[160,32,128]{2,1,0:T(8,128)(2,1)S(1)}, bf16[160,32,128]{2,1,0:T(8,128)(2,1)}, u32[]{:S(2)}, u32[]{:S(2)}) collective-permute-start(bf16[160,32,128]{2,1,0:T(8,128)(2,1)S(1)} %bitcast.21), channel_id=1, source_target_pairs={{0,16},{16,0},{1,17},{17,1},{2,18},{18,2},{3,19},{19,3},{4,20},{20... | collective-permute-start | bytes 3932168 | tf_op jit(solution)/shard_map/ppermute | solution.py:272
  110.0 6.9 %collective-permute-start.4 = (bf16[24,32,128]{2,1,0:T(8,128)(2,1)S(1)}, bf16[24,32,128]{2,1,0:T(8,128)(2,1)S(1)}, u32[]{:S(2)}, u32[]{:S(2)}) collective-permute-start(bf16[24,32,128]{2,1,0:T(8,128)(2,1)S(1)} %slice.6), channel_id=1, source_target_pairs={{0,32},{32,64},{64,96},{96,0},{1,33},{33,65},{65,97},{97,1},{2,34}... | collective-permute-start | bytes 589832 | tf_op jit(solution)/shard_map/ppermute | solution.py:260
  110.1 7.6 %collective-permute-start.7 = (bf16[160,32,128]{2,1,0:T(8,128)(2,1)}, bf16[160,32,128]{2,1,0:T(8,128)(2,1)S(1)}, u32[]{:S(2)}, u32[]{:S(2)}) collective-permute-start(bf16[160,32,128]{2,1,0:T(8,128)(2,1)} %collective-permute-done.up_ref.refs_1_), channel_id=1, source_target_pairs={{0,16},{16,0},{1,17},{17,1},{2,18},{18,2},{3,19},{19,3},{4,20},{20... | collective-permute-start | bytes 3932168 | tf_op jit(solution)/shard_map/ppermute | solution.py:272
  110.2 7.5 %collective-permute-start.8 = (bf16[160,32,128]{2,1,0:T(8,128)(2,1)S(1)}, bf16[160,32,128]{2,1,0:T(8,128)(2,1)S(1)}, u32[]{:S(2)}, u32[]{:S(2)}) collective-permute-start(bf16[160,32,128]{2,1,0:T(8,128)(2,1)S(1)} %copy-done.3), channel_id=1, source_target_pairs={{0,16},{16,0},{1,17},{17,1},{2,18},{18,2},{3,19},{19,3},{4,20},{20... | collective-permute-start | bytes 3932168 | tf_op jit(solution)/shard_map/ppermute | solution.py:272
  112.3 8.5 %collective-permute-start.9 = (bf16[128,32,128]{2,1,0:T(8,128)(2,1)}, bf16[128,32,128]{2,1,0:T(8,128)(2,1)S(1)}, u32[]{:S(2)}, u32[]{:S(2)}) collective-permute-start(bf16[128,32,128]{2,1,0:T(8,128)(2,1)} %collective-permute-done.2.refs_3_), channel_id=1, source_target_pairs={{0,16},{16,0},{1,17},{17,1},{2,18},{18,2},{3,19},{19,3},{4,20},{20... | collective-permute-start | bytes 3145736 | tf_op jit(solution)/shard_map/ppermute | solution.py:272
  130.9 18.4 %collective-permute-start.12 = (s16[4,544,128]{2,1,0:T(8,128)(2,1)S(1)}, s16[4,544,128]{2,1,0:T(8,128)(2,1)S(1)}, u32[]{:S(2)}, u32[]{:S(2)}) collective-permute-start(s16[4,544,128]{2,1,0:T(8,128)(2,1)S(1)} %get-tuple-element.108), channel_id=1, source_target_pairs={{0,4},{4,8},{8,12},{12,0},{1,5},{5,9},{9,13},{13,1},{2,6},{6,10},{... | collective-permute-start | bytes 1671176 | tf_op jit(solution)/shard_map/ppermute | solution.py:260
  131.1 18.2 %collective-permute-start.13 = (s16[4,544,128]{2,1,0:T(8,128)(2,1)S(1)}, s16[4,544,128]{2,1,0:T(8,128)(2,1)S(1)}, u32[]{:S(2)}, u32[]{:S(2)}) collective-permute-start(s16[4,544,128]{2,1,0:T(8,128)(2,1)S(1)} %get-tuple-element.109), channel_id=1, source_target_pairs={{0,12},{4,0},{8,4},{12,8},{1,13},{5,1},{9,5},{13,9},{2,14},{6,2},{... | collective-permute-start | bytes 1671176 | tf_op jit(solution)/shard_map/ppermute | solution.py:264
  133.0 16.3 %collective-permute-start.14 = (s16[4,544,128]{2,1,0:T(8,128)(2,1)S(1)}, s16[4,544,128]{2,1,0:T(8,128)(2,1)S(1)}, u32[]{:S(2)}, u32[]{:S(2)}) collective-permute-start(s16[4,544,128]{2,1,0:T(8,128)(2,1)S(1)} %get-tuple-element.112), channel_id=1, source_target_pairs={{0,1},{1,2},{2,3},{3,0},{4,5},{5,6},{6,7},{7,4},{8,9},{9,10},{10,1... | collective-permute-start | bytes 1671176 | tf_op jit(solution)/shard_map/ppermute | solution.py:260
  133.6 15.8 %collective-permute-start.15 = (s16[4,544,128]{2,1,0:T(8,128)(2,1)S(1)}, s16[4,544,128]{2,1,0:T(8,128)(2,1)S(1)}, u32[]{:S(2)}, u32[]{:S(2)}) collective-permute-start(s16[4,544,128]{2,1,0:T(8,128)(2,1)S(1)} %get-tuple-element.113), channel_id=1, source_target_pairs={{0,3},{1,0},{2,1},{3,2},{4,7},{5,4},{6,5},{7,6},{8,11},{9,8},{10,9... | collective-permute-start | bytes 1671176 | tf_op jit(solution)/shard_map/ppermute | solution.py:264
  152.4 25.8 %collective-permute-start.16 = (s16[2,4,544,128]{3,2,1,0:T(8,128)(2,1)S(1)}, s16[2,4,544,128]{3,2,1,0:T(8,128)(2,1)S(1)}, u32[]{:S(2)}, u32[]{:S(2)}) collective-permute-start(s16[2,4,544,128]{3,2,1,0:T(8,128)(2,1)S(1)} %get-tuple-element.114), channel_id=1, source_target_pairs={{0,4},{4,8},{8,12},{12,0},{1,5},{5,9},{9,13},{13,1},{2,6},{6,10},{... | collective-permute-start | bytes 3342344 | tf_op jit(solution)/shard_map/ppermute | solution.py:260
  154.2 26.7 %collective-permute-start.17 = (s16[2,4,544,128]{3,2,1,0:T(8,128)(2,1)S(1)}, s16[2,4,544,128]{3,2,1,0:T(8,128)(2,1)S(1)}, u32[]{:S(2)}, u32[]{:S(2)}) collective-permute-start(s16[2,4,544,128]{3,2,1,0:T(8,128)(2,1)S(1)} %get-tuple-element.115), channel_id=1, source_target_pairs={{0,12},{4,0},{8,4},{12,8},{1,13},{5,1},{9,5},{13,9},{2,14},{6,2},{... | collective-permute-start | bytes 3342344 | tf_op jit(solution)/shard_map/ppermute | solution.py:264
  154.7 26.1 %collective-permute-start.18 = (s16[2,4,544,128]{3,2,1,0:T(8,128)(2,1)S(1)}, s16[2,4,544,128]{3,2,1,0:T(8,128)(2,1)S(1)}, u32[]{:S(2)}, u32[]{:S(2)}) collective-permute-start(s16[2,4,544,128]{3,2,1,0:T(8,128)(2,1)S(1)} %get-tuple-element.116), channel_id=1, source_target_pairs={{0,1},{1,2},{2,3},{3,0},{4,5},{5,6},{6,7},{7,4},{8,9},{9,10},{10,1... | collective-permute-start | bytes 3342344 | tf_op jit(solution)/shard_map/ppermute | solution.py:260
  154.8 26.1 %collective-permute-start.19 = (s16[2,4,544,128]{3,2,1,0:T(8,128)(2,1)S(1)}, s16[2,4,544,128]{3,2,1,0:T(8,128)(2,1)S(1)}, u32[]{:S(2)}, u32[]{:S(2)}) collective-permute-start(s16[2,4,544,128]{3,2,1,0:T(8,128)(2,1)S(1)} %get-tuple-element.117), channel_id=1, source_target_pairs={{0,3},{1,0},{2,1},{3,2},{4,7},{5,4},{6,5},{7,6},{8,11},{9,8},{10,9... | collective-permute-start | bytes 3342344 | tf_op jit(solution)/shard_map/ppermute | solution.py:264
  184.4 6.3 %collective-permute-start.20 = (s16[1,544,128]{2,1,0:T(8,128)(2,1)S(1)}, s16[1,544,128]{2,1,0:T(8,128)(2,1)S(1)}, u32[]{:S(2)}, u32[]{:S(2)}) collective-permute-start(s16[1,544,128]{2,1,0:T(8,128)(2,1)S(1)} %get-tuple-element.121), channel_id=1, source_target_pairs={{0,1},{1,2},{2,3},{3,0},{4,5},{5,6},{6,7},{7,4},{8,9},{9,10},{10,1... | collective-permute-start | bytes 417800 | tf_op jit(solution)/shard_map/ppermute | solution.py:260
  197.7 7.8 %collective-permute-start.24 = (s16[2,544,128]{2,1,0:T(8,128)(2,1)S(1)}, s16[2,544,128]{2,1,0:T(8,128)(2,1)S(1)}, u32[]{:S(2)}, u32[]{:S(2)}) collective-permute-start(s16[2,544,128]{2,1,0:T(8,128)(2,1)S(1)} %get-tuple-element.127), channel_id=1, source_target_pairs={{0,1},{1,2},{2,3},{3,0},{4,5},{5,6},{6,7},{7,4},{8,9},{9,10},{10,1... | collective-permute-start | bytes 835592 | tf_op jit(solution)/shard_map/ppermute | solution.py:260
  197.7 7.7 %collective-permute-start.25 = (s16[2,544,128]{2,1,0:T(8,128)(2,1)S(1)}, s16[2,544,128]{2,1,0:T(8,128)(2,1)S(1)}, u32[]{:S(2)}, u32[]{:S(2)}) collective-permute-start(s16[2,544,128]{2,1,0:T(8,128)(2,1)S(1)} %get-tuple-element.128), channel_id=1, source_target_pairs={{0,3},{1,0},{2,1},{3,2},{4,7},{5,4},{6,5},{7,6},{8,11},{9,8},{10,9... | collective-permute-start | bytes 835592 | tf_op jit(solution)/shard_map/ppermute | solution.py:264
  201.0 6.5 %collective-permute-start.26 = (s16[2,544,128]{2,1,0:T(8,128)(2,1)S(1)}, s16[2,544,128]{2,1,0:T(8,128)(2,1)S(1)}, u32[]{:S(2)}, u32[]{:S(2)}) collective-permute-start(s16[2,544,128]{2,1,0:T(8,128)(2,1)S(1)} %get-tuple-element.129), channel_id=1, source_target_pairs={{0,4},{4,8},{8,12},{12,0},{1,5},{5,9},{9,13},{13,1},{2,6},{6,10},{... | collective-permute-start | bytes 835592 | tf_op jit(solution)/shard_map/ppermute | solution.py:260
  201.0 7.8 %collective-permute-start.27 = (s16[2,544,128]{2,1,0:T(8,128)(2,1)S(1)}, s16[2,544,128]{2,1,0:T(8,128)(2,1)S(1)}, u32[]{:S(2)}, u32[]{:S(2)}) collective-permute-start(s16[2,544,128]{2,1,0:T(8,128)(2,1)S(1)} %get-tuple-element.130), channel_id=1, source_target_pairs={{0,12},{4,0},{8,4},{12,8},{1,13},{5,1},{9,5},{13,9},{2,14},{6,2},{... | collective-permute-start | bytes 835592 | tf_op jit(solution)/shard_map/ppermute | solution.py:264
  (18 other events, 141.1 us)

commit v3 on v2

--- a/solution.py
+++ b/solution.py
@@ -20,10 +20,12 @@
 KB = GROUP // (VTILES * JOCC)
 NB = VTILES * JOCC
 SUB = TILE * TILE // 128
-BATCH = CAP // 2
-EXTRA = 48
-CORE = 4 * COLS * BATCH + 4 * EXTRA
-THIRD = ROWS * (COLS * BATCH - EXTRA)
+BATCH = 8
+FIRST = COLS * BATCH
+SECOND = COLS * (CAP - BATCH)
+EXTRA = 80
+CORE = 4 * FIRST + 4 * EXTRA
+THIRD = ROWS * (SECOND - EXTRA)
 POOL = 2 * CORE + THIRD
 PARTS = 12
 HALF = 512
@@ -59,57 +61,73 @@
     out_ref[...] = out.astype(jnp.int32)
 
 
-def fill_kernel(index_ref, tiles_ref, first_ref, second_ref, filled, sems):
+def fill_kernel(index_ref, tiles_ref, first_ref, second_ref, first_filled, second_filled, sems):
     copies = []
-    for k, out_ref in enumerate((first_ref, second_ref)):
-
-        def group(g, carry, k=k):
-            codes = [index_ref[g, k * BATCH + j] for j in range(BATCH)]
+    for k, (filled, out_ref, base) in enumerate(((first_filled, first_ref, 0), (second_filled, second_ref, BATCH))):
+        size = filled.shape[0] // COLS
+
+        def group(g, carry, filled=filled, size=size, base=base):
+            codes = [index_ref[g, base + j] for j in range(size)]
             tiles = [tiles_ref[code // 2] for code in codes]
-            for j in range(BATCH):
+            for j in range(size):
                 turned = jnp.concatenate([tiles[j][:, TILE:], tiles[j][:, :TILE]], axis=1)
-                filled[k, g * BATCH + j] = jnp.where(codes[j] % 2 == 1, turned, tiles[j])
+                filled[g * size + j] = jnp.where(codes[j] % 2 == 1, turned, tiles[j])
             return carry
 
         lax.fori_loop(0, COLS, group, 0)
-        copies.append(pltpu.make_async_copy(filled.at[k], out_ref, sems.at[k]))
+        copies.append(pltpu.make_async_copy(filled, out_ref, sems.at[k]))
         copies[k].start()
     for copy in copies:
         copy.wait()
 
 
-def mix_kernel(index_ref, second_ref, up_ref, down_ref, up_out, down_out, some_out, rest_out, sems):
-    half = COLS * BATCH // 2
+def compact_kernel(index_ref, spill_ref, second_ref, some_ref, rest_ref):
+    def move(out_ref, base):
+        def body(i, carry):
+            tiles = [second_ref[index_ref[base + i * 16 + k]] for k in range(16)]
+            for k in range(16):
+                out_ref[i * 16 + k] = tiles[k]
+            return carry
+
+        lax.fori_loop(0, out_ref.shape[0] // 16, body, 0)
+
+    move(some_ref, 0)
+
+    @pl.when(spill_ref[0] > 0)
+    def _():
+        move(rest_ref, EXTRA)
+
+
+def join_kernel(up_ref, down_ref, some_ref, up_out, down_out, sems):
+    half = FIRST // 2
     copies = [
         pltpu.make_async_copy(up_ref.at[pl.ds(0, half)], up_out.at[pl.ds(0, half)], sems.at[0]),
         pltpu.make_async_copy(down_ref.at[pl.ds(half, half)], down_out.at[pl.ds(0, half)], sems.at[1]),
+        pltpu.make_async_copy(some_ref, up_out.at[pl.ds(half, EXTRA)], sems.at[2]),
+        pltpu.make_async_copy(some_ref, down_out.at[pl.ds(half, EXTRA)], sems.at[3]),
     ]
     for copy in copies:
         copy.start()
-
-    def body(i, carry):
-        tiles = [second_ref[index_ref[i * 16 + k]] for k in range(16)]
-        for k in range(16):
-            some_out[i * 16 + k] = tiles[k]
-        return carry
-
-    lax.fori_loop(0, EXTRA // 16, body, 0)
-    copies += [
-        pltpu.make_async_copy(some_out, up_out.at[pl.ds(half, EXTRA)], sems.at[2]),
-        pltpu.make_async_copy(some_out, down_out.at[pl.ds(half, EXTRA)], sems.at[3]),
-    ]
-    for copy in copies[2:]:
-        copy.start()
-
-    def body_rest(i, carry):
-        tiles = [second_ref[index_ref[EXTRA + i * 16 + k]] for k in range(16)]
-        for k in range(16):
-            rest_out[i * 16 + k] = tiles[k]
-        return carry
-
-    lax.fori_loop(0, (COLS * BATCH - EXTRA) // 16, body_rest, 0)
     for copy in copies:
         copy.wait()
+
+
+def no_spill_kernel(tiles_ref, out_ref, sem):
+    copy = pltpu.make_async_copy(tiles_ref.at[pl.ds(0, 1)], out_ref.at[pl.ds(0, 1)], sem)
+    copy.start()
+    copy.wait()
+
+
+def no_spill_call(tiles):
+    return pl.pallas_call(
+        no_spill_kernel,
+        in_specs=[pl.BlockSpec(memory_space=pl.ANY)],
+        out_specs=pl.BlockSpec(memory_space=pl.ANY),
+        out_shape=jax.ShapeDtypeStruct((THIRD, SUB, 128), jnp.bfloat16),
+        scratch_shapes=[pltpu.SemaphoreType.DMA],
+        compiler_params=pltpu.CompilerParams(vmem_limit_bytes=VMEM_GRANT),
+        name="no_spill",
+    )(tiles)
 
 
 def prep_kernel(mask_ref, amp_ref, even_ref, odd_ref):
@@ -360,28 +378,28 @@
         name="route",
     )(myself.reshape(1).astype(jnp.int32), eri_slot.reshape(-1, 128))
     vmem = pl.BlockSpec(memory_space=pltpu.VMEM)
-    batch = jax.ShapeDtypeStruct((COLS * BATCH, SUB, 128), jnp.bfloat16)
     outgoing = pl.pallas_call(
         fill_kernel,
         grid_spec=pltpu.PrefetchScalarGridSpec(
             num_scalar_prefetch=1,
             grid=(),
             in_specs=[vmem],
-            out_specs=[pl.BlockSpec(memory_space=pl.ANY)] * 2,
+            out_specs=[pl.BlockSpec(memory_space=pltpu.HBM)] * 2,
             scratch_shapes=[
-                pltpu.VMEM((2, COLS * BATCH, SUB, 128), jnp.bfloat16),
+                pltpu.VMEM((FIRST, SUB, 128), jnp.bfloat16),
+                pltpu.VMEM((SECOND, SUB, 128), jnp.bfloat16),
                 pltpu.SemaphoreType.DMA((2,)),
             ],
         ),
-        out_shape=[batch] * 2,
+        out_shape=[jax.ShapeDtypeStruct((size, SUB, 128), jnp.bfloat16) for size in (FIRST, SECOND)],
         compiler_params=pltpu.CompilerParams(vmem_limit_bytes=VMEM_GRANT),
         name="fill",
     )(send_index, eri_tiles.reshape(slots_dev, SUB, 128))
 
     def send(part):
-        part = part.reshape(COLS, BATCH, SUB, 128)
+        part = part.reshape(COLS, -1, SUB, 128)
         part = lax.all_to_all(part, ("x", "z"), split_axis=0, concat_axis=0, tiled=True)
-        return part.reshape(COLS * BATCH, SUB, 128)
+        return part.reshape(-1, SUB, 128)
 
     first = send(outgoing[0])
     first, second, eri_slot = lax.optimization_barrier((first, outgoing[1], eri_slot))
@@ -397,33 +415,35 @@
     start = upto - tail
     mine_upto = lax.dynamic_index_in_dim(upto, y * 2 + core, 0, keepdims=False)
     mine_start = lax.dynamic_index_in_dim(start, y * 2 + core, 0, keepdims=False)
-    spot = jnp.arange(COLS * BATCH, dtype=jnp.int32)
+    spot = jnp.arange(SECOND, dtype=jnp.int32)
     inside = jnp.logical_and(spot[:, None] >= mine_start[None, :], spot[:, None] < mine_upto[None, :])
-    source = jnp.arange(COLS, dtype=jnp.int32)[None, :] * BATCH + spot[:, None] - mine_start[None, :]
+    source = jnp.arange(COLS, dtype=jnp.int32)[None, :] * (CAP - BATCH) + spot[:, None] - mine_start[None, :]
     source = jnp.sum(jnp.where(inside, source, 0), axis=1).astype(jnp.int32)
-    second, up, down, source, spill = lax.optimization_barrier((second, up, down, source, spill))
-    half = COLS * BATCH // 2
-    mixed = jax.ShapeDtypeStruct((half + EXTRA, SUB, 128), jnp.bfloat16)
-    from_up, from_down, some, rest = pl.pallas_call(
-        mix_kernel,
+    spill = spill.astype(jnp.int32).reshape(1)
+    second, source, spill = lax.optimization_barrier((second, source, spill))
+    half = FIRST // 2
+    some, rest = pl.pallas_call(
+        compact_kernel,
         grid_spec=pltpu.PrefetchScalarGridSpec(
-            num_scalar_prefetch=1,
-            grid=(),
-            in_specs=[vmem] * 3,
-            out_specs=[vmem] * 4,
-            scratch_shapes=[pltpu.SemaphoreType.DMA((4,))],
+            num_scalar_prefetch=2, grid=(), in_specs=[vmem], out_specs=[vmem] * 2
         ),
-        out_shape=[mixed] * 2
-        + [
-            jax.ShapeDtypeStruct((EXTRA, SUB, 128), jnp.bfloat16),
-            jax.ShapeDtypeStruct((COLS * BATCH - EXTRA, SUB, 128), jnp.bfloat16),
-        ],
-        compiler_params=pltpu.CompilerParams(vmem_limit_bytes=VMEM_GRANT),
-        name="mix",
-    )(source, second, up, down)
+        out_shape=[jax.ShapeDtypeStruct((size, SUB, 128), jnp.bfloat16) for size in (EXTRA, SECOND - EXTRA)],
+        compiler_params=pltpu.CompilerParams(vmem_limit_bytes=VMEM_GRANT),
+        name="compact",
+    )(source, spill, second)
+    some, up, down = lax.optimization_barrier((some, up, down))
+    from_up, from_down = pl.pallas_call(
+        join_kernel,
+        in_specs=[vmem] * 3,
+        out_specs=[vmem] * 2,
+        out_shape=[jax.ShapeDtypeStruct((half + EXTRA, SUB, 128), jnp.bfloat16)] * 2,
+        scratch_shapes=[pltpu.SemaphoreType.DMA((4,))],
+        compiler_params=pltpu.CompilerParams(vmem_limit_bytes=VMEM_GRANT),
+        name="join",
+    )(up, down, some)
+    wanted = lax.dynamic_slice_in_dim(eri_slot, group * GROUP, GROUP)
+    from_up, up, down, amplitudes, wanted = lax.optimization_barrier((from_up, up, down, amplitudes, wanted))
     from_up, from_down = ahead("y", from_up), behind("y", from_down)
-    wanted = lax.dynamic_slice_in_dim(eri_slot, group * GROUP, GROUP)
-    some, up, down, amplitudes, wanted = lax.optimization_barrier((some, up, down, amplitudes, wanted))
     swapped = swap([first, up, down])
 
     parted = jax.ShapeDtypeStruct((rows_dev, depth_dev // 2), jnp.bfloat16)
@@ -451,34 +471,32 @@
     owner_row = owner // COLS
     turn = (owner_row // 2 - y) % 4
     turn = jnp.where(turn == 1, 2, jnp.where(turn == 2, 3, jnp.where(turn == 3, 1, 0)))
-    size = COLS * BATCH
+    size = FIRST
     slot = owner % COLS * BATCH + rank
     early = turn * size + slot + jnp.where(jnp.logical_and(turn == 3, slot >= half), EXTRA, 0)
     begins = (4 * size + 2 * EXTRA, 3 * size + half, 4 * size + EXTRA, 4 * size + 3 * EXTRA)
     late = behind_first + sum(jnp.where(turn == k, begin_late, 0) for k, begin_late in enumerate(begins))
     tile_index = jnp.where(rank < BATCH, early, late) + CORE * (owner_row % 2 != core)
-    spilled = 2 * CORE + owner_row * (size - EXTRA) + behind_first - EXTRA
+    spilled = 2 * CORE + owner_row * (SECOND - EXTRA) + behind_first - EXTRA
     tile_index = jnp.where(jnp.logical_or(rank < BATCH, behind_first < EXTRA), tile_index, spilled)
     tile_index = jnp.where(wanted < 0, POOL, tile_index)
-    misc = jnp.stack([x, z, spill.astype(jnp.int32)]).astype(jnp.int32)
+    misc = jnp.stack([x, z, spill[0]]).astype(jnp.int32)
     third = lax.cond(
         misc[2] > 0,
         lambda value: lax.all_gather(value, ("y", "core"), axis=0, tiled=True),
-        lambda value: jnp.zeros((THIRD, SUB, 128), jnp.bfloat16),
+        no_spill_call,
         rest,
     )
-    from_up, from_down, even, odd, tile_index, misc, third = lax.optimization_barrier(
-        (from_up, from_down, even, odd, tile_index, misc, third)
+    from_up, from_down, swapped, even, odd, tile_index, misc, third = lax.optimization_barrier(
+        (from_up, from_down, swapped, even, odd, tile_index, misc, third)
     )
-    tail = jnp.concatenate(
-        [
-            some,
-            ahead("y", from_up[half : half + EXTRA // 2]),
-            behind("y", from_down[half + EXTRA // 2 :]),
-        ]
-    )
-    late_parts = [from_up, from_down, tail]
-    tiles = collect_call(misc, [first, up, down, *late_parts, *swapped, *swap(late_parts)], third)
+    tail_up = ahead("y", from_up[half : half + EXTRA // 2])
+    tail_down = behind("y", from_down[half + EXTRA // 2 :])
+    swapped_late = swap([from_up, from_down])
+    tail_up, tail_down, swapped_late = lax.optimization_barrier((tail_up, tail_down, swapped_late))
+    tail = jnp.concatenate([some, tail_up, tail_down])
+    parts = [first, up, down, from_up, from_down, tail, *swapped, *swapped_late, *swap([tail])]
+    tiles = collect_call(misc, parts, third)
 
     scalars = (tile_index, misc)
     far, arrays = product_call("far", (2,), scalars, (even, odd, tiles))

time: 217 us -> 218 us (level)
  local copies, waits for them, and re-layouts: 15 us -> 10.6 us
  Pallas kernels: 54.1 us -> 56.9 us
  waiting for transfers between devices: 79.6 us -> 82.3 us
    another operation x1 -> x0, local copies, waits for them, and re-layouts: 3.86 us -> none
    pallas_call x1 -> x3, Pallas kernels: 4.92 us -> 6.69 us  [the longest x1 3.75 us: shards(): pl.pallas_call(join_kernel, in_specs=[vmem] * 3, out_specs=[vmem] * 2, ou...]
    unnamed x27 -> x23, local copies, waits for them, and re-layouts: 8.92 us -> 8.2 us
  transfers between devices with their start and end apart: 30 -> 30, of which waited for: 16 -> 14; matrix products, arithmetic and copies ran while one was open for 6% -> 4% of each run, Pallas kernels for 11% -> 13%
where the time goes in v3:
time: 218 us; the launch traced here: 217 us
  waiting for transfers between devices  82.3 us (38%)
  Pallas kernels  56.9 us (26%)
  starting transfers between devices  47.1 us (22%)
  between operations  14.5 us (7%)
  local copies, waits for them, and re-layouts  10.6 us (5%)
  other arithmetic  3.79 us (2%)
    ppermute x11, waiting for transfers between devices, ahead(): return lax.ppermute(value, axis, [(i, (i + 1) % 4) for i in range(4)])  34.4 us
    all_to_all x2, waiting for transfers between devices, send(): lax.all_to_all(part, ('x', 'z'), split_axis=0, concat_axis=0, tiled=True)  29.9 us
    pallas_call x3, Pallas kernels, product_call(): pl.pallas_call(functools.partial(product_kernel, hops), grid_spec=pltpu.P...  26.3 us
    ppermute x11, starting transfers between devices, behind(): return lax.ppermute(value, axis, [(i, (i + 3) % 4) for i in range(4)])  25.2 us
    ppermute x11, waiting for transfers between devices, behind(): return lax.ppermute(value, axis, [(i, (i + 3) % 4) for i in range(4)])  14.9 us
    all_to_all x2, starting transfers between devices, send(): lax.all_to_all(part, ('x', 'z'), split_axis=0, concat_axis=0, tiled=True)  14.4 us
    pallas_call x4, Pallas kernels, whole_call(): pl.pallas_call(body, in_specs=[pl.BlockSpec(memory_space=pltpu.SMEM)] * l...  8.73 us
    unnamed x23, local copies, waits for them, and re-layouts  8.2 us
  transfers between devices with their start and end apart: 30, of which 14 were waited for; matrix products, arithmetic and copies ran while one was open for 4% of the time, Pallas kernels for 13%

profile of v3, /device:TPU:6, one launch (start us, length us, event | category | flops | bytes accessed | tf_op | source)
XLA Modules:
  0.0 217.1 jit_solution(11867363290390569644)
XLA Ops:
  9.8 4.6 %fill.1 = (bf16[128,32,128]{2,1,0:T(8,128)(2,1)S(1)}, bf16[192,32,128]{2,1,0:T(8,128)(2,1)S(1)}) custom-call(s32[16,128]{1,0:T(8,128)S(1)} %route.1.index_ref, bf16[320,32,128]{2,1,0:T(8,128)(2,1)S(1)} %bitcast.19), custom_call_target="tpu_custom_call" | custom-call | tf_op jit(solution)/shard_map/fill/pallas_call | solution.py:381
  16.6 8.3 %all-to-all-start = ((bf16[16,8,32,128]{3,2,1,0:T(8,128)(2,1)}), bf16[16,8,32,128]{3,2,1,0:T(8,128)(2,1)S(1)}, u32[]{:S(2)}, u32[]{:S(2)}) async-start(bf16[16,8,32,128]{3,2,1,0:T(8,128)(2,1)} %bitcast.26), calls=%async_computation | async-start | bytes 2097152 | tf_op jit(solution)/shard_map/all_to_all | solution.py:401
  24.9 15.2 %all-to-all-done = bf16[16,8,32,128]{3,2,1,0:T(8,128)(2,1)S(1)} async-done(((bf16[16,8,32,128]{3,2,1,0:T(8,128)(2,1)}), bf16[16,8,32,128]{3,2,1,0:T(8,128)(2,1)S(1)}, u32[]{:S(2)}, u32[]{:S(2)}) %all-to-all-start) | async-done | bytes 1048608 | tf_op jit(solution)/shard_map/all_to_all | solution.py:401
  43.1 6.1 %all-to-all-start.1 = ((bf16[16,12,32,128]{3,2,1,0:T(8,128)(2,1)}), bf16[16,12,32,128]{3,2,1,0:T(8,128)(2,1)S(1)}, u32[]{:S(2)}, u32[]{:S(2)}) async-start(bf16[16,12,32,128]{3,2,1,0:T(8,128)(2,1)} %bitcast.25), calls=%async_computation.1 | async-start | bytes 3145728 | tf_op jit(solution)/shard_map/all_to_all | solution.py:401
  53.5 14.7 %all-to-all-done.1 = bf16[16,12,32,128]{3,2,1,0:T(8,128)(2,1)S(1)} async-done(((bf16[16,12,32,128]{3,2,1,0:T(8,128)(2,1)}), bf16[16,12,32,128]{3,2,1,0:T(8,128)(2,1)S(1)}, u32[]{:S(2)}, u32[]{:S(2)}) %all-to-all-start.1) | async-done | bytes 1572896 | tf_op jit(solution)/shard_map/all_to_all | solution.py:401
  69.9 3.7 %join.1 = (bf16[144,32,128]{2,1,0:T(8,128)(2,1)}, bf16[144,32,128]{2,1,0:T(8,128)(2,1)}) custom-call(bf16[128,32,128]{2,1,0:T(8,128)(2,1)} %collective-permute-done.up_ref.refs_1_, bf16[128,32,128]{2,1,0:T(8,128)(2,1)} %collective-permute-done.1.down_ref.refs_2_, bf16[80,32,128]{2,1,0:T(8,128)(2,1)S(1)} %get-tuple-element.90.some_ref), custom_call_target="tpu_custom_call" | custom-call | tf_op jit(solution)/shard_map/join/pallas_call | solution.py:435
  79.8 5.7 %prep.1 = (bf16[1024,1024]{1,0:T(8,128)(2,1)S(1)}, bf16[1024,1024]{1,0:T(8,128)(2,1)S(1)}) custom-call(s32[16,32]{1,0:T(8,128)S(1)} %copy-done.8, bf16[1024,2048]{1,0:T(8,128)(2,1)S(1)} %copy-done.2), custom_call_target="tpu_custom_call" | custom-call | tf_op jit(solution)/shard_map/prep/pallas_call | solution.py:450
  90.8 9.7 %collective-permute-done.2.refs_3_ = bf16[144,32,128]{2,1,0:T(8,128)(2,1)} collective-permute-done((bf16[144,32,128]{2,1,0:T(8,128)(2,1)}, bf16[144,32,128]{2,1,0:T(8,128)(2,1)}, u32[]{:S(2)}, u32[]{:S(2)}) %collective-permute-start.2) | collective-permute-done | bytes 1179680 | tf_op jit(solution)/shard_map/ppermute | solution.py:278
  103.0 3.0 %collective-permute-start.8 = (bf16[40,32,128]{2,1,0:T(8,128)(2,1)S(1)}, bf16[40,32,128]{2,1,0:T(8,128)(2,1)S(1)}, u32[]{:S(2)}, u32[]{:S(2)}) collective-permute-start(bf16[40,32,128]{2,1,0:T(8,128)(2,1)S(1)} %slice.7), channel_id=1, source_target_pairs={{0,96},{32,0},{64,32},{96,64},{1,97},{33,1},{65,33},{97,65},{2,98}... | collective-permute-start | bytes 983048 | tf_op jit(solution)/shard_map/ppermute | solution.py:282
  106.1 7.1 %collective-permute-done.8 = bf16[40,32,128]{2,1,0:T(8,128)(2,1)S(1)} collective-permute-done((bf16[40,32,128]{2,1,0:T(8,128)(2,1)S(1)}, bf16[40,32,128]{2,1,0:T(8,128)(2,1)S(1)}, u32[]{:S(2)}, u32[]{:S(2)}) %collective-permute-start.8) | collective-permute-done | bytes 327712 | tf_op jit(solution)/shard_map/ppermute | solution.py:282
  113.2 3.4 %collective-permute-done.7 = bf16[40,32,128]{2,1,0:T(8,128)(2,1)S(1)} collective-permute-done((bf16[40,32,128]{2,1,0:T(8,128)(2,1)S(1)}, bf16[40,32,128]{2,1,0:T(8,128)(2,1)S(1)}, u32[]{:S(2)}, u32[]{:S(2)}) %collective-permute-start.7) | collective-permute-done | bytes 327712 | tf_op jit(solution)/shard_map/ppermute | solution.py:278
  116.8 3.0 %collective-permute-done.11.refs_11_ = bf16[160,32,128]{2,1,0:T(8,128)(2,1)S(1)} collective-permute-done((bf16[160,32,128]{2,1,0:T(8,128)(2,1)S(1)}, bf16[160,32,128]{2,1,0:T(8,128)(2,1)S(1)}, u32[]{:S(2)}, u32[]{:S(2)}) %collective-permute-start.11) | collective-permute-done | bytes 1310752 | tf_op jit(solution)/shard_map/ppermute | solution.py:290
  119.8 4.0 %collect.1.tiles = bf16[2561,32,128]{2,1,0:T(8,128)(2,1)S(1)} custom-call(s32[3]{0:T(128)S(1)} %pad_add_fusion.misc_ref, bf16[128,32,128]{2,1,0:T(8,128)(2,1)S(1)} %bitcast.24, bf16[128,32,128]{2,1,0:T(8,128)(2,1)} %collective-permute-done.up_ref.refs_1_, bf16[128,32,128]{2,1,0:T(8,128)(2,1)} %collective-permute-done.1.down_ref.refs_2_, ...), custom_call_target="tpu_custom_call" | custom-call | bytes 20971520 | tf_op jit(solution)/shard_map/collect/pallas_call | solution.py:192
  123.8 7.1 %far.1 = (s16[4,544,128]{2,1,0:T(8,128)(2,1)S(1)}, s16[4,544,128]{2,1,0:T(8,128)(2,1)S(1)}, s16[4,544,128]{2,1,0:T(8,128)(2,1)S(1)}, s16[4,544,128]{2,1,0:T(8,12...) custom-call(s32[2048]{0:T(1024)S(1)} %select_select_fusion.index_ref, ...), custom_call_target="tpu_custom_call", output_to_operand_aliasing={{4}: (2, {}), {5}: (3, {}), {6}: (4, {})} | custom-call | flops 4294967296 | bytes 20971520 | tf_op jit(solution)/shard_map/far/pallas_call | solution.py:257
  132.9 3.2 %collective-permute-start.15 = (s16[4,544,128]{2,1,0:T(8,128)(2,1)S(1)}, s16[4,544,128]{2,1,0:T(8,128)(2,1)S(1)}, u32[]{:S(2)}, u32[]{:S(2)}) collective-permute-start(s16[4,544,128]{2,1,0:T(8,128)(2,1)S(1)} %get-tuple-element.130), channel_id=1, source_target_pairs={{0,3},{1,0},{2,1},{3,2},{4,7},{5,4},{6,5},{7,6},{8,11},{9,8},{10,9... | collective-permute-start | bytes 1671176 | tf_op jit(solution)/shard_map/ppermute | solution.py:282
  136.2 13.2 %near.1 = (s16[2,4,544,128]{3,2,1,0:T(8,128)(2,1)S(1)}, s16[2,4,544,128]{3,2,1,0:T(8,128)(2,1)S(1)}, s16[2,4,544,128]{3,2,1,0:T(8,128)(2,1)S(1)}, s16[2,4,544,12...) custom-call(s32[2048]{0:T(1024)S(1)} %select_select_fusion.index_ref, ...), custom_call_target="tpu_custom_call", output_to_operand_aliasing={{4}: (2, {}), {5}: (3, {}), {6}: (4, {})} | custom-call | flops 8589934592 | bytes 20971520 | tf_op jit(solution)/shard_map/near/pallas_call | solution.py:257
  149.4 3.1 %add_first.1 = (s16[2,4,544,128]{3,2,1,0:T(8,128)(2,1)S(1)}, s16[2,4,544,128]{3,2,1,0:T(8,128)(2,1)S(1)}, s16[2,4,544,128]{3,2,1,0:T(8,128)(2,1)S(1)}, s16[2,4,544,128]{3,2,1,0:T(8,128)(2,1)S(1)}) custom-call(s16[2,4,544,128]{3,2,1,0:T(8,128)(2,1)S(1)} %get-tuple-element.123.refs_0_, s16[2,4,544,128]{3,2,1,0:T(8,128)(2,1)S(1)} %get-tuple-element.124.refs_1_, ...), custom_call_target="tpu_custom_call" | custom-call | flops 111411200 | bytes 11141120 | tf_op jit(solution)/shard_map/add_first/pallas_call | solution.py:320
  154.6 3.2 %collective-permute-start.19 = (s16[2,4,544,128]{3,2,1,0:T(8,128)(2,1)S(1)}, s16[2,4,544,128]{3,2,1,0:T(8,128)(2,1)S(1)}, u32[]{:S(2)}, u32[]{:S(2)}) collective-permute-start(s16[2,4,544,128]{3,2,1,0:T(8,128)(2,1)S(1)} %get-tuple-element.134), channel_id=1, source_target_pairs={{0,3},{1,0},{2,1},{3,2},{4,7},{5,4},{6,5},{7,6},{8,11},{9,8},{10,9... | collective-permute-start | bytes 3342344 | tf_op jit(solution)/shard_map/ppermute | solution.py:282
  157.8 6.1 %own.1 = (f32[4,1024,128]{2,1,0:T(8,128)S(1)}, f32[4,1024,128]{2,1,0:T(8,128)S(1)}) custom-call(s32[2048]{0:T(1024)S(1)} %select_select_fusion.index_ref, s32[3]{0:T(128)S(1)} %pad_add_fusion.misc_ref, bf16[1024,1024]{1,0:T(8,128)(2,1)S(1)} %get-tuple-element.118.even_ref, bf16[1024,1024]{1,0:T(8,128)(2,1)S(1)} %get-tuple-element.119.odd_ref, ...), custom_call_target="tpu_custom_call" | custom-call | flops 4294967296 | bytes 20971520 | tf_op jit(solution)/shard_map/own/pallas_call | solution.py:257
  163.9 14.1 %collective-permute-done.16.refs_0_ = s16[2,4,544,128]{3,2,1,0:T(8,128)(2,1)S(1)} collective-permute-done((s16[2,4,544,128]{3,2,1,0:T(8,128)(2,1)S(1)}, s16[2,4,544,128]{3,2,1,0:T(8,128)(2,1)S(1)}, u32[]{:S(2)}, u32[]{:S(2)}) %collective-permute-start.16) | collective-permute-done | bytes 1114144 | tf_op jit(solution)/shard_map/ppermute | solution.py:278
  181.0 3.5 %middle.1 = (s16[1,544,128]{2,1,0:T(8,128)(2,1)S(1)}, s16[1,544,128]{2,1,0:T(8,128)(2,1)S(1)}, s16[2,544,128]{2,1,0:T(8,128)(2,1)S(1)}, s16[2,544,128]{2,1,0:T(8...) custom-call(s32[3]{0:T(128)S(1)} %pad_add_fusion.misc_ref, ...), custom_call_target="tpu_custom_call" | custom-call | flops 113704960 | bytes 11370496 | tf_op jit(solution)/shard_map/middle/pallas_call | solution.py:320
  184.6 3.2 %collective-permute-start.21 = (s16[1,544,128]{2,1,0:T(8,128)(2,1)S(1)}, s16[1,544,128]{2,1,0:T(8,128)(2,1)S(1)}, u32[]{:S(2)}, u32[]{:S(2)}) collective-permute-start(s16[1,544,128]{2,1,0:T(8,128)(2,1)S(1)} %get-tuple-element.139), channel_id=1, source_target_pairs={{0,3},{1,0},{2,1},{3,2},{4,7},{5,4},{6,5},{7,6},{8,11},{9,8},{10,9... | collective-permute-start | bytes 417800 | tf_op jit(solution)/shard_map/ppermute | solution.py:282
  193.3 3.7 %collective-permute-done.23.refs_7_ = s16[1,544,128]{2,1,0:T(8,128)(2,1)S(1)} collective-permute-done((s16[1,544,128]{2,1,0:T(8,128)(2,1)S(1)}, s16[1,544,128]{2,1,0:T(8,128)(2,1)S(1)}, u32[]{:S(2)}, u32[]{:S(2)}) %collective-permute-start.23) | collective-permute-done | bytes 139296 | tf_op jit(solution)/shard_map/ppermute | solution.py:282
  197.8 3.2 %collective-permute-start.25 = (s16[2,544,128]{2,1,0:T(8,128)(2,1)S(1)}, s16[2,544,128]{2,1,0:T(8,128)(2,1)S(1)}, u32[]{:S(2)}, u32[]{:S(2)}) collective-permute-start(s16[2,544,128]{2,1,0:T(8,128)(2,1)S(1)} %get-tuple-element.145), channel_id=1, source_target_pairs={{0,3},{1,0},{2,1},{3,2},{4,7},{5,4},{6,5},{7,6},{8,11},{9,8},{10,9... | collective-permute-start | bytes 835592 | tf_op jit(solution)/shard_map/ppermute | solution.py:282
  (102 shorter events, 51.8 us)
Async XLA Ops:
  16.6 23.5 %all-to-all-start = ((bf16[16,8,32,128]{3,2,1,0:T(8,128)(2,1)}), bf16[16,8,32,128]{3,2,1,0:T(8,128)(2,1)S(1)}, u32[]{:S(2)}, u32[]{:S(2)}) async-start(bf16[16,8,32,128]{3,2,1,0:T(8,128)(2,1)} %bitcast.26), calls=%async_computation | async-start | bytes 2097152 | tf_op jit(solution)/shard_map/all_to_all | solution.py:401
  40.1 29.8 %collective-permute-start.1 = (bf16[128,32,128]{2,1,0:T(8,128)(2,1)S(1)}, bf16[128,32,128]{2,1,0:T(8,128)(2,1)}, u32[]{:S(2)}, u32[]{:S(2)}) collective-permute-start(bf16[128,32,128]{2,1,0:T(8,128)(2,1)S(1)} %bitcast.21), channel_id=1, source_target_pairs={{0,96},{32,0},{64,32},{96,64},{1,97},{33,1},{65,33},{97,65},{2,98}... | collective-permute-start | bytes 3145736 | tf_op jit(solution)/shard_map/ppermute | solution.py:282
  43.1 26.8 %collective-permute-start = (bf16[128,32,128]{2,1,0:T(8,128)(2,1)S(1)}, bf16[128,32,128]{2,1,0:T(8,128)(2,1)}, u32[]{:S(2)}, u32[]{:S(2)}) collective-permute-start(bf16[128,32,128]{2,1,0:T(8,128)(2,1)S(1)} %bitcast.22), channel_id=1, source_target_pairs={{0,32},{32,64},{64,96},{96,0},{1,33},{33,65},{65,97},{97,1},{2,34}... | collective-permute-start | bytes 3145736 | tf_op jit(solution)/shard_map/ppermute | solution.py:278
  43.1 25.2 %all-to-all-start.1 = ((bf16[16,12,32,128]{3,2,1,0:T(8,128)(2,1)}), bf16[16,12,32,128]{3,2,1,0:T(8,128)(2,1)S(1)}, u32[]{:S(2)}, u32[]{:S(2)}) async-start(bf16[16,12,32,128]{3,2,1,0:T(8,128)(2,1)} %bitcast.25), calls=%async_computation.1 | async-start | bytes 3145728 | tf_op jit(solution)/shard_map/all_to_all | solution.py:401
  73.6 26.8 %collective-permute-start.2 = (bf16[144,32,128]{2,1,0:T(8,128)(2,1)}, bf16[144,32,128]{2,1,0:T(8,128)(2,1)}, u32[]{:S(2)}, u32[]{:S(2)}) collective-permute-start(bf16[144,32,128]{2,1,0:T(8,128)(2,1)} %get-tuple-element.92), channel_id=1, source_target_pairs={{0,32},{32,64},{64,96},{96,0},{1,33},{33,65},{65,97},{97,1},{2,34}... | collective-permute-start | bytes 3538952 | tf_op jit(solution)/shard_map/ppermute | solution.py:278
  74.0 26.5 %collective-permute-start.3 = (bf16[144,32,128]{2,1,0:T(8,128)(2,1)}, bf16[144,32,128]{2,1,0:T(8,128)(2,1)}, u32[]{:S(2)}, u32[]{:S(2)}) collective-permute-start(bf16[144,32,128]{2,1,0:T(8,128)(2,1)} %get-tuple-element.93), channel_id=1, source_target_pairs={{0,96},{32,0},{64,32},{96,64},{1,97},{33,1},{65,33},{97,65},{2,98}... | collective-permute-start | bytes 3538952 | tf_op jit(solution)/shard_map/ppermute | solution.py:282
  76.9 13.8 %collective-permute-start.4 = (bf16[128,32,128]{2,1,0:T(8,128)(2,1)S(1)}, bf16[128,32,128]{2,1,0:T(8,128)(2,1)}, u32[]{:S(2)}, u32[]{:S(2)}) collective-permute-start(bf16[128,32,128]{2,1,0:T(8,128)(2,1)S(1)} %bitcast.23), channel_id=1, source_target_pairs={{0,16},{16,0},{1,17},{17,1},{2,18},{18,2},{3,19},{19,3},{4,20},{20... | collective-permute-start | bytes 3145736 | tf_op jit(solution)/shard_map/ppermute | solution.py:290
  76.9 13.8 %collective-permute-start.5 = (bf16[128,32,128]{2,1,0:T(8,128)(2,1)}, bf16[128,32,128]{2,1,0:T(8,128)(2,1)}, u32[]{:S(2)}, u32[]{:S(2)}) collective-permute-start(bf16[128,32,128]{2,1,0:T(8,128)(2,1)} %collective-permute-done.up_ref.refs_1_), channel_id=1, source_target_pairs={{0,16},{16,0},{1,17},{17,1},{2,18},{18,2},{3,19},{19,3},{4,20},{20... | collective-permute-start | bytes 3145736 | tf_op jit(solution)/shard_map/ppermute | solution.py:290
  77.5 13.3 %collective-permute-start.6 = (bf16[128,32,128]{2,1,0:T(8,128)(2,1)}, bf16[128,32,128]{2,1,0:T(8,128)(2,1)}, u32[]{:S(2)}, u32[]{:S(2)}) collective-permute-start(bf16[128,32,128]{2,1,0:T(8,128)(2,1)} %collective-permute-done.1.down_ref.refs_2_), channel_id=1, source_target_pairs={{0,16},{16,0},{1,17},{17,1},{2,18},{18,2},{3,19},{19,3},{4,20},{20... | collective-permute-start | bytes 3145736 | tf_op jit(solution)/shard_map/ppermute | solution.py:290
  100.5 16.1 %collective-permute-start.9 = (bf16[144,32,128]{2,1,0:T(8,128)(2,1)}, bf16[144,32,128]{2,1,0:T(8,128)(2,1)S(1)}, u32[]{:S(2)}, u32[]{:S(2)}) collective-permute-start(bf16[144,32,128]{2,1,0:T(8,128)(2,1)} %collective-permute-done.2.refs_3_), channel_id=1, source_target_pairs={{0,16},{16,0},{1,17},{17,1},{2,18},{18,2},{3,19},{19,3},{4,20},{20... | collective-permute-start | bytes 3538952 | tf_op jit(solution)/shard_map/ppermute | solution.py:290
  100.5 16.1 %collective-permute-start.10 = (bf16[144,32,128]{2,1,0:T(8,128)(2,1)}, bf16[144,32,128]{2,1,0:T(8,128)(2,1)S(1)}, u32[]{:S(2)}, u32[]{:S(2)}) collective-permute-start(bf16[144,32,128]{2,1,0:T(8,128)(2,1)} %collective-permute-done.3.refs_4_), channel_id=1, source_target_pairs={{0,16},{16,0},{1,17},{17,1},{2,18},{18,2},{3,19},{19,3},{4,20},{20... | collective-permute-start | bytes 3538952 | tf_op jit(solution)/shard_map/ppermute | solution.py:290
  103.0 10.2 %collective-permute-start.8 = (bf16[40,32,128]{2,1,0:T(8,128)(2,1)S(1)}, bf16[40,32,128]{2,1,0:T(8,128)(2,1)S(1)}, u32[]{:S(2)}, u32[]{:S(2)}) collective-permute-start(bf16[40,32,128]{2,1,0:T(8,128)(2,1)S(1)} %slice.7), channel_id=1, source_target_pairs={{0,96},{32,0},{64,32},{96,64},{1,97},{33,1},{65,33},{97,65},{2,98}... | collective-permute-start | bytes 983048 | tf_op jit(solution)/shard_map/ppermute | solution.py:282
  106.0 10.5 %collective-permute-start.7 = (bf16[40,32,128]{2,1,0:T(8,128)(2,1)S(1)}, bf16[40,32,128]{2,1,0:T(8,128)(2,1)S(1)}, u32[]{:S(2)}, u32[]{:S(2)}) collective-permute-start(bf16[40,32,128]{2,1,0:T(8,128)(2,1)S(1)} %slice.6), channel_id=1, source_target_pairs={{0,32},{32,64},{64,96},{96,0},{1,33},{33,65},{65,97},{97,1},{2,34}... | collective-permute-start | bytes 983048 | tf_op jit(solution)/shard_map/ppermute | solution.py:278
  130.8 18.5 %collective-permute-start.12 = (s16[4,544,128]{2,1,0:T(8,128)(2,1)S(1)}, s16[4,544,128]{2,1,0:T(8,128)(2,1)S(1)}, u32[]{:S(2)}, u32[]{:S(2)}) collective-permute-start(s16[4,544,128]{2,1,0:T(8,128)(2,1)S(1)} %get-tuple-element.125), channel_id=1, source_target_pairs={{0,4},{4,8},{8,12},{12,0},{1,5},{5,9},{9,13},{13,1},{2,6},{6,10},{... | collective-permute-start | bytes 1671176 | tf_op jit(solution)/shard_map/ppermute | solution.py:278
  131.7 17.7 %collective-permute-start.13 = (s16[4,544,128]{2,1,0:T(8,128)(2,1)S(1)}, s16[4,544,128]{2,1,0:T(8,128)(2,1)S(1)}, u32[]{:S(2)}, u32[]{:S(2)}) collective-permute-start(s16[4,544,128]{2,1,0:T(8,128)(2,1)S(1)} %get-tuple-element.126), channel_id=1, source_target_pairs={{0,12},{4,0},{8,4},{12,8},{1,13},{5,1},{9,5},{13,9},{2,14},{6,2},{... | collective-permute-start | bytes 1671176 | tf_op jit(solution)/shard_map/ppermute | solution.py:282
  132.9 16.5 %collective-permute-start.14 = (s16[4,544,128]{2,1,0:T(8,128)(2,1)S(1)}, s16[4,544,128]{2,1,0:T(8,128)(2,1)S(1)}, u32[]{:S(2)}, u32[]{:S(2)}) collective-permute-start(s16[4,544,128]{2,1,0:T(8,128)(2,1)S(1)} %get-tuple-element.129), channel_id=1, source_target_pairs={{0,1},{1,2},{2,3},{3,0},{4,5},{5,6},{6,7},{7,4},{8,9},{9,10},{10,1... | collective-permute-start | bytes 1671176 | tf_op jit(solution)/shard_map/ppermute | solution.py:278
  132.9 16.5 %collective-permute-start.15 = (s16[4,544,128]{2,1,0:T(8,128)(2,1)S(1)}, s16[4,544,128]{2,1,0:T(8,128)(2,1)S(1)}, u32[]{:S(2)}, u32[]{:S(2)}) collective-permute-start(s16[4,544,128]{2,1,0:T(8,128)(2,1)S(1)} %get-tuple-element.130), channel_id=1, source_target_pairs={{0,3},{1,0},{2,1},{3,2},{4,7},{5,4},{6,5},{7,6},{8,11},{9,8},{10,9... | collective-permute-start | bytes 1671176 | tf_op jit(solution)/shard_map/ppermute | solution.py:282
  152.5 25.5 %collective-permute-start.16 = (s16[2,4,544,128]{3,2,1,0:T(8,128)(2,1)S(1)}, s16[2,4,544,128]{3,2,1,0:T(8,128)(2,1)S(1)}, u32[]{:S(2)}, u32[]{:S(2)}) collective-permute-start(s16[2,4,544,128]{3,2,1,0:T(8,128)(2,1)S(1)} %get-tuple-element.131), channel_id=1, source_target_pairs={{0,4},{4,8},{8,12},{12,0},{1,5},{5,9},{9,13},{13,1},{2,6},{6,10},{... | collective-permute-start | bytes 3342344 | tf_op jit(solution)/shard_map/ppermute | solution.py:278
  154.6 26.4 %collective-permute-start.17 = (s16[2,4,544,128]{3,2,1,0:T(8,128)(2,1)S(1)}, s16[2,4,544,128]{3,2,1,0:T(8,128)(2,1)S(1)}, u32[]{:S(2)}, u32[]{:S(2)}) collective-permute-start(s16[2,4,544,128]{3,2,1,0:T(8,128)(2,1)S(1)} %get-tuple-element.132), channel_id=1, source_target_pairs={{0,12},{4,0},{8,4},{12,8},{1,13},{5,1},{9,5},{13,9},{2,14},{6,2},{... | collective-permute-start | bytes 3342344 | tf_op jit(solution)/shard_map/ppermute | solution.py:282
  154.6 26.4 %collective-permute-start.18 = (s16[2,4,544,128]{3,2,1,0:T(8,128)(2,1)S(1)}, s16[2,4,544,128]{3,2,1,0:T(8,128)(2,1)S(1)}, u32[]{:S(2)}, u32[]{:S(2)}) collective-permute-start(s16[2,4,544,128]{3,2,1,0:T(8,128)(2,1)S(1)} %get-tuple-element.133), channel_id=1, source_target_pairs={{0,1},{1,2},{2,3},{3,0},{4,5},{5,6},{6,7},{7,4},{8,9},{9,10},{10,1... | collective-permute-start | bytes 3342344 | tf_op jit(solution)/shard_map/ppermute | solution.py:278
  154.6 26.4 %collective-permute-start.19 = (s16[2,4,544,128]{3,2,1,0:T(8,128)(2,1)S(1)}, s16[2,4,544,128]{3,2,1,0:T(8,128)(2,1)S(1)}, u32[]{:S(2)}, u32[]{:S(2)}) collective-permute-start(s16[2,4,544,128]{3,2,1,0:T(8,128)(2,1)S(1)} %get-tuple-element.134), channel_id=1, source_target_pairs={{0,3},{1,0},{2,1},{3,2},{4,7},{5,4},{6,5},{7,6},{8,11},{9,8},{10,9... | collective-permute-start | bytes 3342344 | tf_op jit(solution)/shard_map/ppermute | solution.py:282
  197.8 7.8 %collective-permute-start.24 = (s16[2,544,128]{2,1,0:T(8,128)(2,1)S(1)}, s16[2,544,128]{2,1,0:T(8,128)(2,1)S(1)}, u32[]{:S(2)}, u32[]{:S(2)}) collective-permute-start(s16[2,544,128]{2,1,0:T(8,128)(2,1)S(1)} %get-tuple-element.144), channel_id=1, source_target_pairs={{0,1},{1,2},{2,3},{3,0},{4,5},{5,6},{6,7},{7,4},{8,9},{9,10},{10,1... | collective-permute-start | bytes 835592 | tf_op jit(solution)/shard_map/ppermute | solution.py:278
  197.8 7.7 %collective-permute-start.25 = (s16[2,544,128]{2,1,0:T(8,128)(2,1)S(1)}, s16[2,544,128]{2,1,0:T(8,128)(2,1)S(1)}, u32[]{:S(2)}, u32[]{:S(2)}) collective-permute-start(s16[2,544,128]{2,1,0:T(8,128)(2,1)S(1)} %get-tuple-element.145), channel_id=1, source_target_pairs={{0,3},{1,0},{2,1},{3,2},{4,7},{5,4},{6,5},{7,6},{8,11},{9,8},{10,9... | collective-permute-start | bytes 835592 | tf_op jit(solution)/shard_map/ppermute | solution.py:282
  201.1 7.8 %collective-permute-start.27 = (s16[2,544,128]{2,1,0:T(8,128)(2,1)S(1)}, s16[2,544,128]{2,1,0:T(8,128)(2,1)S(1)}, u32[]{:S(2)}, u32[]{:S(2)}) collective-permute-start(s16[2,544,128]{2,1,0:T(8,128)(2,1)S(1)} %get-tuple-element.147), channel_id=1, source_target_pairs={{0,12},{4,0},{8,4},{12,8},{1,13},{5,1},{9,5},{13,9},{2,14},{6,2},{... | collective-permute-start | bytes 835592 | tf_op jit(solution)/shard_map/ppermute | solution.py:282
  (16 other events, 104.2 us)

commit v4 on v3

--- a/solution.py
+++ b/solution.py
@@ -20,10 +20,10 @@
 KB = GROUP // (VTILES * JOCC)
 NB = VTILES * JOCC
 SUB = TILE * TILE // 128
-BATCH = 8
+BATCH = 11
 FIRST = COLS * BATCH
 SECOND = COLS * (CAP - BATCH)
-EXTRA = 80
+EXTRA = 32
 CORE = 4 * FIRST + 4 * EXTRA
 THIRD = ROWS * (SECOND - EXTRA)
 POOL = 2 * CORE + THIRD
@@ -98,20 +98,6 @@
         move(rest_ref, EXTRA)
 
 
-def join_kernel(up_ref, down_ref, some_ref, up_out, down_out, sems):
-    half = FIRST // 2
-    copies = [
-        pltpu.make_async_copy(up_ref.at[pl.ds(0, half)], up_out.at[pl.ds(0, half)], sems.at[0]),
-        pltpu.make_async_copy(down_ref.at[pl.ds(half, half)], down_out.at[pl.ds(0, half)], sems.at[1]),
-        pltpu.make_async_copy(some_ref, up_out.at[pl.ds(half, EXTRA)], sems.at[2]),
-        pltpu.make_async_copy(some_ref, down_out.at[pl.ds(half, EXTRA)], sems.at[3]),
-    ]
-    for copy in copies:
-        copy.start()
-    for copy in copies:
-        copy.wait()
-
-
 def no_spill_kernel(tiles_ref, out_ref, sem):
     copy = pltpu.make_async_copy(tiles_ref.at[pl.ds(0, 1)], out_ref.at[pl.ds(0, 1)], sem)
     copy.start()
@@ -290,6 +276,11 @@
     return [lax.ppermute(part, "core", [(0, 1), (1, 0)]) for part in parts]
 
 
+def across(up, down):
+    half = up.shape[0] // 2
+    return [ahead("y", up[:half]), behind("y", down[half:])]
+
+
 def add_first_kernel(*refs):
     def body(i, carry):
         for way in range(2):
@@ -421,7 +412,6 @@
     source = jnp.sum(jnp.where(inside, source, 0), axis=1).astype(jnp.int32)
     spill = spill.astype(jnp.int32).reshape(1)
     second, source, spill = lax.optimization_barrier((second, source, spill))
-    half = FIRST // 2
     some, rest = pl.pallas_call(
         compact_kernel,
         grid_spec=pltpu.PrefetchScalarGridSpec(
@@ -431,20 +421,11 @@
         compiler_params=pltpu.CompilerParams(vmem_limit_bytes=VMEM_GRANT),
         name="compact",
     )(source, spill, second)
-    some, up, down = lax.optimization_barrier((some, up, down))
-    from_up, from_down = pl.pallas_call(
-        join_kernel,
-        in_specs=[vmem] * 3,
-        out_specs=[vmem] * 2,
-        out_shape=[jax.ShapeDtypeStruct((half + EXTRA, SUB, 128), jnp.bfloat16)] * 2,
-        scratch_shapes=[pltpu.SemaphoreType.DMA((4,))],
-        compiler_params=pltpu.CompilerParams(vmem_limit_bytes=VMEM_GRANT),
-        name="join",
-    )(up, down, some)
+    some_up, some_down = reach(some)
+    far_parts = across(up, down)
+    some_far = across(some_up, some_down)
     wanted = lax.dynamic_slice_in_dim(eri_slot, group * GROUP, GROUP)
-    from_up, up, down, amplitudes, wanted = lax.optimization_barrier((from_up, up, down, amplitudes, wanted))
-    from_up, from_down = ahead("y", from_up), behind("y", from_down)
-    swapped = swap([first, up, down])
+    some, amplitudes, wanted = lax.optimization_barrier((some, amplitudes, wanted))
 
     parted = jax.ShapeDtypeStruct((rows_dev, depth_dev // 2), jnp.bfloat16)
     even, odd = pl.pallas_call(
@@ -471,11 +452,8 @@
     owner_row = owner // COLS
     turn = (owner_row // 2 - y) % 4
     turn = jnp.where(turn == 1, 2, jnp.where(turn == 2, 3, jnp.where(turn == 3, 1, 0)))
-    size = FIRST
-    slot = owner % COLS * BATCH + rank
-    early = turn * size + slot + jnp.where(jnp.logical_and(turn == 3, slot >= half), EXTRA, 0)
-    begins = (4 * size + 2 * EXTRA, 3 * size + half, 4 * size + EXTRA, 4 * size + 3 * EXTRA)
-    late = behind_first + sum(jnp.where(turn == k, begin_late, 0) for k, begin_late in enumerate(begins))
+    early = (turn * COLS + owner % COLS) * BATCH + rank
+    late = 4 * FIRST + turn * EXTRA + behind_first
     tile_index = jnp.where(rank < BATCH, early, late) + CORE * (owner_row % 2 != core)
     spilled = 2 * CORE + owner_row * (SECOND - EXTRA) + behind_first - EXTRA
     tile_index = jnp.where(jnp.logical_or(rank < BATCH, behind_first < EXTRA), tile_index, spilled)
@@ -487,16 +465,12 @@
         no_spill_call,
         rest,
     )
-    from_up, from_down, swapped, even, odd, tile_index, misc, third = lax.optimization_barrier(
-        (from_up, from_down, swapped, even, odd, tile_index, misc, third)
+    some = jnp.concatenate([some, some_up, some_down, *some_far])
+    first, up, down, far_parts, some, even, odd, tile_index, misc, third = lax.optimization_barrier(
+        (first, up, down, far_parts, some, even, odd, tile_index, misc, third)
     )
-    tail_up = ahead("y", from_up[half : half + EXTRA // 2])
-    tail_down = behind("y", from_down[half + EXTRA // 2 :])
-    swapped_late = swap([from_up, from_down])
-    tail_up, tail_down, swapped_late = lax.optimization_barrier((tail_up, tail_down, swapped_late))
-    tail = jnp.concatenate([some, tail_up, tail_down])
-    parts = [first, up, down, from_up, from_down, tail, *swapped, *swapped_late, *swap([tail])]
-    tiles = collect_call(misc, parts, third)
+    parts = [first, up, down, *far_parts, some]
+    tiles = collect_call(misc, parts + swap(parts), third)
 
     scalars = (tile_index, misc)
     far, arrays = product_call("far", (2,), scalars, (even, odd, tiles))

time: 218 us -> 220 us (level)
  local copies, waits for them, and re-layouts: 10.6 us -> 19.9 us
  waiting for transfers between devices: 82.3 us -> 73.2 us
  Pallas kernels: 56.9 us -> 52.5 us
  starting transfers between devices: 47.1 us -> 51.4 us
    ppermute x11 -> x12, waiting for transfers between devices: 34.4 us -> 23.7 us  [ahead(): return lax.ppermute(value, axis, [(i, (i + 1) % 4) for i in range(4)])]
    ppermute x6, waiting for transfers between devices: 3.03 us -> 9.88 us  [swap(): return [lax.ppermute(part, 'core', [(0, 1), (1, 0)]) for part in parts]]
    ppermute x11 -> x12, waiting for transfers between devices: 14.9 us -> 9.36 us  [behind(): return lax.ppermute(value, axis, [(i, (i + 3) % 4) for i in range(4)])]
    unnamed x23 -> x21, local copies, waits for them, and re-layouts: 8.2 us -> 12.9 us
    slice x2 -> x4, local copies, waits for them, and re-layouts: 1.99 us -> 5.92 us  [across(): return [ahead('y', up[:half]), behind('y', down[half:])]]
    pallas_call x1 -> x0, Pallas kernels: 3.75 us -> none  [shards(): pl.pallas_call(join_kernel, in_specs=[vmem] * 3, out_specs=[vmem] * 2, ou...]
    ppermute x11 -> x12, starting transfers between devices: 25.2 us -> 28.3 us  [behind(): return lax.ppermute(value, axis, [(i, (i + 3) % 4) for i in range(4)])]
    ppermute x11 -> x12, starting transfers between devices: 6.41 us -> 7.5 us  [ahead(): return lax.ppermute(value, axis, [(i, (i + 1) % 4) for i in range(4)])]
  transfers between devices with their start and end apart: 30 -> 32, of which waited for: 14 -> 14; matrix products, arithmetic and copies ran while one was open for 4% -> 9% of each run, Pallas kernels for 13% -> 13%
where the time goes in v4:
time: 220 us; the launch traced here: 219 us
  waiting for transfers between devices  73.2 us (33%)
  Pallas kernels  52.5 us (24%)
  starting transfers between devices  51.4 us (23%)
  local copies, waits for them, and re-layouts  19.9 us (9%)
  between operations  14.4 us (7%)
  other arithmetic  5.09 us (2%)
  matrix products  2.56 us (1%)
    all_to_all x2, waiting for transfers between devices, send(): lax.all_to_all(part, ('x', 'z'), split_axis=0, concat_axis=0, tiled=True)  30.2 us
    ppermute x12, starting transfers between devices, behind(): return lax.ppermute(value, axis, [(i, (i + 3) % 4) for i in range(4)])  28.3 us
    pallas_call x3, Pallas kernels, product_call(): pl.pallas_call(functools.partial(product_kernel, hops), grid_spec=pltpu.P...  26.1 us
    ppermute x12, waiting for transfers between devices, ahead(): return lax.ppermute(value, axis, [(i, (i + 1) % 4) for i in range(4)])  23.7 us
    all_to_all x2, starting transfers between devices, send(): lax.all_to_all(part, ('x', 'z'), split_axis=0, concat_axis=0, tiled=True)  14.3 us
    unnamed x21, local copies, waits for them, and re-layouts  12.9 us
    ppermute x6, waiting for transfers between devices, swap(): return [lax.ppermute(part, 'core', [(0, 1), (1, 0)]) for part in parts]  9.88 us
    ppermute x12, waiting for transfers between devices, behind(): return lax.ppermute(value, axis, [(i, (i + 3) % 4) for i in range(4)])  9.36 us
  transfers between devices with their start and end apart: 32, of which 14 were waited for; matrix products, arithmetic and copies ran while one was open for 9% of the time, Pallas kernels for 13%

profile of v4, /device:TPU:6, one launch (start us, length us, event | category | flops | bytes accessed | tf_op | source)
XLA Modules:
  0.0 218.9 jit_solution(3918160390948263949)
XLA Ops:
  9.8 4.9 %fill.1 = (bf16[176,32,128]{2,1,0:T(8,128)(2,1)S(1)}, bf16[144,32,128]{2,1,0:T(8,128)(2,1)S(1)}) custom-call(s32[16,128]{1,0:T(8,128)S(1)} %route.1.index_ref, bf16[320,32,128]{2,1,0:T(8,128)(2,1)S(1)} %bitcast.19), custom_call_target="tpu_custom_call" | custom-call | tf_op jit(solution)/shard_map/fill/pallas_call | solution.py:372
  16.9 8.3 %all-to-all-start = ((bf16[16,11,32,128]{3,2,1,0:T(8,128)(2,1)}), bf16[16,11,32,128]{3,2,1,0:T(8,128)(2,1)S(1)}, u32[]{:S(2)}, u32[]{:S(2)}) async-start(bf16[16,11,32,128]{3,2,1,0:T(8,128)(2,1)} %bitcast.25), calls=%async_computation | async-start | bytes 2883584 | tf_op jit(solution)/shard_map/all_to_all | solution.py:392
  25.2 19.9 %all-to-all-done = bf16[16,11,32,128]{3,2,1,0:T(8,128)(2,1)S(1)} async-done(((bf16[16,11,32,128]{3,2,1,0:T(8,128)(2,1)}), bf16[16,11,32,128]{3,2,1,0:T(8,128)(2,1)S(1)}, u32[]{:S(2)}, u32[]{:S(2)}) %all-to-all-start) | async-done | bytes 1441824 | tf_op jit(solution)/shard_map/all_to_all | solution.py:392
  45.1 3.0 %collective-permute-start.1 = (bf16[176,32,128]{2,1,0:T(8,128)(2,1)S(1)}, bf16[176,32,128]{2,1,0:T(8,128)(2,1)}, u32[]{:S(2)}, u32[]{:S(2)}) collective-permute-start(bf16[176,32,128]{2,1,0:T(8,128)(2,1)S(1)} %bitcast.20), channel_id=1, source_target_pairs={{0,96},{32,0},{64,32},{96,64},{1,97},{33,1},{65,33},{97,65},{2,98}... | collective-permute-start | bytes 4325384 | tf_op jit(solution)/shard_map/ppermute | solution.py:268
  48.2 6.0 %all-to-all-start.1 = ((bf16[16,9,32,128]{3,2,1,0:T(8,128)(2,1)}), bf16[16,9,32,128]{3,2,1,0:T(8,128)(2,1)S(1)}, u32[]{:S(2)}, u32[]{:S(2)}) async-start(bf16[16,9,32,128]{3,2,1,0:T(8,128)(2,1)} %bitcast.26), calls=%async_computation.1 | async-start | bytes 2359296 | tf_op jit(solution)/shard_map/all_to_all | solution.py:392
  58.6 10.3 %all-to-all-done.1 = bf16[16,9,32,128]{3,2,1,0:T(8,128)(2,1)S(1)} async-done(((bf16[16,9,32,128]{3,2,1,0:T(8,128)(2,1)}), bf16[16,9,32,128]{3,2,1,0:T(8,128)(2,1)S(1)}, u32[]{:S(2)}, u32[]{:S(2)}) %all-to-all-start.1) | async-done | bytes 1179680 | tf_op jit(solution)/shard_map/all_to_all | solution.py:392
  70.6 3.0 %collective-permute-start.5 = (bf16[32,32,128]{2,1,0:T(8,128)(2,1)}, bf16[32,32,128]{2,1,0:T(8,128)(2,1)}, u32[]{:S(2)}, u32[]{:S(2)}) collective-permute-start(bf16[32,32,128]{2,1,0:T(8,128)(2,1)} %get-tuple-element.78), channel_id=1, source_target_pairs={{0,96},{32,0},{64,32},{96,64},{1,97},{33,1},{65,33},{97,65},{2,98}... | collective-permute-start | bytes 786440 | tf_op jit(solution)/shard_map/ppermute | solution.py:268
  81.9 3.8 %collective-permute-start.3 = (bf16[88,32,128]{2,1,0:T(8,128)(2,1)}, bf16[88,32,128]{2,1,0:T(8,128)(2,1)}, u32[]{:S(2)}, u32[]{:S(2)}) collective-permute-start(bf16[88,32,128]{2,1,0:T(8,128)(2,1)} %slice.17), channel_id=1, source_target_pairs={{0,96},{32,0},{64,32},{96,64},{1,97},{33,1},{65,33},{97,65},{2,98}... | collective-permute-start | bytes 2162696 | tf_op jit(solution)/shard_map/ppermute | solution.py:268
  87.8 5.7 %prep.1 = (bf16[1024,1024]{1,0:T(8,128)(2,1)S(1)}, bf16[1024,1024]{1,0:T(8,128)(2,1)S(1)}) custom-call(s32[16,32]{1,0:T(8,128)S(1)} %copy-done.7, bf16[1024,2048]{1,0:T(8,128)(2,1)S(1)} %copy-done.2), custom_call_target="tpu_custom_call" | custom-call | tf_op jit(solution)/shard_map/prep/pallas_call | solution.py:431
  98.0 3.3 %collective-permute-start.7 = (bf16[16,32,128]{2,1,0:T(8,128)(2,1)S(1)}, bf16[16,32,128]{2,1,0:T(8,128)(2,1)S(1)}, u32[]{:S(2)}, u32[]{:S(2)}) collective-permute-start(bf16[16,32,128]{2,1,0:T(8,128)(2,1)S(1)} %slice.19), channel_id=1, source_target_pairs={{0,96},{32,0},{64,32},{96,64},{1,97},{33,1},{65,33},{97,65},{2,98}... | collective-permute-start | bytes 393224 | tf_op jit(solution)/shard_map/ppermute | solution.py:268
  112.5 8.5 %collective-permute-done.12.refs_10_ = bf16[88,32,128]{2,1,0:T(8,128)(2,1)S(1)} collective-permute-done((bf16[88,32,128]{2,1,0:T(8,128)(2,1)}, bf16[88,32,128]{2,1,0:T(8,128)(2,1)S(1)}, u32[]{:S(2)}, u32[]{:S(2)}) %collective-permute-start.12) | collective-permute-done | bytes 720928 | tf_op jit(solution)/shard_map/ppermute | solution.py:276
  122.3 3.1 %collect.1.tiles = bf16[2561,32,128]{2,1,0:T(8,128)(2,1)S(1)} custom-call(s32[3]{0:T(128)S(1)} %pad_add_fusion.misc_ref, bf16[176,32,128]{2,1,0:T(8,128)(2,1)S(1)} %bitcast.23, bf16[176,32,128]{2,1,0:T(8,128)(2,1)} %collective-permute-done.refs_1_, bf16[176,32,128]{2,1,0:T(8,128)(2,1)} %collective-permute-done.1.refs_2_, ...), custom_call_target="tpu_custom_call" | custom-call | bytes 20971520 | tf_op jit(solution)/shard_map/collect/pallas_call | solution.py:178
  125.4 7.0 %far.1 = (s16[4,544,128]{2,1,0:T(8,128)(2,1)S(1)}, s16[4,544,128]{2,1,0:T(8,128)(2,1)S(1)}, s16[4,544,128]{2,1,0:T(8,128)(2,1)S(1)}, s16[4,544,128]{2,1,0:T(8,12...) custom-call(s32[2048]{0:T(1024)S(1)} %fusion.16.index_ref, ...), custom_call_target="tpu_custom_call", output_to_operand_aliasing={{4}: (2, {}), {5}: (3, {}), {6}: (4, {})} | custom-call | flops 4294967296 | bytes 20971520 | tf_op jit(solution)/shard_map/far/pallas_call | solution.py:243
  137.7 13.1 %near.1 = (s16[2,4,544,128]{3,2,1,0:T(8,128)(2,1)S(1)}, s16[2,4,544,128]{3,2,1,0:T(8,128)(2,1)S(1)}, s16[2,4,544,128]{3,2,1,0:T(8,128)(2,1)S(1)}, s16[2,4,544,12...) custom-call(s32[2048]{0:T(1024)S(1)} %fusion.16.index_ref, ...), custom_call_target="tpu_custom_call", output_to_operand_aliasing={{4}: (2, {}), {5}: (3, {}), {6}: (4, {})} | custom-call | flops 8589934592 | bytes 20971520 | tf_op jit(solution)/shard_map/near/pallas_call | solution.py:243
  150.9 3.1 %add_first.1 = (s16[2,4,544,128]{3,2,1,0:T(8,128)(2,1)S(1)}, s16[2,4,544,128]{3,2,1,0:T(8,128)(2,1)S(1)}, s16[2,4,544,128]{3,2,1,0:T(8,128)(2,1)S(1)}, s16[2,4,544,128]{3,2,1,0:T(8,128)(2,1)S(1)}) custom-call(s16[2,4,544,128]{3,2,1,0:T(8,128)(2,1)S(1)} %get-tuple-element.103.refs_0_, s16[2,4,544,128]{3,2,1,0:T(8,128)(2,1)S(1)} %get-tuple-element.104.refs_1_, ...), custom_call_target="tpu_custom_call" | custom-call | flops 111411200 | bytes 11141120 | tf_op jit(solution)/shard_map/add_first/pallas_call | solution.py:311
  156.4 3.2 %collective-permute-start.21 = (s16[2,4,544,128]{3,2,1,0:T(8,128)(2,1)S(1)}, s16[2,4,544,128]{3,2,1,0:T(8,128)(2,1)S(1)}, u32[]{:S(2)}, u32[]{:S(2)}) collective-permute-start(s16[2,4,544,128]{3,2,1,0:T(8,128)(2,1)S(1)} %get-tuple-element.114), channel_id=1, source_target_pairs={{0,3},{1,0},{2,1},{3,2},{4,7},{5,4},{6,5},{7,6},{8,11},{9,8},{10,9... | collective-permute-start | bytes 3342344 | tf_op jit(solution)/shard_map/ppermute | solution.py:268
  159.7 6.0 %own.1 = (f32[4,1024,128]{2,1,0:T(8,128)S(1)}, f32[4,1024,128]{2,1,0:T(8,128)S(1)}) custom-call(s32[2048]{0:T(1024)S(1)} %fusion.16.index_ref, s32[3]{0:T(128)S(1)} %pad_add_fusion.misc_ref, bf16[1024,1024]{1,0:T(8,128)(2,1)S(1)} %get-tuple-element.98.even_ref, bf16[1024,1024]{1,0:T(8,128)(2,1)S(1)} %get-tuple-element.99.odd_ref, ...), custom_call_target="tpu_custom_call" | custom-call | flops 4294967296 | bytes 20971520 | tf_op jit(solution)/shard_map/own/pallas_call | solution.py:243
  165.7 13.8 %collective-permute-done.18.refs_0_ = s16[2,4,544,128]{3,2,1,0:T(8,128)(2,1)S(1)} collective-permute-done((s16[2,4,544,128]{3,2,1,0:T(8,128)(2,1)S(1)}, s16[2,4,544,128]{3,2,1,0:T(8,128)(2,1)S(1)}, u32[]{:S(2)}, u32[]{:S(2)}) %collective-permute-start.18) | collective-permute-done | bytes 1114144 | tf_op jit(solution)/shard_map/ppermute | solution.py:264
  179.5 3.3 %collective-permute-done.19.refs_1_ = s16[2,4,544,128]{3,2,1,0:T(8,128)(2,1)S(1)} collective-permute-done((s16[2,4,544,128]{3,2,1,0:T(8,128)(2,1)S(1)}, s16[2,4,544,128]{3,2,1,0:T(8,128)(2,1)S(1)}, u32[]{:S(2)}, u32[]{:S(2)}) %collective-permute-start.19) | collective-permute-done | bytes 1114144 | tf_op jit(solution)/shard_map/ppermute | solution.py:268
  182.8 3.5 %middle.1 = (s16[1,544,128]{2,1,0:T(8,128)(2,1)S(1)}, s16[1,544,128]{2,1,0:T(8,128)(2,1)S(1)}, s16[2,544,128]{2,1,0:T(8,128)(2,1)S(1)}, s16[2,544,128]{2,1,0:T(8...) custom-call(s32[3]{0:T(128)S(1)} %pad_add_fusion.misc_ref, ...), custom_call_target="tpu_custom_call" | custom-call | flops 113704960 | bytes 11370496 | tf_op jit(solution)/shard_map/middle/pallas_call | solution.py:311
  186.4 3.2 %collective-permute-start.23 = (s16[1,544,128]{2,1,0:T(8,128)(2,1)S(1)}, s16[1,544,128]{2,1,0:T(8,128)(2,1)S(1)}, u32[]{:S(2)}, u32[]{:S(2)}) collective-permute-start(s16[1,544,128]{2,1,0:T(8,128)(2,1)S(1)} %get-tuple-element.119), channel_id=1, source_target_pairs={{0,3},{1,0},{2,1},{3,2},{4,7},{5,4},{6,5},{7,6},{8,11},{9,8},{10,9... | collective-permute-start | bytes 417800 | tf_op jit(solution)/shard_map/ppermute | solution.py:268
  189.6 3.0 %collective-permute-start.24 = (s16[1,544,128]{2,1,0:T(8,128)(2,1)S(1)}, s16[1,544,128]{2,1,0:T(8,128)(2,1)S(1)}, u32[]{:S(2)}, u32[]{:S(2)}) collective-permute-start(s16[1,544,128]{2,1,0:T(8,128)(2,1)S(1)} %get-tuple-element.122), channel_id=1, source_target_pairs={{0,4},{4,8},{8,12},{12,0},{1,5},{5,9},{9,13},{13,1},{2,6},{6,10},{... | collective-permute-start | bytes 417800 | tf_op jit(solution)/shard_map/ppermute | solution.py:264
  195.2 3.7 %collective-permute-done.25.refs_7_ = s16[1,544,128]{2,1,0:T(8,128)(2,1)S(1)} collective-permute-done((s16[1,544,128]{2,1,0:T(8,128)(2,1)S(1)}, s16[1,544,128]{2,1,0:T(8,128)(2,1)S(1)}, u32[]{:S(2)}, u32[]{:S(2)}) %collective-permute-start.25) | collective-permute-done | bytes 139296 | tf_op jit(solution)/shard_map/ppermute | solution.py:268
  199.7 3.2 %collective-permute-start.27 = (s16[2,544,128]{2,1,0:T(8,128)(2,1)S(1)}, s16[2,544,128]{2,1,0:T(8,128)(2,1)S(1)}, u32[]{:S(2)}, u32[]{:S(2)}) collective-permute-start(s16[2,544,128]{2,1,0:T(8,128)(2,1)S(1)} %get-tuple-element.125), channel_id=1, source_target_pairs={{0,3},{1,0},{2,1},{3,2},{4,7},{5,4},{6,5},{7,6},{8,11},{9,8},{10,9... | collective-permute-start | bytes 835592 | tf_op jit(solution)/shard_map/ppermute | solution.py:268
  (105 shorter events, 60.1 us)
Async XLA Ops:
  16.9 28.2 %all-to-all-start = ((bf16[16,11,32,128]{3,2,1,0:T(8,128)(2,1)}), bf16[16,11,32,128]{3,2,1,0:T(8,128)(2,1)S(1)}, u32[]{:S(2)}, u32[]{:S(2)}) async-start(bf16[16,11,32,128]{3,2,1,0:T(8,128)(2,1)} %bitcast.25), calls=%async_computation | async-start | bytes 2883584 | tf_op jit(solution)/shard_map/all_to_all | solution.py:392
  45.1 34.7 %collective-permute-start.1 = (bf16[176,32,128]{2,1,0:T(8,128)(2,1)S(1)}, bf16[176,32,128]{2,1,0:T(8,128)(2,1)}, u32[]{:S(2)}, u32[]{:S(2)}) collective-permute-start(bf16[176,32,128]{2,1,0:T(8,128)(2,1)S(1)} %bitcast.20), channel_id=1, source_target_pairs={{0,96},{32,0},{64,32},{96,64},{1,97},{33,1},{65,33},{97,65},{2,98}... | collective-permute-start | bytes 4325384 | tf_op jit(solution)/shard_map/ppermute | solution.py:268
  48.2 37.5 %collective-permute-start = (bf16[176,32,128]{2,1,0:T(8,128)(2,1)S(1)}, bf16[176,32,128]{2,1,0:T(8,128)(2,1)}, u32[]{:S(2)}, u32[]{:S(2)}) collective-permute-start(bf16[176,32,128]{2,1,0:T(8,128)(2,1)S(1)} %bitcast.21), channel_id=1, source_target_pairs={{0,32},{32,64},{64,96},{96,0},{1,33},{33,65},{65,97},{97,1},{2,34}... | collective-permute-start | bytes 4325384 | tf_op jit(solution)/shard_map/ppermute | solution.py:264
  48.2 20.7 %all-to-all-start.1 = ((bf16[16,9,32,128]{3,2,1,0:T(8,128)(2,1)}), bf16[16,9,32,128]{3,2,1,0:T(8,128)(2,1)S(1)}, u32[]{:S(2)}, u32[]{:S(2)}) async-start(bf16[16,9,32,128]{3,2,1,0:T(8,128)(2,1)} %bitcast.26), calls=%async_computation.1 | async-start | bytes 2359296 | tf_op jit(solution)/shard_map/all_to_all | solution.py:392
  70.6 26.5 %collective-permute-start.5 = (bf16[32,32,128]{2,1,0:T(8,128)(2,1)}, bf16[32,32,128]{2,1,0:T(8,128)(2,1)}, u32[]{:S(2)}, u32[]{:S(2)}) collective-permute-start(bf16[32,32,128]{2,1,0:T(8,128)(2,1)} %get-tuple-element.78), channel_id=1, source_target_pairs={{0,96},{32,0},{64,32},{96,64},{1,97},{33,1},{65,33},{97,65},{2,98}... | collective-permute-start | bytes 786440 | tf_op jit(solution)/shard_map/ppermute | solution.py:268
  73.6 27.8 %collective-permute-start.4 = (bf16[32,32,128]{2,1,0:T(8,128)(2,1)}, bf16[32,32,128]{2,1,0:T(8,128)(2,1)}, u32[]{:S(2)}, u32[]{:S(2)}) collective-permute-start(bf16[32,32,128]{2,1,0:T(8,128)(2,1)} %get-tuple-element.78), channel_id=1, source_target_pairs={{0,32},{32,64},{64,96},{96,0},{1,33},{33,65},{65,97},{97,1},{2,34}... | collective-permute-start | bytes 786440 | tf_op jit(solution)/shard_map/ppermute | solution.py:264
  81.9 28.0 %collective-permute-start.3 = (bf16[88,32,128]{2,1,0:T(8,128)(2,1)}, bf16[88,32,128]{2,1,0:T(8,128)(2,1)}, u32[]{:S(2)}, u32[]{:S(2)}) collective-permute-start(bf16[88,32,128]{2,1,0:T(8,128)(2,1)} %slice.17), channel_id=1, source_target_pairs={{0,96},{32,0},{64,32},{96,64},{1,97},{33,1},{65,33},{97,65},{2,98}... | collective-permute-start | bytes 2162696 | tf_op jit(solution)/shard_map/ppermute | solution.py:268
  87.7 22.1 %collective-permute-start.2 = (bf16[88,32,128]{2,1,0:T(8,128)(2,1)}, bf16[88,32,128]{2,1,0:T(8,128)(2,1)}, u32[]{:S(2)}, u32[]{:S(2)}) collective-permute-start(bf16[88,32,128]{2,1,0:T(8,128)(2,1)} %slice.16), channel_id=1, source_target_pairs={{0,32},{32,64},{64,96},{96,0},{1,33},{33,65},{65,97},{97,1},{2,34}... | collective-permute-start | bytes 2162696 | tf_op jit(solution)/shard_map/ppermute | solution.py:264
  98.0 11.1 %collective-permute-start.7 = (bf16[16,32,128]{2,1,0:T(8,128)(2,1)S(1)}, bf16[16,32,128]{2,1,0:T(8,128)(2,1)S(1)}, u32[]{:S(2)}, u32[]{:S(2)}) collective-permute-start(bf16[16,32,128]{2,1,0:T(8,128)(2,1)S(1)} %slice.19), channel_id=1, source_target_pairs={{0,96},{32,0},{64,32},{96,64},{1,97},{33,1},{65,33},{97,65},{2,98}... | collective-permute-start | bytes 393224 | tf_op jit(solution)/shard_map/ppermute | solution.py:268
  109.9 11.1 %collective-permute-start.8 = (bf16[176,32,128]{2,1,0:T(8,128)(2,1)S(1)}, bf16[176,32,128]{2,1,0:T(8,128)(2,1)S(1)}, u32[]{:S(2)}, u32[]{:S(2)}) collective-permute-start(bf16[176,32,128]{2,1,0:T(8,128)(2,1)S(1)} %bitcast.22), channel_id=1, source_target_pairs={{0,16},{16,0},{1,17},{17,1},{2,18},{18,2},{3,19},{19,3},{4,20},{20... | collective-permute-start | bytes 4325384 | tf_op jit(solution)/shard_map/ppermute | solution.py:276
  110.4 10.6 %collective-permute-start.9 = (bf16[176,32,128]{2,1,0:T(8,128)(2,1)}, bf16[176,32,128]{2,1,0:T(8,128)(2,1)S(1)}, u32[]{:S(2)}, u32[]{:S(2)}) collective-permute-start(bf16[176,32,128]{2,1,0:T(8,128)(2,1)} %collective-permute-done.refs_1_), channel_id=1, source_target_pairs={{0,16},{16,0},{1,17},{17,1},{2,18},{18,2},{3,19},{19,3},{4,20},{20... | collective-permute-start | bytes 4325384 | tf_op jit(solution)/shard_map/ppermute | solution.py:276
  110.5 10.5 %collective-permute-start.10 = (bf16[176,32,128]{2,1,0:T(8,128)(2,1)}, bf16[176,32,128]{2,1,0:T(8,128)(2,1)S(1)}, u32[]{:S(2)}, u32[]{:S(2)}) collective-permute-start(bf16[176,32,128]{2,1,0:T(8,128)(2,1)} %collective-permute-done.1.refs_2_), channel_id=1, source_target_pairs={{0,16},{16,0},{1,17},{17,1},{2,18},{18,2},{3,19},{19,3},{4,20},{20... | collective-permute-start | bytes 4325384 | tf_op jit(solution)/shard_map/ppermute | solution.py:276
  110.9 10.1 %collective-permute-start.13 = (bf16[128,32,128]{2,1,0:T(8,128)(2,1)}, bf16[128,32,128]{2,1,0:T(8,128)(2,1)S(1)}, u32[]{:S(2)}, u32[]{:S(2)}) collective-permute-start(bf16[128,32,128]{2,1,0:T(8,128)(2,1)} %constant_dynamic-update-slice_fusion.refs_5_), channel_id=1, source_target_pairs={{0,16},{16,0},{1,17},{17,1},{2,18},{18,2},{3,19},{19,3},{4,20},{20... | collective-permute-start | bytes 3145736 | tf_op jit(solution)/shard_map/ppermute | solution.py:276
  112.4 8.6 %collective-permute-start.12 = (bf16[88,32,128]{2,1,0:T(8,128)(2,1)}, bf16[88,32,128]{2,1,0:T(8,128)(2,1)S(1)}, u32[]{:S(2)}, u32[]{:S(2)}) collective-permute-start(bf16[88,32,128]{2,1,0:T(8,128)(2,1)} %collective-permute-done.3.refs_4_), channel_id=1, source_target_pairs={{0,16},{16,0},{1,17},{17,1},{2,18},{18,2},{3,19},{19,3},{4,20},{20... | collective-permute-start | bytes 2162696 | tf_op jit(solution)/shard_map/ppermute | solution.py:276
  132.4 18.4 %collective-permute-start.14 = (s16[4,544,128]{2,1,0:T(8,128)(2,1)S(1)}, s16[4,544,128]{2,1,0:T(8,128)(2,1)S(1)}, u32[]{:S(2)}, u32[]{:S(2)}) collective-permute-start(s16[4,544,128]{2,1,0:T(8,128)(2,1)S(1)} %get-tuple-element.105), channel_id=1, source_target_pairs={{0,4},{4,8},{8,12},{12,0},{1,5},{5,9},{9,13},{13,1},{2,6},{6,10},{... | collective-permute-start | bytes 1671176 | tf_op jit(solution)/shard_map/ppermute | solution.py:264
  133.7 17.1 %collective-permute-start.15 = (s16[4,544,128]{2,1,0:T(8,128)(2,1)S(1)}, s16[4,544,128]{2,1,0:T(8,128)(2,1)S(1)}, u32[]{:S(2)}, u32[]{:S(2)}) collective-permute-start(s16[4,544,128]{2,1,0:T(8,128)(2,1)S(1)} %get-tuple-element.106), channel_id=1, source_target_pairs={{0,12},{4,0},{8,4},{12,8},{1,13},{5,1},{9,5},{13,9},{2,14},{6,2},{... | collective-permute-start | bytes 1671176 | tf_op jit(solution)/shard_map/ppermute | solution.py:268
  134.5 16.3 %collective-permute-start.16 = (s16[4,544,128]{2,1,0:T(8,128)(2,1)S(1)}, s16[4,544,128]{2,1,0:T(8,128)(2,1)S(1)}, u32[]{:S(2)}, u32[]{:S(2)}) collective-permute-start(s16[4,544,128]{2,1,0:T(8,128)(2,1)S(1)} %get-tuple-element.109), channel_id=1, source_target_pairs={{0,1},{1,2},{2,3},{3,0},{4,5},{5,6},{6,7},{7,4},{8,9},{9,10},{10,1... | collective-permute-start | bytes 1671176 | tf_op jit(solution)/shard_map/ppermute | solution.py:264
  135.1 15.8 %collective-permute-start.17 = (s16[4,544,128]{2,1,0:T(8,128)(2,1)S(1)}, s16[4,544,128]{2,1,0:T(8,128)(2,1)S(1)}, u32[]{:S(2)}, u32[]{:S(2)}) collective-permute-start(s16[4,544,128]{2,1,0:T(8,128)(2,1)S(1)} %get-tuple-element.110), channel_id=1, source_target_pairs={{0,3},{1,0},{2,1},{3,2},{4,7},{5,4},{6,5},{7,6},{8,11},{9,8},{10,9... | collective-permute-start | bytes 1671176 | tf_op jit(solution)/shard_map/ppermute | solution.py:268
  153.9 25.5 %collective-permute-start.18 = (s16[2,4,544,128]{3,2,1,0:T(8,128)(2,1)S(1)}, s16[2,4,544,128]{3,2,1,0:T(8,128)(2,1)S(1)}, u32[]{:S(2)}, u32[]{:S(2)}) collective-permute-start(s16[2,4,544,128]{3,2,1,0:T(8,128)(2,1)S(1)} %get-tuple-element.111), channel_id=1, source_target_pairs={{0,4},{4,8},{8,12},{12,0},{1,5},{5,9},{9,13},{13,1},{2,6},{6,10},{... | collective-permute-start | bytes 3342344 | tf_op jit(solution)/shard_map/ppermute | solution.py:264
  156.4 26.4 %collective-permute-start.19 = (s16[2,4,544,128]{3,2,1,0:T(8,128)(2,1)S(1)}, s16[2,4,544,128]{3,2,1,0:T(8,128)(2,1)S(1)}, u32[]{:S(2)}, u32[]{:S(2)}) collective-permute-start(s16[2,4,544,128]{3,2,1,0:T(8,128)(2,1)S(1)} %get-tuple-element.112), channel_id=1, source_target_pairs={{0,12},{4,0},{8,4},{12,8},{1,13},{5,1},{9,5},{13,9},{2,14},{6,2},{... | collective-permute-start | bytes 3342344 | tf_op jit(solution)/shard_map/ppermute | solution.py:268
  156.4 26.4 %collective-permute-start.20 = (s16[2,4,544,128]{3,2,1,0:T(8,128)(2,1)S(1)}, s16[2,4,544,128]{3,2,1,0:T(8,128)(2,1)S(1)}, u32[]{:S(2)}, u32[]{:S(2)}) collective-permute-start(s16[2,4,544,128]{3,2,1,0:T(8,128)(2,1)S(1)} %get-tuple-element.113), channel_id=1, source_target_pairs={{0,1},{1,2},{2,3},{3,0},{4,5},{5,6},{6,7},{7,4},{8,9},{9,10},{10,1... | collective-permute-start | bytes 3342344 | tf_op jit(solution)/shard_map/ppermute | solution.py:264
  156.4 26.4 %collective-permute-start.21 = (s16[2,4,544,128]{3,2,1,0:T(8,128)(2,1)S(1)}, s16[2,4,544,128]{3,2,1,0:T(8,128)(2,1)S(1)}, u32[]{:S(2)}, u32[]{:S(2)}) collective-permute-start(s16[2,4,544,128]{3,2,1,0:T(8,128)(2,1)S(1)} %get-tuple-element.114), channel_id=1, source_target_pairs={{0,3},{1,0},{2,1},{3,2},{4,7},{5,4},{6,5},{7,6},{8,11},{9,8},{10,9... | collective-permute-start | bytes 3342344 | tf_op jit(solution)/shard_map/ppermute | solution.py:268
  199.6 7.8 %collective-permute-start.26 = (s16[2,544,128]{2,1,0:T(8,128)(2,1)S(1)}, s16[2,544,128]{2,1,0:T(8,128)(2,1)S(1)}, u32[]{:S(2)}, u32[]{:S(2)}) collective-permute-start(s16[2,544,128]{2,1,0:T(8,128)(2,1)S(1)} %get-tuple-element.124), channel_id=1, source_target_pairs={{0,1},{1,2},{2,3},{3,0},{4,5},{5,6},{6,7},{7,4},{8,9},{9,10},{10,1... | collective-permute-start | bytes 835592 | tf_op jit(solution)/shard_map/ppermute | solution.py:264
  202.9 7.8 %collective-permute-start.29 = (s16[2,544,128]{2,1,0:T(8,128)(2,1)S(1)}, s16[2,544,128]{2,1,0:T(8,128)(2,1)S(1)}, u32[]{:S(2)}, u32[]{:S(2)}) collective-permute-start(s16[2,544,128]{2,1,0:T(8,128)(2,1)S(1)} %get-tuple-element.127), channel_id=1, source_target_pairs={{0,12},{4,0},{8,4},{12,8},{1,13},{5,1},{9,5},{13,9},{2,14},{6,2},{... | collective-permute-start | bytes 835592 | tf_op jit(solution)/shard_map/ppermute | solution.py:268
  (16 other events, 91.1 us)

commit v5 on v3

--- a/solution.py
+++ b/solution.py
@@ -27,7 +27,7 @@
 CORE = 4 * FIRST + 4 * EXTRA
 THIRD = ROWS * (SECOND - EXTRA)
 POOL = 2 * CORE + THIRD
-PARTS = 12
+PARTS = 14
 HALF = 512
 PACKED = HALF + HALF // 16
 VMEM_GRANT = 10 * 1024 * 1024
@@ -195,7 +195,7 @@
         out_specs=pl.BlockSpec(memory_space=pltpu.VMEM),
         out_shape=jax.ShapeDtypeStruct((POOL + 1, SUB, 128), jnp.bfloat16),
         scratch_shapes=[pltpu.SemaphoreType.DMA((PARTS + 1,))],
-        compiler_params=pltpu.CompilerParams(vmem_limit_bytes=VMEM_GRANT),
+        compiler_params=pltpu.CompilerParams(vmem_limit_bytes=2 * 1024 * 1024),
         cost_estimate=pl.CostEstimate(flops=0, bytes_accessed=POOL * 8192, transcendentals=0),
         name="collect",
     )(misc, *parts, third)
@@ -490,13 +490,11 @@
     from_up, from_down, swapped, even, odd, tile_index, misc, third = lax.optimization_barrier(
         (from_up, from_down, swapped, even, odd, tile_index, misc, third)
     )
-    tail_up = ahead("y", from_up[half : half + EXTRA // 2])
-    tail_down = behind("y", from_down[half + EXTRA // 2 :])
-    swapped_late = swap([from_up, from_down])
-    tail_up, tail_down, swapped_late = lax.optimization_barrier((tail_up, tail_down, swapped_late))
-    tail = jnp.concatenate([some, tail_up, tail_down])
-    parts = [first, up, down, from_up, from_down, tail, *swapped, *swapped_late, *swap([tail])]
-    tiles = collect_call(misc, parts, third)
+    tails = from_up[half : half + EXTRA // 2], from_down[half + EXTRA // 2 :]
+    tails, from_up, from_down = lax.optimization_barrier((tails, from_up, from_down))
+    tail_up, tail_down = ahead("y", tails[0]), behind("y", tails[1])
+    parts = [first, up, down, from_up, from_down, some, jnp.concatenate([tail_up, tail_down])]
+    tiles = collect_call(misc, parts + swapped + swap(parts[3:]), third)
 
     scalars = (tile_index, misc)
     far, arrays = product_call("far", (2,), scalars, (even, odd, tiles))

time: 218 us -> 214 us (0.982)
  waiting for transfers between devices: 82.3 us -> 78 us
    ppermute x11, waiting for transfers between devices: 14.9 us -> 10.4 us  [behind(): return lax.ppermute(value, axis, [(i, (i + 3) % 4) for i in range(4)])]
    unnamed x23 -> x22, local copies, waits for them, and re-layouts: 8.2 us -> 8.14 us
  transfers between devices with their start and end apart: 30 -> 31, of which waited for: 14 -> 14; matrix products, arithmetic and copies ran while one was open for 4% -> 3% of each run, Pallas kernels for 13% -> 13%
where the time goes in v5:
time: 214 us; the launch traced here: 213 us
  waiting for transfers between devices  78 us (36%)
  Pallas kernels  56.7 us (26%)
  starting transfers between devices  47.5 us (22%)
  between operations  14.5 us (7%)
  local copies, waits for them, and re-layouts  10.5 us (5%)
  other arithmetic  3.79 us (2%)
    ppermute x11, waiting for transfers between devices, ahead(): return lax.ppermute(value, axis, [(i, (i + 1) % 4) for i in range(4)])  35.6 us
    all_to_all x2, waiting for transfers between devices, send(): lax.all_to_all(part, ('x', 'z'), split_axis=0, concat_axis=0, tiled=True)  29.9 us
    pallas_call x3, Pallas kernels, product_call(): pl.pallas_call(functools.partial(product_kernel, hops), grid_spec=pltpu.P...  26.1 us
    ppermute x11, starting transfers between devices, behind(): return lax.ppermute(value, axis, [(i, (i + 3) % 4) for i in range(4)])  24.8 us
    all_to_all x2, starting transfers between devices, send(): lax.all_to_all(part, ('x', 'z'), split_axis=0, concat_axis=0, tiled=True)  14.4 us
    ppermute x11, waiting for transfers between devices, behind(): return lax.ppermute(value, axis, [(i, (i + 3) % 4) for i in range(4)])  10.4 us
    pallas_call x4, Pallas kernels, whole_call(): pl.pallas_call(body, in_specs=[pl.BlockSpec(memory_space=pltpu.SMEM)] * l...  8.73 us
    unnamed x22, local copies, waits for them, and re-layouts  8.14 us
  transfers between devices with their start and end apart: 31, of which 14 were waited for; matrix products, arithmetic and copies ran while one was open for 3% of the time, Pallas kernels for 13%

profile of v5, /device:TPU:6, one launch (start us, length us, event | category | flops | bytes accessed | tf_op | source)
XLA Modules:
  0.0 213.0 jit_solution(282642444908526713)
XLA Ops:
  9.8 4.6 %fill.1 = (bf16[128,32,128]{2,1,0:T(8,128)(2,1)S(1)}, bf16[192,32,128]{2,1,0:T(8,128)(2,1)S(1)}) custom-call(s32[16,128]{1,0:T(8,128)S(1)} %route.1.index_ref, bf16[320,32,128]{2,1,0:T(8,128)(2,1)S(1)} %bitcast.19), custom_call_target="tpu_custom_call" | custom-call | tf_op jit(solution)/shard_map/fill/pallas_call | solution.py:381
  16.6 8.3 %all-to-all-start = ((bf16[16,8,32,128]{3,2,1,0:T(8,128)(2,1)}), bf16[16,8,32,128]{3,2,1,0:T(8,128)(2,1)S(1)}, u32[]{:S(2)}, u32[]{:S(2)}) async-start(bf16[16,8,32,128]{3,2,1,0:T(8,128)(2,1)} %bitcast.26), calls=%async_computation | async-start | bytes 2097152 | tf_op jit(solution)/shard_map/all_to_all | solution.py:401
  24.9 15.2 %all-to-all-done = bf16[16,8,32,128]{3,2,1,0:T(8,128)(2,1)S(1)} async-done(((bf16[16,8,32,128]{3,2,1,0:T(8,128)(2,1)}), bf16[16,8,32,128]{3,2,1,0:T(8,128)(2,1)S(1)}, u32[]{:S(2)}, u32[]{:S(2)}) %all-to-all-start) | async-done | bytes 1048608 | tf_op jit(solution)/shard_map/all_to_all | solution.py:401
  40.1 3.0 %collective-permute-start.1 = (bf16[128,32,128]{2,1,0:T(8,128)(2,1)S(1)}, bf16[128,32,128]{2,1,0:T(8,128)(2,1)}, u32[]{:S(2)}, u32[]{:S(2)}) collective-permute-start(bf16[128,32,128]{2,1,0:T(8,128)(2,1)S(1)} %bitcast.21), channel_id=1, source_target_pairs={{0,96},{32,0},{64,32},{96,64},{1,97},{33,1},{65,33},{97,65},{2,98}... | collective-permute-start | bytes 3145736 | tf_op jit(solution)/shard_map/ppermute | solution.py:282
  43.1 6.1 %all-to-all-start.1 = ((bf16[16,12,32,128]{3,2,1,0:T(8,128)(2,1)}), bf16[16,12,32,128]{3,2,1,0:T(8,128)(2,1)S(1)}, u32[]{:S(2)}, u32[]{:S(2)}) async-start(bf16[16,12,32,128]{3,2,1,0:T(8,128)(2,1)} %bitcast.25), calls=%async_computation.1 | async-start | bytes 3145728 | tf_op jit(solution)/shard_map/all_to_all | solution.py:401
  53.5 14.7 %all-to-all-done.1 = bf16[16,12,32,128]{3,2,1,0:T(8,128)(2,1)S(1)} async-done(((bf16[16,12,32,128]{3,2,1,0:T(8,128)(2,1)}), bf16[16,12,32,128]{3,2,1,0:T(8,128)(2,1)S(1)}, u32[]{:S(2)}, u32[]{:S(2)}) %all-to-all-start.1) | async-done | bytes 1572896 | tf_op jit(solution)/shard_map/all_to_all | solution.py:401
  69.9 3.7 %join.1 = (bf16[144,32,128]{2,1,0:T(8,128)(2,1)}, bf16[144,32,128]{2,1,0:T(8,128)(2,1)}) custom-call(bf16[128,32,128]{2,1,0:T(8,128)(2,1)} %collective-permute-done.up_ref.refs_1_, bf16[128,32,128]{2,1,0:T(8,128)(2,1)} %collective-permute-done.1.down_ref.refs_2_, bf16[80,32,128]{2,1,0:T(8,128)(2,1)S(1)} %get-tuple-element.90.some_ref.refs_5_), custom_call_target="tpu_custom_call" | custom-call | tf_op jit(solution)/shard_map/join/pallas_call | solution.py:435
  74.0 2.9 %collective-permute-start.3 = (bf16[144,32,128]{2,1,0:T(8,128)(2,1)}, bf16[144,32,128]{2,1,0:T(8,128)(2,1)}, u32[]{:S(2)}, u32[]{:S(2)}) collective-permute-start(bf16[144,32,128]{2,1,0:T(8,128)(2,1)} %get-tuple-element.93), channel_id=1, source_target_pairs={{0,96},{32,0},{64,32},{96,64},{1,97},{33,1},{65,33},{97,65},{2,98}... | collective-permute-start | bytes 3538952 | tf_op jit(solution)/shard_map/ppermute | solution.py:282
  79.8 5.7 %prep.1 = (bf16[1024,1024]{1,0:T(8,128)(2,1)S(1)}, bf16[1024,1024]{1,0:T(8,128)(2,1)S(1)}) custom-call(s32[16,32]{1,0:T(8,128)S(1)} %copy-done.8, bf16[1024,2048]{1,0:T(8,128)(2,1)S(1)} %copy-done.2), custom_call_target="tpu_custom_call" | custom-call | tf_op jit(solution)/shard_map/prep/pallas_call | solution.py:450
  90.8 9.7 %collective-permute-done.2.refs_3_ = bf16[144,32,128]{2,1,0:T(8,128)(2,1)} collective-permute-done((bf16[144,32,128]{2,1,0:T(8,128)(2,1)}, bf16[144,32,128]{2,1,0:T(8,128)(2,1)}, u32[]{:S(2)}, u32[]{:S(2)}) %collective-permute-start.2) | collective-permute-done | bytes 1179680 | tf_op jit(solution)/shard_map/ppermute | solution.py:278
  106.3 4.5 %collective-permute-done.7 = bf16[40,32,128]{2,1,0:T(8,128)(2,1)S(1)} collective-permute-done((bf16[40,32,128]{2,1,0:T(8,128)(2,1)S(1)}, bf16[40,32,128]{2,1,0:T(8,128)(2,1)S(1)}, u32[]{:S(2)}, u32[]{:S(2)}) %collective-permute-start.7) | collective-permute-done | bytes 327712 | tf_op jit(solution)/shard_map/ppermute | solution.py:278
  116.1 4.0 %collect.1.tiles = bf16[2561,32,128]{2,1,0:T(8,128)(2,1)S(1)} custom-call(s32[3]{0:T(128)S(1)} %pad_add_fusion.misc_ref, bf16[128,32,128]{2,1,0:T(8,128)(2,1)S(1)} %bitcast.24, bf16[128,32,128]{2,1,0:T(8,128)(2,1)} %collective-permute-done.up_ref.refs_1_, bf16[128,32,128]{2,1,0:T(8,128)(2,1)} %collective-permute-done.1.down_ref.refs_2_, ...), custom_call_target="tpu_custom_call" | custom-call | bytes 20971520 | tf_op jit(solution)/shard_map/collect/pallas_call | solution.py:192
  120.2 7.0 %far.1 = (s16[4,544,128]{2,1,0:T(8,128)(2,1)S(1)}, s16[4,544,128]{2,1,0:T(8,128)(2,1)S(1)}, s16[4,544,128]{2,1,0:T(8,128)(2,1)S(1)}, s16[4,544,128]{2,1,0:T(8,12...) custom-call(s32[2048]{0:T(1024)S(1)} %select_select_fusion.index_ref, ...), custom_call_target="tpu_custom_call", output_to_operand_aliasing={{4}: (2, {}), {5}: (3, {}), {6}: (4, {})} | custom-call | flops 4294967296 | bytes 20971520 | tf_op jit(solution)/shard_map/far/pallas_call | solution.py:257
  129.3 3.2 %collective-permute-start.16 = (s16[4,544,128]{2,1,0:T(8,128)(2,1)S(1)}, s16[4,544,128]{2,1,0:T(8,128)(2,1)S(1)}, u32[]{:S(2)}, u32[]{:S(2)}) collective-permute-start(s16[4,544,128]{2,1,0:T(8,128)(2,1)S(1)} %get-tuple-element.130), channel_id=1, source_target_pairs={{0,3},{1,0},{2,1},{3,2},{4,7},{5,4},{6,5},{7,6},{8,11},{9,8},{10,9... | collective-permute-start | bytes 1671176 | tf_op jit(solution)/shard_map/ppermute | solution.py:282
  132.5 13.1 %near.1 = (s16[2,4,544,128]{3,2,1,0:T(8,128)(2,1)S(1)}, s16[2,4,544,128]{3,2,1,0:T(8,128)(2,1)S(1)}, s16[2,4,544,128]{3,2,1,0:T(8,128)(2,1)S(1)}, s16[2,4,544,12...) custom-call(s32[2048]{0:T(1024)S(1)} %select_select_fusion.index_ref, ...), custom_call_target="tpu_custom_call", output_to_operand_aliasing={{4}: (2, {}), {5}: (3, {}), {6}: (4, {})} | custom-call | flops 8589934592 | bytes 20971520 | tf_op jit(solution)/shard_map/near/pallas_call | solution.py:257
  145.6 3.1 %add_first.1 = (s16[2,4,544,128]{3,2,1,0:T(8,128)(2,1)S(1)}, s16[2,4,544,128]{3,2,1,0:T(8,128)(2,1)S(1)}, s16[2,4,544,128]{3,2,1,0:T(8,128)(2,1)S(1)}, s16[2,4,544,128]{3,2,1,0:T(8,128)(2,1)S(1)}) custom-call(s16[2,4,544,128]{3,2,1,0:T(8,128)(2,1)S(1)} %get-tuple-element.123.refs_0_, s16[2,4,544,128]{3,2,1,0:T(8,128)(2,1)S(1)} %get-tuple-element.124.refs_1_, ...), custom_call_target="tpu_custom_call" | custom-call | flops 111411200 | bytes 11141120 | tf_op jit(solution)/shard_map/add_first/pallas_call | solution.py:320
  150.9 3.1 %collective-permute-start.20 = (s16[2,4,544,128]{3,2,1,0:T(8,128)(2,1)S(1)}, s16[2,4,544,128]{3,2,1,0:T(8,128)(2,1)S(1)}, u32[]{:S(2)}, u32[]{:S(2)}) collective-permute-start(s16[2,4,544,128]{3,2,1,0:T(8,128)(2,1)S(1)} %get-tuple-element.134), channel_id=1, source_target_pairs={{0,3},{1,0},{2,1},{3,2},{4,7},{5,4},{6,5},{7,6},{8,11},{9,8},{10,9... | collective-permute-start | bytes 3342344 | tf_op jit(solution)/shard_map/ppermute | solution.py:282
  154.0 6.0 %own.1 = (f32[4,1024,128]{2,1,0:T(8,128)S(1)}, f32[4,1024,128]{2,1,0:T(8,128)S(1)}) custom-call(s32[2048]{0:T(1024)S(1)} %select_select_fusion.index_ref, s32[3]{0:T(128)S(1)} %pad_add_fusion.misc_ref, bf16[1024,1024]{1,0:T(8,128)(2,1)S(1)} %get-tuple-element.118.even_ref, bf16[1024,1024]{1,0:T(8,128)(2,1)S(1)} %get-tuple-element.119.odd_ref, ...), custom_call_target="tpu_custom_call" | custom-call | flops 4294967296 | bytes 20971520 | tf_op jit(solution)/shard_map/own/pallas_call | solution.py:257
  160.1 14.2 %collective-permute-done.17.refs_0_ = s16[2,4,544,128]{3,2,1,0:T(8,128)(2,1)S(1)} collective-permute-done((s16[2,4,544,128]{3,2,1,0:T(8,128)(2,1)S(1)}, s16[2,4,544,128]{3,2,1,0:T(8,128)(2,1)S(1)}, u32[]{:S(2)}, u32[]{:S(2)}) %collective-permute-start.17) | collective-permute-done | bytes 1114144 | tf_op jit(solution)/shard_map/ppermute | solution.py:278
  177.0 3.5 %middle.1 = (s16[1,544,128]{2,1,0:T(8,128)(2,1)S(1)}, s16[1,544,128]{2,1,0:T(8,128)(2,1)S(1)}, s16[2,544,128]{2,1,0:T(8,128)(2,1)S(1)}, s16[2,544,128]{2,1,0:T(8...) custom-call(s32[3]{0:T(128)S(1)} %pad_add_fusion.misc_ref, ...), custom_call_target="tpu_custom_call" | custom-call | flops 113704960 | bytes 11370496 | tf_op jit(solution)/shard_map/middle/pallas_call | solution.py:320
  180.5 3.2 %collective-permute-start.22 = (s16[1,544,128]{2,1,0:T(8,128)(2,1)S(1)}, s16[1,544,128]{2,1,0:T(8,128)(2,1)S(1)}, u32[]{:S(2)}, u32[]{:S(2)}) collective-permute-start(s16[1,544,128]{2,1,0:T(8,128)(2,1)S(1)} %get-tuple-element.139), channel_id=1, source_target_pairs={{0,3},{1,0},{2,1},{3,2},{4,7},{5,4},{6,5},{7,6},{8,11},{9,8},{10,9... | collective-permute-start | bytes 417800 | tf_op jit(solution)/shard_map/ppermute | solution.py:282
  183.7 2.9 %collective-permute-start.23 = (s16[1,544,128]{2,1,0:T(8,128)(2,1)S(1)}, s16[1,544,128]{2,1,0:T(8,128)(2,1)S(1)}, u32[]{:S(2)}, u32[]{:S(2)}) collective-permute-start(s16[1,544,128]{2,1,0:T(8,128)(2,1)S(1)} %get-tuple-element.142), channel_id=1, source_target_pairs={{0,4},{4,8},{8,12},{12,0},{1,5},{5,9},{9,13},{13,1},{2,6},{6,10},{... | collective-permute-start | bytes 417800 | tf_op jit(solution)/shard_map/ppermute | solution.py:278
  189.3 3.7 %collective-permute-done.24.refs_7_ = s16[1,544,128]{2,1,0:T(8,128)(2,1)S(1)} collective-permute-done((s16[1,544,128]{2,1,0:T(8,128)(2,1)S(1)}, s16[1,544,128]{2,1,0:T(8,128)(2,1)S(1)}, u32[]{:S(2)}, u32[]{:S(2)}) %collective-permute-start.24) | collective-permute-done | bytes 139296 | tf_op jit(solution)/shard_map/ppermute | solution.py:282
  193.8 3.2 %collective-permute-start.26 = (s16[2,544,128]{2,1,0:T(8,128)(2,1)S(1)}, s16[2,544,128]{2,1,0:T(8,128)(2,1)S(1)}, u32[]{:S(2)}, u32[]{:S(2)}) collective-permute-start(s16[2,544,128]{2,1,0:T(8,128)(2,1)S(1)} %get-tuple-element.145), channel_id=1, source_target_pairs={{0,3},{1,0},{2,1},{3,2},{4,7},{5,4},{6,5},{7,6},{8,11},{9,8},{10,9... | collective-permute-start | bytes 835592 | tf_op jit(solution)/shard_map/ppermute | solution.py:282
  (103 shorter events, 51.1 us)
Async XLA Ops:
  16.6 23.5 %all-to-all-start = ((bf16[16,8,32,128]{3,2,1,0:T(8,128)(2,1)}), bf16[16,8,32,128]{3,2,1,0:T(8,128)(2,1)S(1)}, u32[]{:S(2)}, u32[]{:S(2)}) async-start(bf16[16,8,32,128]{3,2,1,0:T(8,128)(2,1)} %bitcast.26), calls=%async_computation | async-start | bytes 2097152 | tf_op jit(solution)/shard_map/all_to_all | solution.py:401
  40.1 29.8 %collective-permute-start.1 = (bf16[128,32,128]{2,1,0:T(8,128)(2,1)S(1)}, bf16[128,32,128]{2,1,0:T(8,128)(2,1)}, u32[]{:S(2)}, u32[]{:S(2)}) collective-permute-start(bf16[128,32,128]{2,1,0:T(8,128)(2,1)S(1)} %bitcast.21), channel_id=1, source_target_pairs={{0,96},{32,0},{64,32},{96,64},{1,97},{33,1},{65,33},{97,65},{2,98}... | collective-permute-start | bytes 3145736 | tf_op jit(solution)/shard_map/ppermute | solution.py:282
  43.1 26.8 %collective-permute-start = (bf16[128,32,128]{2,1,0:T(8,128)(2,1)S(1)}, bf16[128,32,128]{2,1,0:T(8,128)(2,1)}, u32[]{:S(2)}, u32[]{:S(2)}) collective-permute-start(bf16[128,32,128]{2,1,0:T(8,128)(2,1)S(1)} %bitcast.22), channel_id=1, source_target_pairs={{0,32},{32,64},{64,96},{96,0},{1,33},{33,65},{65,97},{97,1},{2,34}... | collective-permute-start | bytes 3145736 | tf_op jit(solution)/shard_map/ppermute | solution.py:278
  43.1 25.2 %all-to-all-start.1 = ((bf16[16,12,32,128]{3,2,1,0:T(8,128)(2,1)}), bf16[16,12,32,128]{3,2,1,0:T(8,128)(2,1)S(1)}, u32[]{:S(2)}, u32[]{:S(2)}) async-start(bf16[16,12,32,128]{3,2,1,0:T(8,128)(2,1)} %bitcast.25), calls=%async_computation.1 | async-start | bytes 3145728 | tf_op jit(solution)/shard_map/all_to_all | solution.py:401
  73.6 26.8 %collective-permute-start.2 = (bf16[144,32,128]{2,1,0:T(8,128)(2,1)}, bf16[144,32,128]{2,1,0:T(8,128)(2,1)}, u32[]{:S(2)}, u32[]{:S(2)}) collective-permute-start(bf16[144,32,128]{2,1,0:T(8,128)(2,1)} %get-tuple-element.92), channel_id=1, source_target_pairs={{0,32},{32,64},{64,96},{96,0},{1,33},{33,65},{65,97},{97,1},{2,34}... | collective-permute-start | bytes 3538952 | tf_op jit(solution)/shard_map/ppermute | solution.py:278
  74.0 26.5 %collective-permute-start.3 = (bf16[144,32,128]{2,1,0:T(8,128)(2,1)}, bf16[144,32,128]{2,1,0:T(8,128)(2,1)}, u32[]{:S(2)}, u32[]{:S(2)}) collective-permute-start(bf16[144,32,128]{2,1,0:T(8,128)(2,1)} %get-tuple-element.93), channel_id=1, source_target_pairs={{0,96},{32,0},{64,32},{96,64},{1,97},{33,1},{65,33},{97,65},{2,98}... | collective-permute-start | bytes 3538952 | tf_op jit(solution)/shard_map/ppermute | solution.py:282
  76.9 13.8 %collective-permute-start.4 = (bf16[128,32,128]{2,1,0:T(8,128)(2,1)S(1)}, bf16[128,32,128]{2,1,0:T(8,128)(2,1)}, u32[]{:S(2)}, u32[]{:S(2)}) collective-permute-start(bf16[128,32,128]{2,1,0:T(8,128)(2,1)S(1)} %bitcast.23), channel_id=1, source_target_pairs={{0,16},{16,0},{1,17},{17,1},{2,18},{18,2},{3,19},{19,3},{4,20},{20... | collective-permute-start | bytes 3145736 | tf_op jit(solution)/shard_map/ppermute | solution.py:290
  76.9 13.8 %collective-permute-start.5 = (bf16[128,32,128]{2,1,0:T(8,128)(2,1)}, bf16[128,32,128]{2,1,0:T(8,128)(2,1)}, u32[]{:S(2)}, u32[]{:S(2)}) collective-permute-start(bf16[128,32,128]{2,1,0:T(8,128)(2,1)} %collective-permute-done.up_ref.refs_1_), channel_id=1, source_target_pairs={{0,16},{16,0},{1,17},{17,1},{2,18},{18,2},{3,19},{19,3},{4,20},{20... | collective-permute-start | bytes 3145736 | tf_op jit(solution)/shard_map/ppermute | solution.py:290
  77.4 13.3 %collective-permute-start.6 = (bf16[128,32,128]{2,1,0:T(8,128)(2,1)}, bf16[128,32,128]{2,1,0:T(8,128)(2,1)}, u32[]{:S(2)}, u32[]{:S(2)}) collective-permute-start(bf16[128,32,128]{2,1,0:T(8,128)(2,1)} %collective-permute-done.1.down_ref.refs_2_), channel_id=1, source_target_pairs={{0,16},{16,0},{1,17},{17,1},{2,18},{18,2},{3,19},{19,3},{4,20},{20... | collective-permute-start | bytes 3145736 | tf_op jit(solution)/shard_map/ppermute | solution.py:290
  102.5 8.4 %collective-permute-start.7 = (bf16[40,32,128]{2,1,0:T(8,128)(2,1)S(1)}, bf16[40,32,128]{2,1,0:T(8,128)(2,1)S(1)}, u32[]{:S(2)}, u32[]{:S(2)}) collective-permute-start(bf16[40,32,128]{2,1,0:T(8,128)(2,1)S(1)} %slice.6), channel_id=1, source_target_pairs={{0,32},{32,64},{64,96},{96,0},{1,33},{33,65},{65,97},{97,1},{2,34}... | collective-permute-start | bytes 983048 | tf_op jit(solution)/shard_map/ppermute | solution.py:278
  103.6 12.5 %collective-permute-start.9 = (bf16[144,32,128]{2,1,0:T(8,128)(2,1)}, bf16[144,32,128]{2,1,0:T(8,128)(2,1)S(1)}, u32[]{:S(2)}, u32[]{:S(2)}) collective-permute-start(bf16[144,32,128]{2,1,0:T(8,128)(2,1)} %collective-permute-done.2.refs_3_), channel_id=1, source_target_pairs={{0,16},{16,0},{1,17},{17,1},{2,18},{18,2},{3,19},{19,3},{4,20},{20... | collective-permute-start | bytes 3538952 | tf_op jit(solution)/shard_map/ppermute | solution.py:290
  103.6 12.5 %collective-permute-start.10 = (bf16[144,32,128]{2,1,0:T(8,128)(2,1)}, bf16[144,32,128]{2,1,0:T(8,128)(2,1)S(1)}, u32[]{:S(2)}, u32[]{:S(2)}) collective-permute-start(bf16[144,32,128]{2,1,0:T(8,128)(2,1)} %collective-permute-done.3.refs_4_), channel_id=1, source_target_pairs={{0,16},{16,0},{1,17},{17,1},{2,18},{18,2},{3,19},{19,3},{4,20},{20... | collective-permute-start | bytes 3538952 | tf_op jit(solution)/shard_map/ppermute | solution.py:290
  104.1 9.6 %collective-permute-start.8 = (bf16[40,32,128]{2,1,0:T(8,128)(2,1)S(1)}, bf16[40,32,128]{2,1,0:T(8,128)(2,1)S(1)}, u32[]{:S(2)}, u32[]{:S(2)}) collective-permute-start(bf16[40,32,128]{2,1,0:T(8,128)(2,1)S(1)} %slice.7), channel_id=1, source_target_pairs={{0,96},{32,0},{64,32},{96,64},{1,97},{33,1},{65,33},{97,65},{2,98}... | collective-permute-start | bytes 983048 | tf_op jit(solution)/shard_map/ppermute | solution.py:282
  127.2 18.4 %collective-permute-start.13 = (s16[4,544,128]{2,1,0:T(8,128)(2,1)S(1)}, s16[4,544,128]{2,1,0:T(8,128)(2,1)S(1)}, u32[]{:S(2)}, u32[]{:S(2)}) collective-permute-start(s16[4,544,128]{2,1,0:T(8,128)(2,1)S(1)} %get-tuple-element.125), channel_id=1, source_target_pairs={{0,4},{4,8},{8,12},{12,0},{1,5},{5,9},{9,13},{13,1},{2,6},{6,10},{... | collective-permute-start | bytes 1671176 | tf_op jit(solution)/shard_map/ppermute | solution.py:278
  127.8 17.8 %collective-permute-start.14 = (s16[4,544,128]{2,1,0:T(8,128)(2,1)S(1)}, s16[4,544,128]{2,1,0:T(8,128)(2,1)S(1)}, u32[]{:S(2)}, u32[]{:S(2)}) collective-permute-start(s16[4,544,128]{2,1,0:T(8,128)(2,1)S(1)} %get-tuple-element.126), channel_id=1, source_target_pairs={{0,12},{4,0},{8,4},{12,8},{1,13},{5,1},{9,5},{13,9},{2,14},{6,2},{... | collective-permute-start | bytes 1671176 | tf_op jit(solution)/shard_map/ppermute | solution.py:282
  129.3 16.3 %collective-permute-start.15 = (s16[4,544,128]{2,1,0:T(8,128)(2,1)S(1)}, s16[4,544,128]{2,1,0:T(8,128)(2,1)S(1)}, u32[]{:S(2)}, u32[]{:S(2)}) collective-permute-start(s16[4,544,128]{2,1,0:T(8,128)(2,1)S(1)} %get-tuple-element.129), channel_id=1, source_target_pairs={{0,1},{1,2},{2,3},{3,0},{4,5},{5,6},{6,7},{7,4},{8,9},{9,10},{10,1... | collective-permute-start | bytes 1671176 | tf_op jit(solution)/shard_map/ppermute | solution.py:278
  129.3 16.3 %collective-permute-start.16 = (s16[4,544,128]{2,1,0:T(8,128)(2,1)S(1)}, s16[4,544,128]{2,1,0:T(8,128)(2,1)S(1)}, u32[]{:S(2)}, u32[]{:S(2)}) collective-permute-start(s16[4,544,128]{2,1,0:T(8,128)(2,1)S(1)} %get-tuple-element.130), channel_id=1, source_target_pairs={{0,3},{1,0},{2,1},{3,2},{4,7},{5,4},{6,5},{7,6},{8,11},{9,8},{10,9... | collective-permute-start | bytes 1671176 | tf_op jit(solution)/shard_map/ppermute | solution.py:282
  148.7 25.6 %collective-permute-start.17 = (s16[2,4,544,128]{3,2,1,0:T(8,128)(2,1)S(1)}, s16[2,4,544,128]{3,2,1,0:T(8,128)(2,1)S(1)}, u32[]{:S(2)}, u32[]{:S(2)}) collective-permute-start(s16[2,4,544,128]{3,2,1,0:T(8,128)(2,1)S(1)} %get-tuple-element.131), channel_id=1, source_target_pairs={{0,4},{4,8},{8,12},{12,0},{1,5},{5,9},{9,13},{13,1},{2,6},{6,10},{... | collective-permute-start | bytes 3342344 | tf_op jit(solution)/shard_map/ppermute | solution.py:278
  150.5 26.4 %collective-permute-start.18 = (s16[2,4,544,128]{3,2,1,0:T(8,128)(2,1)S(1)}, s16[2,4,544,128]{3,2,1,0:T(8,128)(2,1)S(1)}, u32[]{:S(2)}, u32[]{:S(2)}) collective-permute-start(s16[2,4,544,128]{3,2,1,0:T(8,128)(2,1)S(1)} %get-tuple-element.132), channel_id=1, source_target_pairs={{0,12},{4,0},{8,4},{12,8},{1,13},{5,1},{9,5},{13,9},{2,14},{6,2},{... | collective-permute-start | bytes 3342344 | tf_op jit(solution)/shard_map/ppermute | solution.py:282
  150.8 26.1 %collective-permute-start.19 = (s16[2,4,544,128]{3,2,1,0:T(8,128)(2,1)S(1)}, s16[2,4,544,128]{3,2,1,0:T(8,128)(2,1)S(1)}, u32[]{:S(2)}, u32[]{:S(2)}) collective-permute-start(s16[2,4,544,128]{3,2,1,0:T(8,128)(2,1)S(1)} %get-tuple-element.133), channel_id=1, source_target_pairs={{0,1},{1,2},{2,3},{3,0},{4,5},{5,6},{6,7},{7,4},{8,9},{9,10},{10,1... | collective-permute-start | bytes 3342344 | tf_op jit(solution)/shard_map/ppermute | solution.py:278
  150.9 26.0 %collective-permute-start.20 = (s16[2,4,544,128]{3,2,1,0:T(8,128)(2,1)S(1)}, s16[2,4,544,128]{3,2,1,0:T(8,128)(2,1)S(1)}, u32[]{:S(2)}, u32[]{:S(2)}) collective-permute-start(s16[2,4,544,128]{3,2,1,0:T(8,128)(2,1)S(1)} %get-tuple-element.134), channel_id=1, source_target_pairs={{0,3},{1,0},{2,1},{3,2},{4,7},{5,4},{6,5},{7,6},{8,11},{9,8},{10,9... | collective-permute-start | bytes 3342344 | tf_op jit(solution)/shard_map/ppermute | solution.py:282
  193.7 7.8 %collective-permute-start.25 = (s16[2,544,128]{2,1,0:T(8,128)(2,1)S(1)}, s16[2,544,128]{2,1,0:T(8,128)(2,1)S(1)}, u32[]{:S(2)}, u32[]{:S(2)}) collective-permute-start(s16[2,544,128]{2,1,0:T(8,128)(2,1)S(1)} %get-tuple-element.144), channel_id=1, source_target_pairs={{0,1},{1,2},{2,3},{3,0},{4,5},{5,6},{6,7},{7,4},{8,9},{9,10},{10,1... | collective-permute-start | bytes 835592 | tf_op jit(solution)/shard_map/ppermute | solution.py:278
  193.8 7.7 %collective-permute-start.26 = (s16[2,544,128]{2,1,0:T(8,128)(2,1)S(1)}, s16[2,544,128]{2,1,0:T(8,128)(2,1)S(1)}, u32[]{:S(2)}, u32[]{:S(2)}) collective-permute-start(s16[2,544,128]{2,1,0:T(8,128)(2,1)S(1)} %get-tuple-element.145), channel_id=1, source_target_pairs={{0,3},{1,0},{2,1},{3,2},{4,7},{5,4},{6,5},{7,6},{8,11},{9,8},{10,9... | collective-permute-start | bytes 835592 | tf_op jit(solution)/shard_map/ppermute | solution.py:282
  197.0 7.8 %collective-permute-start.28 = (s16[2,544,128]{2,1,0:T(8,128)(2,1)S(1)}, s16[2,544,128]{2,1,0:T(8,128)(2,1)S(1)}, u32[]{:S(2)}, u32[]{:S(2)}) collective-permute-start(s16[2,544,128]{2,1,0:T(8,128)(2,1)S(1)} %get-tuple-element.147), channel_id=1, source_target_pairs={{0,12},{4,0},{8,4},{12,8},{1,13},{5,1},{9,5},{13,9},{2,14},{6,2},{... | collective-permute-start | bytes 835592 | tf_op jit(solution)/shard_map/ppermute | solution.py:282
  (17 other events, 114.1 us)

commit v6 on v5

--- a/solution.py
+++ b/solution.py
@@ -29,7 +29,8 @@
 POOL = 2 * CORE + THIRD
 PARTS = 14
 HALF = 512
-PACKED = HALF + HALF // 16
+SHARE = 32
+PACKED = HALF + HALF // SHARE
 VMEM_GRANT = 10 * 1024 * 1024
 
 
@@ -103,13 +104,34 @@
     copies = [
         pltpu.make_async_copy(up_ref.at[pl.ds(0, half)], up_out.at[pl.ds(0, half)], sems.at[0]),
         pltpu.make_async_copy(down_ref.at[pl.ds(half, half)], down_out.at[pl.ds(0, half)], sems.at[1]),
-        pltpu.make_async_copy(some_ref, up_out.at[pl.ds(half, EXTRA)], sems.at[2]),
-        pltpu.make_async_copy(some_ref, down_out.at[pl.ds(half, EXTRA)], sems.at[3]),
     ]
     for copy in copies:
         copy.start()
+
+    def body(i, carry):
+        tiles = [some_ref[i * 16 + k] for k in range(16)]
+        for k in range(16):
+            up_out[half + i * 16 + k] = tiles[k]
+            down_out[half + i * 16 + k] = tiles[k]
+        return carry
+
+    lax.fori_loop(0, EXTRA // 16, body, 0)
     for copy in copies:
         copy.wait()
+
+
+def tail_kernel(some_ref, up_ref, down_ref, out_ref):
+    size = EXTRA // 2
+
+    def body(i, carry):
+        sources = [(some_ref, size), (up_ref, 0), (down_ref, 0)]
+        tiles = [[ref[base + i * 8 + k] for k in range(8)] for ref, base in sources]
+        for part in range(3):
+            for k in range(8):
+                out_ref[part * size + i * 8 + k] = tiles[part][k]
+        return carry
+
+    lax.fori_loop(0, size // 8, body, 0)
 
 
 def no_spill_kernel(tiles_ref, out_ref, sem):
@@ -152,18 +174,18 @@
 
 
 def pack(out_ref, value):
-    value = value.reshape(HALF // 16, 16, 128)
+    value = value.reshape(HALF // SHARE, SHARE, 128)
     top = jnp.maximum(jnp.max(jnp.abs(value), axis=1), 1e-30)
     exponent = jnp.ceil(jnp.log2(top * 1.0001))
     scaled = jnp.round(value * jnp.exp2(15.0 - exponent)[:, None, :]).reshape(HALF, 128)
     out_ref[pl.ds(0, HALF)] = scaled.astype(jnp.int32).astype(jnp.int16)
-    out_ref[pl.ds(HALF, HALF // 16)] = exponent.astype(jnp.int32).astype(jnp.int16)
+    out_ref[pl.ds(HALF, HALF // SHARE)] = exponent.astype(jnp.int32).astype(jnp.int16)
 
 
 def unpack(ref):
     mantissa = ref[pl.ds(0, HALF)].astype(jnp.int32).astype(jnp.float32)
-    exponent = ref[pl.ds(HALF, HALF // 16)].astype(jnp.int32).astype(jnp.float32)
-    value = mantissa.reshape(HALF // 16, 16, 128) * jnp.exp2(exponent - 15.0)[:, None, :]
+    exponent = ref[pl.ds(HALF, HALF // SHARE)].astype(jnp.int32).astype(jnp.float32)
+    value = mantissa.reshape(HALF // SHARE, SHARE, 128) * jnp.exp2(exponent - 15.0)[:, None, :]
     return value.reshape(HALF, 128)
 
 
@@ -437,7 +459,7 @@
         in_specs=[vmem] * 3,
         out_specs=[vmem] * 2,
         out_shape=[jax.ShapeDtypeStruct((half + EXTRA, SUB, 128), jnp.bfloat16)] * 2,
-        scratch_shapes=[pltpu.SemaphoreType.DMA((4,))],
+        scratch_shapes=[pltpu.SemaphoreType.DMA((2,))],
         compiler_params=pltpu.CompilerParams(vmem_limit_bytes=VMEM_GRANT),
         name="join",
     )(up, down, some)
@@ -493,7 +515,9 @@
     tails = from_up[half : half + EXTRA // 2], from_down[half + EXTRA // 2 :]
     tails, from_up, from_down = lax.optimization_barrier((tails, from_up, from_down))
     tail_up, tail_down = ahead("y", tails[0]), behind("y", tails[1])
-    parts = [first, up, down, from_up, from_down, some, jnp.concatenate([tail_up, tail_down])]
+    tail = jax.ShapeDtypeStruct((3 * EXTRA // 2, SUB, 128), jnp.bfloat16)
+    (tail,) = whole_call(tail_kernel, "tail", [tail], some, tail_up, tail_down)
+    parts = [first, up, down, from_up, from_down, some[: EXTRA // 2], tail]
     tiles = collect_call(misc, parts + swapped + swap(parts[3:]), third)
 
     scalars = (tile_index, misc)

time: 214 us -> 208 us (0.972)
  waiting for transfers between devices: 78 us -> 74.8 us
  Pallas kernels: 56.7 us -> 53.8 us
    ppermute x11, waiting for transfers between devices: 10.4 us -> 7.82 us  [behind(): return lax.ppermute(value, axis, [(i, (i + 3) % 4) for i in range(4)])]
    pallas_call x4 -> x5, Pallas kernels: 8.73 us -> 7.14 us  [whole_call(): pl.pallas_call(body, in_specs=[pl.BlockSpec(memory_space=pltpu.SMEM)] * l...]
    unnamed x22 -> x23, local copies, waits for them, and re-layouts: 8.14 us -> 8.11 us
  transfers between devices with their start and end apart: 31 -> 31, of which waited for: 14 -> 12; matrix products, arithmetic and copies ran while one was open for 3% -> 3% of each run, Pallas kernels for 13% -> 13%
where the time goes in v6:
time: 208 us; the launch traced here: 207 us
  waiting for transfers between devices  74.8 us (36%)
  Pallas kernels  53.8 us (26%)
  starting transfers between devices  48.1 us (23%)
  between operations  14.5 us (7%)
  local copies, waits for them, and re-layouts  10.5 us (5%)
  other arithmetic  3.79 us (2%)
    ppermute x11, waiting for transfers between devices, ahead(): return lax.ppermute(value, axis, [(i, (i + 1) % 4) for i in range(4)])  34.7 us
    all_to_all x2, waiting for transfers between devices, send(): lax.all_to_all(part, ('x', 'z'), split_axis=0, concat_axis=0, tiled=True)  29.9 us
    pallas_call x3, Pallas kernels, product_call(): pl.pallas_call(functools.partial(product_kernel, hops), grid_spec=pltpu.P...  25 us
    ppermute x11, starting transfers between devices, behind(): return lax.ppermute(value, axis, [(i, (i + 3) % 4) for i in range(4)])  23.9 us
    all_to_all x2, starting transfers between devices, send(): lax.all_to_all(part, ('x', 'z'), split_axis=0, concat_axis=0, tiled=True)  14.4 us
    unnamed x23, local copies, waits for them, and re-layouts  8.11 us
    ppermute x11, starting transfers between devices, ahead(): return lax.ppermute(value, axis, [(i, (i + 1) % 4) for i in range(4)])  7.96 us
    ppermute x11, waiting for transfers between devices, behind(): return lax.ppermute(value, axis, [(i, (i + 3) % 4) for i in range(4)])  7.82 us
  transfers between devices with their start and end apart: 31, of which 12 were waited for; matrix products, arithmetic and copies ran while one was open for 3% of the time, Pallas kernels for 13%

profile of v6, /device:TPU:6, one launch (start us, length us, event | category | flops | bytes accessed | tf_op | source)
XLA Modules:
  0.0 207.4 jit_solution(17141718879564389559)
XLA Ops:
  9.8 4.6 %fill.1 = (bf16[128,32,128]{2,1,0:T(8,128)(2,1)S(1)}, bf16[192,32,128]{2,1,0:T(8,128)(2,1)S(1)}) custom-call(s32[16,128]{1,0:T(8,128)S(1)} %route.1.index_ref, bf16[320,32,128]{2,1,0:T(8,128)(2,1)S(1)} %bitcast.19), custom_call_target="tpu_custom_call" | custom-call | tf_op jit(solution)/shard_map/fill/pallas_call | solution.py:403
  16.6 8.3 %all-to-all-start = ((bf16[16,8,32,128]{3,2,1,0:T(8,128)(2,1)}), bf16[16,8,32,128]{3,2,1,0:T(8,128)(2,1)S(1)}, u32[]{:S(2)}, u32[]{:S(2)}) async-start(bf16[16,8,32,128]{3,2,1,0:T(8,128)(2,1)} %bitcast.26), calls=%async_computation | async-start | bytes 2097152 | tf_op jit(solution)/shard_map/all_to_all | solution.py:423
  24.9 15.2 %all-to-all-done = bf16[16,8,32,128]{3,2,1,0:T(8,128)(2,1)S(1)} async-done(((bf16[16,8,32,128]{3,2,1,0:T(8,128)(2,1)}), bf16[16,8,32,128]{3,2,1,0:T(8,128)(2,1)S(1)}, u32[]{:S(2)}, u32[]{:S(2)}) %all-to-all-start) | async-done | bytes 1048608 | tf_op jit(solution)/shard_map/all_to_all | solution.py:423
  40.1 3.0 %collective-permute-start.1 = (bf16[128,32,128]{2,1,0:T(8,128)(2,1)S(1)}, bf16[128,32,128]{2,1,0:T(8,128)(2,1)}, u32[]{:S(2)}, u32[]{:S(2)}) collective-permute-start(bf16[128,32,128]{2,1,0:T(8,128)(2,1)S(1)} %bitcast.21), channel_id=1, source_target_pairs={{0,96},{32,0},{64,32},{96,64},{1,97},{33,1},{65,33},{97,65},{2,98}... | collective-permute-start | bytes 3145736 | tf_op jit(solution)/shard_map/ppermute | solution.py:304
  43.1 6.1 %all-to-all-start.1 = ((bf16[16,12,32,128]{3,2,1,0:T(8,128)(2,1)}), bf16[16,12,32,128]{3,2,1,0:T(8,128)(2,1)S(1)}, u32[]{:S(2)}, u32[]{:S(2)}) async-start(bf16[16,12,32,128]{3,2,1,0:T(8,128)(2,1)} %bitcast.25), calls=%async_computation.1 | async-start | bytes 3145728 | tf_op jit(solution)/shard_map/all_to_all | solution.py:423
  53.6 14.7 %all-to-all-done.1 = bf16[16,12,32,128]{3,2,1,0:T(8,128)(2,1)S(1)} async-done(((bf16[16,12,32,128]{3,2,1,0:T(8,128)(2,1)}), bf16[16,12,32,128]{3,2,1,0:T(8,128)(2,1)S(1)}, u32[]{:S(2)}, u32[]{:S(2)}) %all-to-all-start.1) | async-done | bytes 1572896 | tf_op jit(solution)/shard_map/all_to_all | solution.py:423
  69.9 3.5 %join.1 = (bf16[144,32,128]{2,1,0:T(8,128)(2,1)}, bf16[144,32,128]{2,1,0:T(8,128)(2,1)}) custom-call(bf16[128,32,128]{2,1,0:T(8,128)(2,1)} %collective-permute-done.up_ref.refs_1_, bf16[128,32,128]{2,1,0:T(8,128)(2,1)} %collective-permute-done.1.down_ref.refs_2_, bf16[80,32,128]{2,1,0:T(8,128)(2,1)S(1)} %get-tuple-element.90.some_ref), custom_call_target="tpu_custom_call" | custom-call | tf_op jit(solution)/shard_map/join/pallas_call | solution.py:457
  73.7 2.9 %collective-permute-start.3 = (bf16[144,32,128]{2,1,0:T(8,128)(2,1)}, bf16[144,32,128]{2,1,0:T(8,128)(2,1)}, u32[]{:S(2)}, u32[]{:S(2)}) collective-permute-start(bf16[144,32,128]{2,1,0:T(8,128)(2,1)} %get-tuple-element.93), channel_id=1, source_target_pairs={{0,96},{32,0},{64,32},{96,64},{1,97},{33,1},{65,33},{97,65},{2,98}... | collective-permute-start | bytes 3538952 | tf_op jit(solution)/shard_map/ppermute | solution.py:304
  79.6 5.7 %prep.1 = (bf16[1024,1024]{1,0:T(8,128)(2,1)S(1)}, bf16[1024,1024]{1,0:T(8,128)(2,1)S(1)}) custom-call(s32[16,32]{1,0:T(8,128)S(1)} %copy-done.8, bf16[1024,2048]{1,0:T(8,128)(2,1)S(1)} %copy-done.2), custom_call_target="tpu_custom_call" | custom-call | tf_op jit(solution)/shard_map/prep/pallas_call | solution.py:472
  90.5 9.7 %collective-permute-done.2.refs_3_ = bf16[144,32,128]{2,1,0:T(8,128)(2,1)} collective-permute-done((bf16[144,32,128]{2,1,0:T(8,128)(2,1)}, bf16[144,32,128]{2,1,0:T(8,128)(2,1)}, u32[]{:S(2)}, u32[]{:S(2)}) %collective-permute-start.2) | collective-permute-done | bytes 1179680 | tf_op jit(solution)/shard_map/ppermute | solution.py:300
  106.0 4.5 %collective-permute-done.7.up_ref = bf16[40,32,128]{2,1,0:T(8,128)(2,1)S(1)} collective-permute-done((bf16[40,32,128]{2,1,0:T(8,128)(2,1)S(1)}, bf16[40,32,128]{2,1,0:T(8,128)(2,1)S(1)}, u32[]{:S(2)}, u32[]{:S(2)}) %collective-permute-start.7) | collective-permute-done | bytes 327712 | tf_op jit(solution)/shard_map/ppermute | solution.py:300
  113.8 4.0 %collect.1.tiles = bf16[2561,32,128]{2,1,0:T(8,128)(2,1)S(1)} custom-call(s32[3]{0:T(128)S(1)} %pad_add_fusion.misc_ref, bf16[128,32,128]{2,1,0:T(8,128)(2,1)S(1)} %bitcast.24, bf16[128,32,128]{2,1,0:T(8,128)(2,1)} %collective-permute-done.up_ref.refs_1_, bf16[128,32,128]{2,1,0:T(8,128)(2,1)} %collective-permute-done.1.down_ref.refs_2_, ...), custom_call_target="tpu_custom_call" | custom-call | bytes 20971520 | tf_op jit(solution)/shard_map/collect/pallas_call | solution.py:214
  117.9 6.6 %far.1 = (s16[4,528,128]{2,1,0:T(8,128)(2,1)S(1)}, s16[4,528,128]{2,1,0:T(8,128)(2,1)S(1)}, s16[4,528,128]{2,1,0:T(8,128)(2,1)S(1)}, s16[4,528,128]{2,1,0:T(8,12...) custom-call(s32[2048]{0:T(1024)S(1)} %select_select_fusion.index_ref, ...), custom_call_target="tpu_custom_call", output_to_operand_aliasing={{4}: (2, {}), {5}: (3, {}), {6}: (4, {})} | custom-call | flops 4294967296 | bytes 20971520 | tf_op jit(solution)/shard_map/far/pallas_call | solution.py:279
  126.6 3.2 %collective-permute-start.16 = (s16[4,528,128]{2,1,0:T(8,128)(2,1)S(1)}, s16[4,528,128]{2,1,0:T(8,128)(2,1)S(1)}, u32[]{:S(2)}, u32[]{:S(2)}) collective-permute-start(s16[4,528,128]{2,1,0:T(8,128)(2,1)S(1)} %get-tuple-element.130), channel_id=1, source_target_pairs={{0,3},{1,0},{2,1},{3,2},{4,7},{5,4},{6,5},{7,6},{8,11},{9,8},{10,9... | collective-permute-start | bytes 1622024 | tf_op jit(solution)/shard_map/ppermute | solution.py:304
  129.8 12.3 %near.1 = (s16[2,4,528,128]{3,2,1,0:T(8,128)(2,1)S(1)}, s16[2,4,528,128]{3,2,1,0:T(8,128)(2,1)S(1)}, s16[2,4,528,128]{3,2,1,0:T(8,128)(2,1)S(1)}, s16[2,4,528,12...) custom-call(s32[2048]{0:T(1024)S(1)} %select_select_fusion.index_ref, ...), custom_call_target="tpu_custom_call", output_to_operand_aliasing={{4}: (2, {}), {5}: (3, {}), {6}: (4, {})} | custom-call | flops 8589934592 | bytes 20971520 | tf_op jit(solution)/shard_map/near/pallas_call | solution.py:279
  147.1 2.8 %collective-permute-start.20 = (s16[2,4,528,128]{3,2,1,0:T(8,128)(2,1)S(1)}, s16[2,4,528,128]{3,2,1,0:T(8,128)(2,1)S(1)}, u32[]{:S(2)}, u32[]{:S(2)}) collective-permute-start(s16[2,4,528,128]{3,2,1,0:T(8,128)(2,1)S(1)} %get-tuple-element.134), channel_id=1, source_target_pairs={{0,3},{1,0},{2,1},{3,2},{4,7},{5,4},{6,5},{7,6},{8,11},{9,8},{10,9... | collective-permute-start | bytes 3244040 | tf_op jit(solution)/shard_map/ppermute | solution.py:304
  149.8 6.0 %own.1 = (f32[4,1024,128]{2,1,0:T(8,128)S(1)}, f32[4,1024,128]{2,1,0:T(8,128)S(1)}) custom-call(s32[2048]{0:T(1024)S(1)} %select_select_fusion.index_ref, s32[3]{0:T(128)S(1)} %pad_add_fusion.misc_ref, bf16[1024,1024]{1,0:T(8,128)(2,1)S(1)} %get-tuple-element.118.even_ref, bf16[1024,1024]{1,0:T(8,128)(2,1)S(1)} %get-tuple-element.119.odd_ref, ...), custom_call_target="tpu_custom_call" | custom-call | flops 4294967296 | bytes 20971520 | tf_op jit(solution)/shard_map/own/pallas_call | solution.py:279
  155.9 13.5 %collective-permute-done.17.refs_0_ = s16[2,4,528,128]{3,2,1,0:T(8,128)(2,1)S(1)} collective-permute-done((s16[2,4,528,128]{3,2,1,0:T(8,128)(2,1)S(1)}, s16[2,4,528,128]{3,2,1,0:T(8,128)(2,1)S(1)}, u32[]{:S(2)}, u32[]{:S(2)}) %collective-permute-start.17) | collective-permute-done | bytes 1081376 | tf_op jit(solution)/shard_map/ppermute | solution.py:300
  169.3 2.9 %collective-permute-done.18.refs_1_ = s16[2,4,528,128]{3,2,1,0:T(8,128)(2,1)S(1)} collective-permute-done((s16[2,4,528,128]{3,2,1,0:T(8,128)(2,1)S(1)}, s16[2,4,528,128]{3,2,1,0:T(8,128)(2,1)S(1)}, u32[]{:S(2)}, u32[]{:S(2)}) %collective-permute-start.18) | collective-permute-done | bytes 1081376 | tf_op jit(solution)/shard_map/ppermute | solution.py:304
  172.3 2.8 %middle.1 = (s16[1,528,128]{2,1,0:T(8,128)(2,1)S(1)}, s16[1,528,128]{2,1,0:T(8,128)(2,1)S(1)}, s16[2,528,128]{2,1,0:T(8,128)(2,1)S(1)}, s16[2,528,128]{2,1,0:T(8...) custom-call(s32[3]{0:T(128)S(1)} %pad_add_fusion.misc_ref, ...), custom_call_target="tpu_custom_call" | custom-call | flops 111902720 | bytes 11190272 | tf_op jit(solution)/shard_map/middle/pallas_call | solution.py:342
  175.2 3.2 %collective-permute-start.22 = (s16[1,528,128]{2,1,0:T(8,128)(2,1)S(1)}, s16[1,528,128]{2,1,0:T(8,128)(2,1)S(1)}, u32[]{:S(2)}, u32[]{:S(2)}) collective-permute-start(s16[1,528,128]{2,1,0:T(8,128)(2,1)S(1)} %get-tuple-element.139), channel_id=1, source_target_pairs={{0,3},{1,0},{2,1},{3,2},{4,7},{5,4},{6,5},{7,6},{8,11},{9,8},{10,9... | collective-permute-start | bytes 405512 | tf_op jit(solution)/shard_map/ppermute | solution.py:304
  178.4 3.0 %collective-permute-start.23 = (s16[1,528,128]{2,1,0:T(8,128)(2,1)S(1)}, s16[1,528,128]{2,1,0:T(8,128)(2,1)S(1)}, u32[]{:S(2)}, u32[]{:S(2)}) collective-permute-start(s16[1,528,128]{2,1,0:T(8,128)(2,1)S(1)} %get-tuple-element.142), channel_id=1, source_target_pairs={{0,4},{4,8},{8,12},{12,0},{1,5},{5,9},{9,13},{13,1},{2,6},{6,10},{... | collective-permute-start | bytes 405512 | tf_op jit(solution)/shard_map/ppermute | solution.py:300
  183.9 3.7 %collective-permute-done.24.refs_7_ = s16[1,528,128]{2,1,0:T(8,128)(2,1)S(1)} collective-permute-done((s16[1,528,128]{2,1,0:T(8,128)(2,1)S(1)}, s16[1,528,128]{2,1,0:T(8,128)(2,1)S(1)}, u32[]{:S(2)}, u32[]{:S(2)}) %collective-permute-start.24) | collective-permute-done | bytes 135200 | tf_op jit(solution)/shard_map/ppermute | solution.py:304
  188.3 3.2 %collective-permute-start.26 = (s16[2,528,128]{2,1,0:T(8,128)(2,1)S(1)}, s16[2,528,128]{2,1,0:T(8,128)(2,1)S(1)}, u32[]{:S(2)}, u32[]{:S(2)}) collective-permute-start(s16[2,528,128]{2,1,0:T(8,128)(2,1)S(1)} %get-tuple-element.145), channel_id=1, source_target_pairs={{0,3},{1,0},{2,1},{3,2},{4,7},{5,4},{6,5},{7,6},{8,11},{9,8},{10,9... | collective-permute-start | bytes 811016 | tf_op jit(solution)/shard_map/ppermute | solution.py:304
  (106 shorter events, 48.6 us)
Async XLA Ops:
  16.6 23.5 %all-to-all-start = ((bf16[16,8,32,128]{3,2,1,0:T(8,128)(2,1)}), bf16[16,8,32,128]{3,2,1,0:T(8,128)(2,1)S(1)}, u32[]{:S(2)}, u32[]{:S(2)}) async-start(bf16[16,8,32,128]{3,2,1,0:T(8,128)(2,1)} %bitcast.26), calls=%async_computation | async-start | bytes 2097152 | tf_op jit(solution)/shard_map/all_to_all | solution.py:423
  40.1 29.8 %collective-permute-start.1 = (bf16[128,32,128]{2,1,0:T(8,128)(2,1)S(1)}, bf16[128,32,128]{2,1,0:T(8,128)(2,1)}, u32[]{:S(2)}, u32[]{:S(2)}) collective-permute-start(bf16[128,32,128]{2,1,0:T(8,128)(2,1)S(1)} %bitcast.21), channel_id=1, source_target_pairs={{0,96},{32,0},{64,32},{96,64},{1,97},{33,1},{65,33},{97,65},{2,98}... | collective-permute-start | bytes 3145736 | tf_op jit(solution)/shard_map/ppermute | solution.py:304
  43.1 26.8 %collective-permute-start = (bf16[128,32,128]{2,1,0:T(8,128)(2,1)S(1)}, bf16[128,32,128]{2,1,0:T(8,128)(2,1)}, u32[]{:S(2)}, u32[]{:S(2)}) collective-permute-start(bf16[128,32,128]{2,1,0:T(8,128)(2,1)S(1)} %bitcast.22), channel_id=1, source_target_pairs={{0,32},{32,64},{64,96},{96,0},{1,33},{33,65},{65,97},{97,1},{2,34}... | collective-permute-start | bytes 3145736 | tf_op jit(solution)/shard_map/ppermute | solution.py:300
  43.1 25.2 %all-to-all-start.1 = ((bf16[16,12,32,128]{3,2,1,0:T(8,128)(2,1)}), bf16[16,12,32,128]{3,2,1,0:T(8,128)(2,1)S(1)}, u32[]{:S(2)}, u32[]{:S(2)}) async-start(bf16[16,12,32,128]{3,2,1,0:T(8,128)(2,1)} %bitcast.25), calls=%async_computation.1 | async-start | bytes 3145728 | tf_op jit(solution)/shard_map/all_to_all | solution.py:423
  73.4 26.8 %collective-permute-start.2 = (bf16[144,32,128]{2,1,0:T(8,128)(2,1)}, bf16[144,32,128]{2,1,0:T(8,128)(2,1)}, u32[]{:S(2)}, u32[]{:S(2)}) collective-permute-start(bf16[144,32,128]{2,1,0:T(8,128)(2,1)} %get-tuple-element.92), channel_id=1, source_target_pairs={{0,32},{32,64},{64,96},{96,0},{1,33},{33,65},{65,97},{97,1},{2,34}... | collective-permute-start | bytes 3538952 | tf_op jit(solution)/shard_map/ppermute | solution.py:300
  73.7 26.5 %collective-permute-start.3 = (bf16[144,32,128]{2,1,0:T(8,128)(2,1)}, bf16[144,32,128]{2,1,0:T(8,128)(2,1)}, u32[]{:S(2)}, u32[]{:S(2)}) collective-permute-start(bf16[144,32,128]{2,1,0:T(8,128)(2,1)} %get-tuple-element.93), channel_id=1, source_target_pairs={{0,96},{32,0},{64,32},{96,64},{1,97},{33,1},{65,33},{97,65},{2,98}... | collective-permute-start | bytes 3538952 | tf_op jit(solution)/shard_map/ppermute | solution.py:304
  76.7 13.8 %collective-permute-start.4 = (bf16[128,32,128]{2,1,0:T(8,128)(2,1)S(1)}, bf16[128,32,128]{2,1,0:T(8,128)(2,1)}, u32[]{:S(2)}, u32[]{:S(2)}) collective-permute-start(bf16[128,32,128]{2,1,0:T(8,128)(2,1)S(1)} %bitcast.23), channel_id=1, source_target_pairs={{0,16},{16,0},{1,17},{17,1},{2,18},{18,2},{3,19},{19,3},{4,20},{20... | collective-permute-start | bytes 3145736 | tf_op jit(solution)/shard_map/ppermute | solution.py:312
  76.7 13.8 %collective-permute-start.5 = (bf16[128,32,128]{2,1,0:T(8,128)(2,1)}, bf16[128,32,128]{2,1,0:T(8,128)(2,1)}, u32[]{:S(2)}, u32[]{:S(2)}) collective-permute-start(bf16[128,32,128]{2,1,0:T(8,128)(2,1)} %collective-permute-done.up_ref.refs_1_), channel_id=1, source_target_pairs={{0,16},{16,0},{1,17},{17,1},{2,18},{18,2},{3,19},{19,3},{4,20},{20... | collective-permute-start | bytes 3145736 | tf_op jit(solution)/shard_map/ppermute | solution.py:312
  77.2 13.3 %collective-permute-start.6 = (bf16[128,32,128]{2,1,0:T(8,128)(2,1)}, bf16[128,32,128]{2,1,0:T(8,128)(2,1)}, u32[]{:S(2)}, u32[]{:S(2)}) collective-permute-start(bf16[128,32,128]{2,1,0:T(8,128)(2,1)} %collective-permute-done.1.down_ref.refs_2_), channel_id=1, source_target_pairs={{0,16},{16,0},{1,17},{17,1},{2,18},{18,2},{3,19},{19,3},{4,20},{20... | collective-permute-start | bytes 3145736 | tf_op jit(solution)/shard_map/ppermute | solution.py:312
  102.2 8.4 %collective-permute-start.7 = (bf16[40,32,128]{2,1,0:T(8,128)(2,1)S(1)}, bf16[40,32,128]{2,1,0:T(8,128)(2,1)S(1)}, u32[]{:S(2)}, u32[]{:S(2)}) collective-permute-start(bf16[40,32,128]{2,1,0:T(8,128)(2,1)S(1)} %slice.9), channel_id=1, source_target_pairs={{0,32},{32,64},{64,96},{96,0},{1,33},{33,65},{65,97},{97,1},{2,34}... | collective-permute-start | bytes 983048 | tf_op jit(solution)/shard_map/ppermute | solution.py:300
  103.3 7.3 %collective-permute-start.8 = (bf16[40,32,128]{2,1,0:T(8,128)(2,1)S(1)}, bf16[40,32,128]{2,1,0:T(8,128)(2,1)S(1)}, u32[]{:S(2)}, u32[]{:S(2)}) collective-permute-start(bf16[40,32,128]{2,1,0:T(8,128)(2,1)S(1)} %slice.10), channel_id=1, source_target_pairs={{0,96},{32,0},{64,32},{96,64},{1,97},{33,1},{65,33},{97,65},{2,98}... | collective-permute-start | bytes 983048 | tf_op jit(solution)/shard_map/ppermute | solution.py:304
  105.5 8.2 %collective-permute-start.9 = (bf16[144,32,128]{2,1,0:T(8,128)(2,1)}, bf16[144,32,128]{2,1,0:T(8,128)(2,1)S(1)}, u32[]{:S(2)}, u32[]{:S(2)}) collective-permute-start(bf16[144,32,128]{2,1,0:T(8,128)(2,1)} %collective-permute-done.2.refs_3_), channel_id=1, source_target_pairs={{0,16},{16,0},{1,17},{17,1},{2,18},{18,2},{3,19},{19,3},{4,20},{20... | collective-permute-start | bytes 3538952 | tf_op jit(solution)/shard_map/ppermute | solution.py:312
  105.5 8.2 %collective-permute-start.10 = (bf16[144,32,128]{2,1,0:T(8,128)(2,1)}, bf16[144,32,128]{2,1,0:T(8,128)(2,1)S(1)}, u32[]{:S(2)}, u32[]{:S(2)}) collective-permute-start(bf16[144,32,128]{2,1,0:T(8,128)(2,1)} %collective-permute-done.3.refs_4_), channel_id=1, source_target_pairs={{0,16},{16,0},{1,17},{17,1},{2,18},{18,2},{3,19},{19,3},{4,20},{20... | collective-permute-start | bytes 3538952 | tf_op jit(solution)/shard_map/ppermute | solution.py:312
  124.5 17.7 %collective-permute-start.13 = (s16[4,528,128]{2,1,0:T(8,128)(2,1)S(1)}, s16[4,528,128]{2,1,0:T(8,128)(2,1)S(1)}, u32[]{:S(2)}, u32[]{:S(2)}) collective-permute-start(s16[4,528,128]{2,1,0:T(8,128)(2,1)S(1)} %get-tuple-element.125), channel_id=1, source_target_pairs={{0,4},{4,8},{8,12},{12,0},{1,5},{5,9},{9,13},{13,1},{2,6},{6,10},{... | collective-permute-start | bytes 1622024 | tf_op jit(solution)/shard_map/ppermute | solution.py:300
  125.4 16.8 %collective-permute-start.14 = (s16[4,528,128]{2,1,0:T(8,128)(2,1)S(1)}, s16[4,528,128]{2,1,0:T(8,128)(2,1)S(1)}, u32[]{:S(2)}, u32[]{:S(2)}) collective-permute-start(s16[4,528,128]{2,1,0:T(8,128)(2,1)S(1)} %get-tuple-element.126), channel_id=1, source_target_pairs={{0,12},{4,0},{8,4},{12,8},{1,13},{5,1},{9,5},{13,9},{2,14},{6,2},{... | collective-permute-start | bytes 1622024 | tf_op jit(solution)/shard_map/ppermute | solution.py:304
  126.6 15.6 %collective-permute-start.15 = (s16[4,528,128]{2,1,0:T(8,128)(2,1)S(1)}, s16[4,528,128]{2,1,0:T(8,128)(2,1)S(1)}, u32[]{:S(2)}, u32[]{:S(2)}) collective-permute-start(s16[4,528,128]{2,1,0:T(8,128)(2,1)S(1)} %get-tuple-element.129), channel_id=1, source_target_pairs={{0,1},{1,2},{2,3},{3,0},{4,5},{5,6},{6,7},{7,4},{8,9},{9,10},{10,1... | collective-permute-start | bytes 1622024 | tf_op jit(solution)/shard_map/ppermute | solution.py:300
  126.6 15.6 %collective-permute-start.16 = (s16[4,528,128]{2,1,0:T(8,128)(2,1)S(1)}, s16[4,528,128]{2,1,0:T(8,128)(2,1)S(1)}, u32[]{:S(2)}, u32[]{:S(2)}) collective-permute-start(s16[4,528,128]{2,1,0:T(8,128)(2,1)S(1)} %get-tuple-element.130), channel_id=1, source_target_pairs={{0,3},{1,0},{2,1},{3,2},{4,7},{5,4},{6,5},{7,6},{8,11},{9,8},{10,9... | collective-permute-start | bytes 1622024 | tf_op jit(solution)/shard_map/ppermute | solution.py:304
  144.5 24.8 %collective-permute-start.17 = (s16[2,4,528,128]{3,2,1,0:T(8,128)(2,1)S(1)}, s16[2,4,528,128]{3,2,1,0:T(8,128)(2,1)S(1)}, u32[]{:S(2)}, u32[]{:S(2)}) collective-permute-start(s16[2,4,528,128]{3,2,1,0:T(8,128)(2,1)S(1)} %get-tuple-element.131), channel_id=1, source_target_pairs={{0,4},{4,8},{8,12},{12,0},{1,5},{5,9},{9,13},{13,1},{2,6},{6,10},{... | collective-permute-start | bytes 3244040 | tf_op jit(solution)/shard_map/ppermute | solution.py:300
  146.6 25.7 %collective-permute-start.18 = (s16[2,4,528,128]{3,2,1,0:T(8,128)(2,1)S(1)}, s16[2,4,528,128]{3,2,1,0:T(8,128)(2,1)S(1)}, u32[]{:S(2)}, u32[]{:S(2)}) collective-permute-start(s16[2,4,528,128]{3,2,1,0:T(8,128)(2,1)S(1)} %get-tuple-element.132), channel_id=1, source_target_pairs={{0,12},{4,0},{8,4},{12,8},{1,13},{5,1},{9,5},{13,9},{2,14},{6,2},{... | collective-permute-start | bytes 3244040 | tf_op jit(solution)/shard_map/ppermute | solution.py:304
  146.6 25.7 %collective-permute-start.19 = (s16[2,4,528,128]{3,2,1,0:T(8,128)(2,1)S(1)}, s16[2,4,528,128]{3,2,1,0:T(8,128)(2,1)S(1)}, u32[]{:S(2)}, u32[]{:S(2)}) collective-permute-start(s16[2,4,528,128]{3,2,1,0:T(8,128)(2,1)S(1)} %get-tuple-element.133), channel_id=1, source_target_pairs={{0,1},{1,2},{2,3},{3,0},{4,5},{5,6},{6,7},{7,4},{8,9},{9,10},{10,1... | collective-permute-start | bytes 3244040 | tf_op jit(solution)/shard_map/ppermute | solution.py:300
  147.1 25.2 %collective-permute-start.20 = (s16[2,4,528,128]{3,2,1,0:T(8,128)(2,1)S(1)}, s16[2,4,528,128]{3,2,1,0:T(8,128)(2,1)S(1)}, u32[]{:S(2)}, u32[]{:S(2)}) collective-permute-start(s16[2,4,528,128]{3,2,1,0:T(8,128)(2,1)S(1)} %get-tuple-element.134), channel_id=1, source_target_pairs={{0,3},{1,0},{2,1},{3,2},{4,7},{5,4},{6,5},{7,6},{8,11},{9,8},{10,9... | collective-permute-start | bytes 3244040 | tf_op jit(solution)/shard_map/ppermute | solution.py:304
  188.2 7.7 %collective-permute-start.25 = (s16[2,528,128]{2,1,0:T(8,128)(2,1)S(1)}, s16[2,528,128]{2,1,0:T(8,128)(2,1)S(1)}, u32[]{:S(2)}, u32[]{:S(2)}) collective-permute-start(s16[2,528,128]{2,1,0:T(8,128)(2,1)S(1)} %get-tuple-element.144), channel_id=1, source_target_pairs={{0,1},{1,2},{2,3},{3,0},{4,5},{5,6},{6,7},{7,4},{8,9},{9,10},{10,1... | collective-permute-start | bytes 811016 | tf_op jit(solution)/shard_map/ppermute | solution.py:300
  188.3 7.7 %collective-permute-start.26 = (s16[2,528,128]{2,1,0:T(8,128)(2,1)S(1)}, s16[2,528,128]{2,1,0:T(8,128)(2,1)S(1)}, u32[]{:S(2)}, u32[]{:S(2)}) collective-permute-start(s16[2,528,128]{2,1,0:T(8,128)(2,1)S(1)} %get-tuple-element.145), channel_id=1, source_target_pairs={{0,3},{1,0},{2,1},{3,2},{4,7},{5,4},{6,5},{7,6},{8,11},{9,8},{10,9... | collective-permute-start | bytes 811016 | tf_op jit(solution)/shard_map/ppermute | solution.py:304
  191.5 7.7 %collective-permute-start.28 = (s16[2,528,128]{2,1,0:T(8,128)(2,1)S(1)}, s16[2,528,128]{2,1,0:T(8,128)(2,1)S(1)}, u32[]{:S(2)}, u32[]{:S(2)}) collective-permute-start(s16[2,528,128]{2,1,0:T(8,128)(2,1)S(1)} %get-tuple-element.147), channel_id=1, source_target_pairs={{0,12},{4,0},{8,4},{12,8},{1,13},{5,1},{9,5},{13,9},{2,14},{6,2},{... | collective-permute-start | bytes 811016 | tf_op jit(solution)/shard_map/ppermute | solution.py:304
  (18 other events, 138.1 us)

commit v7 on v6

--- a/solution.py
+++ b/solution.py
@@ -326,16 +326,6 @@
     lax.fori_loop(0, 4, body, 0)
 
 
-def add_second_kernel(*refs):
-    for way in range(2):
-        ahead_in, behind_in, came_a, came_b = refs[4 * way : 4 * way + 4]
-        ahead_out, behind_out = refs[8 + 2 * way : 10 + 2 * way]
-        pack(ahead_out.at[0], unpack(ahead_in.at[0]) + unpack(came_a.at[0]))
-        ahead_out[1] = ahead_in[1]
-        behind_out[0] = behind_in[0]
-        pack(behind_out.at[1], unpack(behind_in.at[1]) + unpack(came_b.at[0]))
-
-
 def whole_call(body, name, outs, *arrays, scalars=()):
     vmem = pl.BlockSpec(memory_space=pltpu.VMEM)
     size = sum(a.size * a.dtype.itemsize for a in [*arrays, *outs])
@@ -351,10 +341,9 @@
 
 
 def middle_kernel(misc_ref, one_ref, two_ref, *refs):
-    came, outs, own_ref = refs[:4], refs[4:12], refs[12]
+    came, outs, own_ref = refs[:4], refs[4:10], refs[10]
     for way, own in enumerate((one_ref, two_ref)):
         right, left = came[2 * way : 2 * way + 2]
-        far_a, far_b, ahead_ref, behind_ref = outs[4 * way : 4 * way + 4]
         for hop, ahead_by in enumerate((2, 1, 3, 0)):
             at = (misc_ref[1 - way] + ahead_by) % 4
             total = [
@@ -362,22 +351,21 @@
                 for half in range(2)
             ]
             for half in range(2):
-                if hop == 0:
-                    pack((far_a, far_b)[half].at[0], total[half])
-                elif hop < 3:
-                    pack((ahead_ref, behind_ref)[hop - 1].at[half], total[half])
+                if hop < 3:
+                    pack(outs[3 * way + hop].at[half], total[half])
                 else:
                     own_ref[pl.ds(half * HALF, HALF), pl.ds(way * 128, 128)] = total[half]
 
 
 def last_kernel(own_ref, *refs):
-    came, out_ref = refs[:4], refs[4]
+    came, out_ref = refs[:6], refs[6]
     for way in range(2):
-        right, left = came[2 * way : 2 * way + 2]
         columns = pl.ds(way * 128, 128)
         for half in range(2):
             rows = pl.ds(half * HALF, HALF)
-            total = own_ref[rows, columns] + unpack(right.at[half]) + unpack(left.at[half])
+            total = own_ref[rows, columns]
+            for ref in ((came[0], came[1], came[3]), (came[2], came[4], came[5]))[way]:
+                total += unpack(ref.at[half])
             out_ref[columns, rows] = total.T
 
 
@@ -512,9 +500,8 @@
     from_up, from_down, swapped, even, odd, tile_index, misc, third = lax.optimization_barrier(
         (from_up, from_down, swapped, even, odd, tile_index, misc, third)
     )
-    tails = from_up[half : half + EXTRA // 2], from_down[half + EXTRA // 2 :]
-    tails, from_up, from_down = lax.optimization_barrier((tails, from_up, from_down))
-    tail_up, tail_down = ahead("y", tails[0]), behind("y", tails[1])
+    tail_up = ahead("y", from_up[half : half + EXTRA // 2])
+    tail_down = behind("y", from_down[half + EXTRA // 2 :])
     tail = jax.ShapeDtypeStruct((3 * EXTRA // 2, SUB, 128), jnp.bfloat16)
     (tail,) = whole_call(tail_kernel, "tail", [tail], some, tail_up, tail_down)
     parts = [first, up, down, from_up, from_down, some[: EXTRA // 2], tail]
@@ -533,26 +520,25 @@
     for way, axis in enumerate(axes):
         came += [ahead(axis, added[2 * way]), behind(axis, added[2 * way + 1])]
     (one, two), _ = product_call("own", (0,), scalars, arrays)
-    single = jax.ShapeDtypeStruct((1, PACKED, 128), jnp.int16)
     double = jax.ShapeDtypeStruct((2, PACKED, 128), jnp.int16)
     *outs, own = whole_call(
         middle_kernel,
         "middle",
-        [single, single, double, double] * 2 + [jax.ShapeDtypeStruct((rows_dev, 256), jnp.float32)],
+        [double] * 6 + [jax.ShapeDtypeStruct((rows_dev, 256), jnp.float32)],
         one,
         two,
         *came,
         scalars=(misc,),
     )
-    axes = ("z", "x")
-    inputs = []
-    for way, axis in enumerate(axes):
-        far_a, far_b, next_ab, prev_ab = outs[4 * way : 4 * way + 4]
-        inputs += [next_ab, prev_ab, ahead(axis, far_a), behind(axis, far_b)]
-    added = whole_call(add_second_kernel, "add_second", [double] * 4, *inputs)
-    came = []
-    for way, axis in enumerate(axes):
-        came += [ahead(axis, added[2 * way]), behind(axis, added[2 * way + 1])]
+    across_axis = [(i, (i + 2) % 4) for i in range(4)]
+    came = [
+        ahead("z", outs[1]),
+        lax.ppermute(outs[0], "z", across_axis),
+        lax.ppermute(outs[3], "x", across_axis),
+        behind("z", outs[2]),
+        ahead("x", outs[4]),
+        behind("x", outs[5]),
+    ]
     return whole_call(
         last_kernel, "last", [jax.ShapeDtypeStruct((256, rows_dev), jnp.float32)], own, *came
     )[0]

time: 208 us -> 207 us (level)
  starting transfers between devices: 48.1 us -> 43.7 us
  waiting for transfers between devices: 74.8 us -> 76.9 us
    ppermute x11 -> x9, starting transfers between devices: 23.9 us -> 16.3 us  [behind(): return lax.ppermute(value, axis, [(i, (i + 3) % 4) for i in range(4)])]
    ppermute x0 -> x2, starting transfers between devices: none -> 5.94 us  [the longest x1 4.4 us: shards(): lax.ppermute(outs[0], 'z', across_axis)]
    ppermute x0 -> x2, waiting for transfers between devices: none -> 4.25 us  [the longest x1 3.48 us: shards(): lax.ppermute(outs[0], 'z', across_axis)]
    ppermute x11 -> x9, starting transfers between devices: 7.96 us -> 5.21 us  [ahead(): return lax.ppermute(value, axis, [(i, (i + 1) % 4) for i in range(4)])]
    ppermute x11 -> x9, waiting for transfers between devices: 34.7 us -> 32.4 us  [ahead(): return lax.ppermute(value, axis, [(i, (i + 1) % 4) for i in range(4)])]
    pallas_call x5 -> x4, Pallas kernels: 7.14 us -> 6.73 us  [whole_call(): pl.pallas_call(body, in_specs=[pl.BlockSpec(memory_space=pltpu.SMEM)] * l...]
    ppermute x11 -> x9, waiting for transfers between devices: 7.82 us -> 8.08 us  [behind(): return lax.ppermute(value, axis, [(i, (i + 3) % 4) for i in range(4)])]
  transfers between devices with their start and end apart: 31 -> 29, of which waited for: 12 -> 13; matrix products, arithmetic and copies ran while one was open for 3% -> 3% of each run, Pallas kernels for 13% -> 13%
where the time goes in v7:
time: 207 us; the launch traced here: 205 us
  waiting for transfers between devices  76.9 us (37%)
  Pallas kernels  53.4 us (26%)
  starting transfers between devices  43.7 us (21%)
  between operations  14.5 us (7%)
  local copies, waits for them, and re-layouts  10.5 us (5%)
  other arithmetic  3.79 us (2%)
    ppermute x9, waiting for transfers between devices, ahead(): return lax.ppermute(value, axis, [(i, (i + 1) % 4) for i in range(4)])  32.4 us
    all_to_all x2, waiting for transfers between devices, send(): lax.all_to_all(part, ('x', 'z'), split_axis=0, concat_axis=0, tiled=True)  29.9 us
    pallas_call x3, Pallas kernels, product_call(): pl.pallas_call(functools.partial(product_kernel, hops), grid_spec=pltpu.P...  25 us
    ppermute x9, starting transfers between devices, behind(): return lax.ppermute(value, axis, [(i, (i + 3) % 4) for i in range(4)])  16.3 us
    all_to_all x2, starting transfers between devices, send(): lax.all_to_all(part, ('x', 'z'), split_axis=0, concat_axis=0, tiled=True)  14.4 us
    unnamed x23, local copies, waits for them, and re-layouts  8.12 us
    ppermute x9, waiting for transfers between devices, behind(): return lax.ppermute(value, axis, [(i, (i + 3) % 4) for i in range(4)])  8.08 us
    pallas_call x4, Pallas kernels, whole_call(): pl.pallas_call(body, in_specs=[pl.BlockSpec(memory_space=pltpu.SMEM)] * l...  6.73 us
  transfers between devices with their start and end apart: 29, of which 13 were waited for; matrix products, arithmetic and copies ran while one was open for 3% of the time, Pallas kernels for 13%

profile of v7, /device:TPU:6, one launch (start us, length us, event | category | flops | bytes accessed | tf_op | source)
XLA Modules:
  0.0 204.8 jit_solution(7923461229294090782)
XLA Ops:
  9.8 4.6 %fill.1 = (bf16[128,32,128]{2,1,0:T(8,128)(2,1)S(1)}, bf16[192,32,128]{2,1,0:T(8,128)(2,1)S(1)}) custom-call(s32[16,128]{1,0:T(8,128)S(1)} %route.1.index_ref, bf16[320,32,128]{2,1,0:T(8,128)(2,1)S(1)} %bitcast.19), custom_call_target="tpu_custom_call" | custom-call | tf_op jit(solution)/shard_map/fill/pallas_call | solution.py:391
  16.6 8.3 %all-to-all-start = ((bf16[16,8,32,128]{3,2,1,0:T(8,128)(2,1)}), bf16[16,8,32,128]{3,2,1,0:T(8,128)(2,1)S(1)}, u32[]{:S(2)}, u32[]{:S(2)}) async-start(bf16[16,8,32,128]{3,2,1,0:T(8,128)(2,1)} %bitcast.26), calls=%async_computation | async-start | bytes 2097152 | tf_op jit(solution)/shard_map/all_to_all | solution.py:411
  24.9 15.2 %all-to-all-done = bf16[16,8,32,128]{3,2,1,0:T(8,128)(2,1)S(1)} async-done(((bf16[16,8,32,128]{3,2,1,0:T(8,128)(2,1)}), bf16[16,8,32,128]{3,2,1,0:T(8,128)(2,1)S(1)}, u32[]{:S(2)}, u32[]{:S(2)}) %all-to-all-start) | async-done | bytes 1048608 | tf_op jit(solution)/shard_map/all_to_all | solution.py:411
  40.1 3.0 %collective-permute-start.1 = (bf16[128,32,128]{2,1,0:T(8,128)(2,1)S(1)}, bf16[128,32,128]{2,1,0:T(8,128)(2,1)}, u32[]{:S(2)}, u32[]{:S(2)}) collective-permute-start(bf16[128,32,128]{2,1,0:T(8,128)(2,1)S(1)} %bitcast.21), channel_id=1, source_target_pairs={{0,96},{32,0},{64,32},{96,64},{1,97},{33,1},{65,33},{97,65},{2,98}... | collective-permute-start | bytes 3145736 | tf_op jit(solution)/shard_map/ppermute | solution.py:304
  43.1 6.1 %all-to-all-start.1 = ((bf16[16,12,32,128]{3,2,1,0:T(8,128)(2,1)}), bf16[16,12,32,128]{3,2,1,0:T(8,128)(2,1)S(1)}, u32[]{:S(2)}, u32[]{:S(2)}) async-start(bf16[16,12,32,128]{3,2,1,0:T(8,128)(2,1)} %bitcast.25), calls=%async_computation.1 | async-start | bytes 3145728 | tf_op jit(solution)/shard_map/all_to_all | solution.py:411
  53.5 14.7 %all-to-all-done.1 = bf16[16,12,32,128]{3,2,1,0:T(8,128)(2,1)S(1)} async-done(((bf16[16,12,32,128]{3,2,1,0:T(8,128)(2,1)}), bf16[16,12,32,128]{3,2,1,0:T(8,128)(2,1)S(1)}, u32[]{:S(2)}, u32[]{:S(2)}) %all-to-all-start.1) | async-done | bytes 1572896 | tf_op jit(solution)/shard_map/all_to_all | solution.py:411
  69.9 3.5 %join.1 = (bf16[144,32,128]{2,1,0:T(8,128)(2,1)}, bf16[144,32,128]{2,1,0:T(8,128)(2,1)}) custom-call(bf16[128,32,128]{2,1,0:T(8,128)(2,1)} %collective-permute-done.up_ref.refs_1_, bf16[128,32,128]{2,1,0:T(8,128)(2,1)} %collective-permute-done.1.down_ref.refs_2_, bf16[80,32,128]{2,1,0:T(8,128)(2,1)S(1)} %get-tuple-element.80.some_ref), custom_call_target="tpu_custom_call" | custom-call | tf_op jit(solution)/shard_map/join/pallas_call | solution.py:445
  73.8 2.9 %collective-permute-start.3 = (bf16[144,32,128]{2,1,0:T(8,128)(2,1)}, bf16[144,32,128]{2,1,0:T(8,128)(2,1)}, u32[]{:S(2)}, u32[]{:S(2)}) collective-permute-start(bf16[144,32,128]{2,1,0:T(8,128)(2,1)} %get-tuple-element.83), channel_id=1, source_target_pairs={{0,96},{32,0},{64,32},{96,64},{1,97},{33,1},{65,33},{97,65},{2,98}... | collective-permute-start | bytes 3538952 | tf_op jit(solution)/shard_map/ppermute | solution.py:304
  79.6 5.7 %prep.1 = (bf16[1024,1024]{1,0:T(8,128)(2,1)S(1)}, bf16[1024,1024]{1,0:T(8,128)(2,1)S(1)}) custom-call(s32[16,32]{1,0:T(8,128)S(1)} %copy-done.8, bf16[1024,2048]{1,0:T(8,128)(2,1)S(1)} %copy-done.2), custom_call_target="tpu_custom_call" | custom-call | tf_op jit(solution)/shard_map/prep/pallas_call | solution.py:460
  90.5 9.7 %collective-permute-done.2.refs_3_ = bf16[144,32,128]{2,1,0:T(8,128)(2,1)} collective-permute-done((bf16[144,32,128]{2,1,0:T(8,128)(2,1)}, bf16[144,32,128]{2,1,0:T(8,128)(2,1)}, u32[]{:S(2)}, u32[]{:S(2)}) %collective-permute-start.2) | collective-permute-done | bytes 1179680 | tf_op jit(solution)/shard_map/ppermute | solution.py:300
  102.2 3.0 %collective-permute-start.8 = (bf16[40,32,128]{2,1,0:T(8,128)(2,1)S(1)}, bf16[40,32,128]{2,1,0:T(8,128)(2,1)S(1)}, u32[]{:S(2)}, u32[]{:S(2)}) collective-permute-start(bf16[40,32,128]{2,1,0:T(8,128)(2,1)S(1)} %slice.11), channel_id=1, source_target_pairs={{0,96},{32,0},{64,32},{96,64},{1,97},{33,1},{65,33},{97,65},{2,98}... | collective-permute-start | bytes 983048 | tf_op jit(solution)/shard_map/ppermute | solution.py:304
  105.8 4.1 %collective-permute-done.8.down_ref = bf16[40,32,128]{2,1,0:T(8,128)(2,1)S(1)} collective-permute-done((bf16[40,32,128]{2,1,0:T(8,128)(2,1)S(1)}, bf16[40,32,128]{2,1,0:T(8,128)(2,1)S(1)}, u32[]{:S(2)}, u32[]{:S(2)}) %collective-permute-start.8) | collective-permute-done | bytes 327712 | tf_op jit(solution)/shard_map/ppermute | solution.py:304
  109.8 3.7 %collective-permute-done.7.up_ref = bf16[40,32,128]{2,1,0:T(8,128)(2,1)S(1)} collective-permute-done((bf16[40,32,128]{2,1,0:T(8,128)(2,1)S(1)}, bf16[40,32,128]{2,1,0:T(8,128)(2,1)S(1)}, u32[]{:S(2)}, u32[]{:S(2)}) %collective-permute-start.7) | collective-permute-done | bytes 327712 | tf_op jit(solution)/shard_map/ppermute | solution.py:300
  116.8 4.0 %collect.1.tiles = bf16[2561,32,128]{2,1,0:T(8,128)(2,1)S(1)} custom-call(s32[3]{0:T(128)S(1)} %pad_add_fusion.misc_ref, bf16[128,32,128]{2,1,0:T(8,128)(2,1)S(1)} %bitcast.24, bf16[128,32,128]{2,1,0:T(8,128)(2,1)} %collective-permute-done.up_ref.refs_1_, bf16[128,32,128]{2,1,0:T(8,128)(2,1)} %collective-permute-done.1.down_ref.refs_2_, ...), custom_call_target="tpu_custom_call" | custom-call | bytes 20971520 | tf_op jit(solution)/shard_map/collect/pallas_call | solution.py:214
  120.8 6.6 %far.1 = (s16[4,528,128]{2,1,0:T(8,128)(2,1)S(1)}, s16[4,528,128]{2,1,0:T(8,128)(2,1)S(1)}, s16[4,528,128]{2,1,0:T(8,128)(2,1)S(1)}, s16[4,528,128]{2,1,0:T(8,12...) custom-call(s32[2048]{0:T(1024)S(1)} %select_select_fusion.index_ref, ...), custom_call_target="tpu_custom_call", output_to_operand_aliasing={{4}: (2, {}), {5}: (3, {}), {6}: (4, {})} | custom-call | flops 4294967296 | bytes 20971520 | tf_op jit(solution)/shard_map/far/pallas_call | solution.py:279
  129.6 3.2 %collective-permute-start.16 = (s16[4,528,128]{2,1,0:T(8,128)(2,1)S(1)}, s16[4,528,128]{2,1,0:T(8,128)(2,1)S(1)}, u32[]{:S(2)}, u32[]{:S(2)}) collective-permute-start(s16[4,528,128]{2,1,0:T(8,128)(2,1)S(1)} %get-tuple-element.116), channel_id=1, source_target_pairs={{0,3},{1,0},{2,1},{3,2},{4,7},{5,4},{6,5},{7,6},{8,11},{9,8},{10,9... | collective-permute-start | bytes 1622024 | tf_op jit(solution)/shard_map/ppermute | solution.py:304
  132.8 12.3 %near.1 = (s16[2,4,528,128]{3,2,1,0:T(8,128)(2,1)S(1)}, s16[2,4,528,128]{3,2,1,0:T(8,128)(2,1)S(1)}, s16[2,4,528,128]{3,2,1,0:T(8,128)(2,1)S(1)}, s16[2,4,528,12...) custom-call(s32[2048]{0:T(1024)S(1)} %select_select_fusion.index_ref, ...), custom_call_target="tpu_custom_call", output_to_operand_aliasing={{4}: (2, {}), {5}: (3, {}), {6}: (4, {})} | custom-call | flops 8589934592 | bytes 20971520 | tf_op jit(solution)/shard_map/near/pallas_call | solution.py:279
  152.8 6.0 %own.1 = (f32[4,1024,128]{2,1,0:T(8,128)S(1)}, f32[4,1024,128]{2,1,0:T(8,128)S(1)}) custom-call(s32[2048]{0:T(1024)S(1)} %select_select_fusion.index_ref, s32[3]{0:T(128)S(1)} %pad_add_fusion.misc_ref, bf16[1024,1024]{1,0:T(8,128)(2,1)S(1)} %get-tuple-element.104.even_ref, bf16[1024,1024]{1,0:T(8,128)(2,1)S(1)} %get-tuple-element.105.odd_ref, ...), custom_call_target="tpu_custom_call" | custom-call | flops 4294967296 | bytes 20971520 | tf_op jit(solution)/shard_map/own/pallas_call | solution.py:279
  158.8 13.5 %collective-permute-done.17.refs_0_ = s16[2,4,528,128]{3,2,1,0:T(8,128)(2,1)S(1)} collective-permute-done((s16[2,4,528,128]{3,2,1,0:T(8,128)(2,1)S(1)}, s16[2,4,528,128]{3,2,1,0:T(8,128)(2,1)S(1)}, u32[]{:S(2)}, u32[]{:S(2)}) %collective-permute-start.17) | collective-permute-done | bytes 1081376 | tf_op jit(solution)/shard_map/ppermute | solution.py:300
  172.3 2.9 %collective-permute-done.18.refs_1_ = s16[2,4,528,128]{3,2,1,0:T(8,128)(2,1)S(1)} collective-permute-done((s16[2,4,528,128]{3,2,1,0:T(8,128)(2,1)S(1)}, s16[2,4,528,128]{3,2,1,0:T(8,128)(2,1)S(1)}, u32[]{:S(2)}, u32[]{:S(2)}) %collective-permute-start.18) | collective-permute-done | bytes 1081376 | tf_op jit(solution)/shard_map/ppermute | solution.py:304
  175.3 2.8 %middle.1 = (s16[2,528,128]{2,1,0:T(8,128)(2,1)S(1)}, s16[2,528,128]{2,1,0:T(8,128)(2,1)S(1)}, s16[2,528,128]{2,1,0:T(8,128)(2,1)S(1)}, s16[2,528,128]{2,1,0:T(8...) custom-call(s32[3]{0:T(128)S(1)} %pad_add_fusion.misc_ref, ...), custom_call_target="tpu_custom_call" | custom-call | flops 111902720 | bytes 11190272 | tf_op jit(solution)/shard_map/middle/pallas_call | solution.py:332
  178.2 4.4 %collective-permute-start.22 = (s16[2,528,128]{2,1,0:T(8,128)(2,1)S(1)}, s16[2,528,128]{2,1,0:T(8,128)(2,1)S(1)}, u32[]{:S(2)}, u32[]{:S(2)}) collective-permute-start(s16[2,528,128]{2,1,0:T(8,128)(2,1)S(1)} %get-tuple-element.123), channel_id=1, source_target_pairs={{0,2},{1,3},{2,0},{3,1},{4,6},{5,7},{6,4},{7,5},{8,10},{9,11},{10,... | collective-permute-start | bytes 811016 | tf_op jit(solution)/shard_map/ppermute | solution.py:536
  185.5 3.2 %collective-permute-done.21.refs_0_ = s16[2,528,128]{2,1,0:T(8,128)(2,1)S(1)} collective-permute-done((s16[2,528,128]{2,1,0:T(8,128)(2,1)S(1)}, s16[2,528,128]{2,1,0:T(8,128)(2,1)S(1)}, u32[]{:S(2)}, u32[]{:S(2)}) %collective-permute-start.21) | collective-permute-done | bytes 270368 | tf_op jit(solution)/shard_map/ppermute | solution.py:300
  188.7 3.5 %collective-permute-done.22.refs_1_ = s16[2,528,128]{2,1,0:T(8,128)(2,1)S(1)} collective-permute-done((s16[2,528,128]{2,1,0:T(8,128)(2,1)S(1)}, s16[2,528,128]{2,1,0:T(8,128)(2,1)S(1)}, u32[]{:S(2)}, u32[]{:S(2)}) %collective-permute-start.22) | collective-permute-done | bytes 270368 | tf_op jit(solution)/shard_map/ppermute | solution.py:536
  (101 shorter events, 44.5 us)
Async XLA Ops:
  16.6 23.5 %all-to-all-start = ((bf16[16,8,32,128]{3,2,1,0:T(8,128)(2,1)}), bf16[16,8,32,128]{3,2,1,0:T(8,128)(2,1)S(1)}, u32[]{:S(2)}, u32[]{:S(2)}) async-start(bf16[16,8,32,128]{3,2,1,0:T(8,128)(2,1)} %bitcast.26), calls=%async_computation | async-start | bytes 2097152 | tf_op jit(solution)/shard_map/all_to_all | solution.py:411
  40.1 29.8 %collective-permute-start.1 = (bf16[128,32,128]{2,1,0:T(8,128)(2,1)S(1)}, bf16[128,32,128]{2,1,0:T(8,128)(2,1)}, u32[]{:S(2)}, u32[]{:S(2)}) collective-permute-start(bf16[128,32,128]{2,1,0:T(8,128)(2,1)S(1)} %bitcast.21), channel_id=1, source_target_pairs={{0,96},{32,0},{64,32},{96,64},{1,97},{33,1},{65,33},{97,65},{2,98}... | collective-permute-start | bytes 3145736 | tf_op jit(solution)/shard_map/ppermute | solution.py:304
  43.1 26.8 %collective-permute-start = (bf16[128,32,128]{2,1,0:T(8,128)(2,1)S(1)}, bf16[128,32,128]{2,1,0:T(8,128)(2,1)}, u32[]{:S(2)}, u32[]{:S(2)}) collective-permute-start(bf16[128,32,128]{2,1,0:T(8,128)(2,1)S(1)} %bitcast.22), channel_id=1, source_target_pairs={{0,32},{32,64},{64,96},{96,0},{1,33},{33,65},{65,97},{97,1},{2,34}... | collective-permute-start | bytes 3145736 | tf_op jit(solution)/shard_map/ppermute | solution.py:300
  43.1 25.2 %all-to-all-start.1 = ((bf16[16,12,32,128]{3,2,1,0:T(8,128)(2,1)}), bf16[16,12,32,128]{3,2,1,0:T(8,128)(2,1)S(1)}, u32[]{:S(2)}, u32[]{:S(2)}) async-start(bf16[16,12,32,128]{3,2,1,0:T(8,128)(2,1)} %bitcast.25), calls=%async_computation.1 | async-start | bytes 3145728 | tf_op jit(solution)/shard_map/all_to_all | solution.py:411
  73.4 26.8 %collective-permute-start.2 = (bf16[144,32,128]{2,1,0:T(8,128)(2,1)}, bf16[144,32,128]{2,1,0:T(8,128)(2,1)}, u32[]{:S(2)}, u32[]{:S(2)}) collective-permute-start(bf16[144,32,128]{2,1,0:T(8,128)(2,1)} %get-tuple-element.82), channel_id=1, source_target_pairs={{0,32},{32,64},{64,96},{96,0},{1,33},{33,65},{65,97},{97,1},{2,34}... | collective-permute-start | bytes 3538952 | tf_op jit(solution)/shard_map/ppermute | solution.py:300
  73.8 26.5 %collective-permute-start.3 = (bf16[144,32,128]{2,1,0:T(8,128)(2,1)}, bf16[144,32,128]{2,1,0:T(8,128)(2,1)}, u32[]{:S(2)}, u32[]{:S(2)}) collective-permute-start(bf16[144,32,128]{2,1,0:T(8,128)(2,1)} %get-tuple-element.83), channel_id=1, source_target_pairs={{0,96},{32,0},{64,32},{96,64},{1,97},{33,1},{65,33},{97,65},{2,98}... | collective-permute-start | bytes 3538952 | tf_op jit(solution)/shard_map/ppermute | solution.py:304
  76.7 13.8 %collective-permute-start.4 = (bf16[128,32,128]{2,1,0:T(8,128)(2,1)S(1)}, bf16[128,32,128]{2,1,0:T(8,128)(2,1)}, u32[]{:S(2)}, u32[]{:S(2)}) collective-permute-start(bf16[128,32,128]{2,1,0:T(8,128)(2,1)S(1)} %bitcast.23), channel_id=1, source_target_pairs={{0,16},{16,0},{1,17},{17,1},{2,18},{18,2},{3,19},{19,3},{4,20},{20... | collective-permute-start | bytes 3145736 | tf_op jit(solution)/shard_map/ppermute | solution.py:312
  76.7 13.8 %collective-permute-start.5 = (bf16[128,32,128]{2,1,0:T(8,128)(2,1)}, bf16[128,32,128]{2,1,0:T(8,128)(2,1)}, u32[]{:S(2)}, u32[]{:S(2)}) collective-permute-start(bf16[128,32,128]{2,1,0:T(8,128)(2,1)} %collective-permute-done.up_ref.refs_1_), channel_id=1, source_target_pairs={{0,16},{16,0},{1,17},{17,1},{2,18},{18,2},{3,19},{19,3},{4,20},{20... | collective-permute-start | bytes 3145736 | tf_op jit(solution)/shard_map/ppermute | solution.py:312
  77.2 13.3 %collective-permute-start.6 = (bf16[128,32,128]{2,1,0:T(8,128)(2,1)}, bf16[128,32,128]{2,1,0:T(8,128)(2,1)}, u32[]{:S(2)}, u32[]{:S(2)}) collective-permute-start(bf16[128,32,128]{2,1,0:T(8,128)(2,1)} %collective-permute-done.1.down_ref.refs_2_), channel_id=1, source_target_pairs={{0,16},{16,0},{1,17},{17,1},{2,18},{18,2},{3,19},{19,3},{4,20},{20... | collective-permute-start | bytes 3145736 | tf_op jit(solution)/shard_map/ppermute | solution.py:312
  105.3 11.5 %collective-permute-start.9 = (bf16[144,32,128]{2,1,0:T(8,128)(2,1)}, bf16[144,32,128]{2,1,0:T(8,128)(2,1)S(1)}, u32[]{:S(2)}, u32[]{:S(2)}) collective-permute-start(bf16[144,32,128]{2,1,0:T(8,128)(2,1)} %collective-permute-done.2.refs_3_), channel_id=1, source_target_pairs={{0,16},{16,0},{1,17},{17,1},{2,18},{18,2},{3,19},{19,3},{4,20},{20... | collective-permute-start | bytes 3538952 | tf_op jit(solution)/shard_map/ppermute | solution.py:312
  105.3 11.5 %collective-permute-start.10 = (bf16[144,32,128]{2,1,0:T(8,128)(2,1)}, bf16[144,32,128]{2,1,0:T(8,128)(2,1)S(1)}, u32[]{:S(2)}, u32[]{:S(2)}) collective-permute-start(bf16[144,32,128]{2,1,0:T(8,128)(2,1)} %collective-permute-done.3.refs_4_), channel_id=1, source_target_pairs={{0,16},{16,0},{1,17},{17,1},{2,18},{18,2},{3,19},{19,3},{4,20},{20... | collective-permute-start | bytes 3538952 | tf_op jit(solution)/shard_map/ppermute | solution.py:312
  127.5 17.7 %collective-permute-start.13 = (s16[4,528,128]{2,1,0:T(8,128)(2,1)S(1)}, s16[4,528,128]{2,1,0:T(8,128)(2,1)S(1)}, u32[]{:S(2)}, u32[]{:S(2)}) collective-permute-start(s16[4,528,128]{2,1,0:T(8,128)(2,1)S(1)} %get-tuple-element.111), channel_id=1, source_target_pairs={{0,4},{4,8},{8,12},{12,0},{1,5},{5,9},{9,13},{13,1},{2,6},{6,10},{... | collective-permute-start | bytes 1622024 | tf_op jit(solution)/shard_map/ppermute | solution.py:300
  128.3 16.8 %collective-permute-start.14 = (s16[4,528,128]{2,1,0:T(8,128)(2,1)S(1)}, s16[4,528,128]{2,1,0:T(8,128)(2,1)S(1)}, u32[]{:S(2)}, u32[]{:S(2)}) collective-permute-start(s16[4,528,128]{2,1,0:T(8,128)(2,1)S(1)} %get-tuple-element.112), channel_id=1, source_target_pairs={{0,12},{4,0},{8,4},{12,8},{1,13},{5,1},{9,5},{13,9},{2,14},{6,2},{... | collective-permute-start | bytes 1622024 | tf_op jit(solution)/shard_map/ppermute | solution.py:304
  129.6 15.6 %collective-permute-start.15 = (s16[4,528,128]{2,1,0:T(8,128)(2,1)S(1)}, s16[4,528,128]{2,1,0:T(8,128)(2,1)S(1)}, u32[]{:S(2)}, u32[]{:S(2)}) collective-permute-start(s16[4,528,128]{2,1,0:T(8,128)(2,1)S(1)} %get-tuple-element.115), channel_id=1, source_target_pairs={{0,1},{1,2},{2,3},{3,0},{4,5},{5,6},{6,7},{7,4},{8,9},{9,10},{10,1... | collective-permute-start | bytes 1622024 | tf_op jit(solution)/shard_map/ppermute | solution.py:300
  129.6 15.6 %collective-permute-start.16 = (s16[4,528,128]{2,1,0:T(8,128)(2,1)S(1)}, s16[4,528,128]{2,1,0:T(8,128)(2,1)S(1)}, u32[]{:S(2)}, u32[]{:S(2)}) collective-permute-start(s16[4,528,128]{2,1,0:T(8,128)(2,1)S(1)} %get-tuple-element.116), channel_id=1, source_target_pairs={{0,3},{1,0},{2,1},{3,2},{4,7},{5,4},{6,5},{7,6},{8,11},{9,8},{10,9... | collective-permute-start | bytes 1622024 | tf_op jit(solution)/shard_map/ppermute | solution.py:304
  147.5 24.9 %collective-permute-start.17 = (s16[2,4,528,128]{3,2,1,0:T(8,128)(2,1)S(1)}, s16[2,4,528,128]{3,2,1,0:T(8,128)(2,1)S(1)}, u32[]{:S(2)}, u32[]{:S(2)}) collective-permute-start(s16[2,4,528,128]{3,2,1,0:T(8,128)(2,1)S(1)} %get-tuple-element.117), channel_id=1, source_target_pairs={{0,4},{4,8},{8,12},{12,0},{1,5},{5,9},{9,13},{13,1},{2,6},{6,10},{... | collective-permute-start | bytes 3244040 | tf_op jit(solution)/shard_map/ppermute | solution.py:300
  149.5 25.7 %collective-permute-start.18 = (s16[2,4,528,128]{3,2,1,0:T(8,128)(2,1)S(1)}, s16[2,4,528,128]{3,2,1,0:T(8,128)(2,1)S(1)}, u32[]{:S(2)}, u32[]{:S(2)}) collective-permute-start(s16[2,4,528,128]{3,2,1,0:T(8,128)(2,1)S(1)} %get-tuple-element.118), channel_id=1, source_target_pairs={{0,12},{4,0},{8,4},{12,8},{1,13},{5,1},{9,5},{13,9},{2,14},{6,2},{... | collective-permute-start | bytes 3244040 | tf_op jit(solution)/shard_map/ppermute | solution.py:304
  149.6 25.7 %collective-permute-start.19 = (s16[2,4,528,128]{3,2,1,0:T(8,128)(2,1)S(1)}, s16[2,4,528,128]{3,2,1,0:T(8,128)(2,1)S(1)}, u32[]{:S(2)}, u32[]{:S(2)}) collective-permute-start(s16[2,4,528,128]{3,2,1,0:T(8,128)(2,1)S(1)} %get-tuple-element.119), channel_id=1, source_target_pairs={{0,1},{1,2},{2,3},{3,0},{4,5},{5,6},{6,7},{7,4},{8,9},{9,10},{10,1... | collective-permute-start | bytes 3244040 | tf_op jit(solution)/shard_map/ppermute | solution.py:300
  150.0 25.2 %collective-permute-start.20 = (s16[2,4,528,128]{3,2,1,0:T(8,128)(2,1)S(1)}, s16[2,4,528,128]{3,2,1,0:T(8,128)(2,1)S(1)}, u32[]{:S(2)}, u32[]{:S(2)}) collective-permute-start(s16[2,4,528,128]{3,2,1,0:T(8,128)(2,1)S(1)} %get-tuple-element.120), channel_id=1, source_target_pairs={{0,3},{1,0},{2,1},{3,2},{4,7},{5,4},{6,5},{7,6},{8,11},{9,8},{10,9... | collective-permute-start | bytes 3244040 | tf_op jit(solution)/shard_map/ppermute | solution.py:304
  178.1 10.6 %collective-permute-start.21 = (s16[2,528,128]{2,1,0:T(8,128)(2,1)S(1)}, s16[2,528,128]{2,1,0:T(8,128)(2,1)S(1)}, u32[]{:S(2)}, u32[]{:S(2)}) collective-permute-start(s16[2,528,128]{2,1,0:T(8,128)(2,1)S(1)} %get-tuple-element.122), channel_id=1, source_target_pairs={{0,1},{1,2},{2,3},{3,0},{4,5},{5,6},{6,7},{7,4},{8,9},{9,10},{10,1... | collective-permute-start | bytes 811016 | tf_op jit(solution)/shard_map/ppermute | solution.py:300
  178.2 14.0 %collective-permute-start.22 = (s16[2,528,128]{2,1,0:T(8,128)(2,1)S(1)}, s16[2,528,128]{2,1,0:T(8,128)(2,1)S(1)}, u32[]{:S(2)}, u32[]{:S(2)}) collective-permute-start(s16[2,528,128]{2,1,0:T(8,128)(2,1)S(1)} %get-tuple-element.123), channel_id=1, source_target_pairs={{0,2},{1,3},{2,0},{3,1},{4,6},{5,7},{6,4},{7,5},{8,10},{9,11},{10,... | collective-permute-start | bytes 811016 | tf_op jit(solution)/shard_map/ppermute | solution.py:536
  182.6 10.4 %collective-permute-start.23 = (s16[2,528,128]{2,1,0:T(8,128)(2,1)S(1)}, s16[2,528,128]{2,1,0:T(8,128)(2,1)S(1)}, u32[]{:S(2)}, u32[]{:S(2)}) collective-permute-start(s16[2,528,128]{2,1,0:T(8,128)(2,1)S(1)} %get-tuple-element.124), channel_id=1, source_target_pairs={{0,8},{4,12},{8,0},{12,4},{1,9},{5,13},{9,1},{13,5},{2,10},{6,14},... | collective-permute-start | bytes 811016 | tf_op jit(solution)/shard_map/ppermute | solution.py:537
  184.1 8.9 %collective-permute-start.24 = (s16[2,528,128]{2,1,0:T(8,128)(2,1)S(1)}, s16[2,528,128]{2,1,0:T(8,128)(2,1)S(1)}, u32[]{:S(2)}, u32[]{:S(2)}) collective-permute-start(s16[2,528,128]{2,1,0:T(8,128)(2,1)S(1)} %get-tuple-element.125), channel_id=1, source_target_pairs={{0,3},{1,0},{2,1},{3,2},{4,7},{5,4},{6,5},{7,6},{8,11},{9,8},{10,9... | collective-permute-start | bytes 811016 | tf_op jit(solution)/shard_map/ppermute | solution.py:304
  184.1 11.2 %collective-permute-start.25 = (s16[2,528,128]{2,1,0:T(8,128)(2,1)S(1)}, s16[2,528,128]{2,1,0:T(8,128)(2,1)S(1)}, u32[]{:S(2)}, u32[]{:S(2)}) collective-permute-start(s16[2,528,128]{2,1,0:T(8,128)(2,1)S(1)} %get-tuple-element.126), channel_id=1, source_target_pairs={{0,4},{4,8},{8,12},{12,0},{1,5},{5,9},{9,13},{13,1},{2,6},{6,10},{... | collective-permute-start | bytes 811016 | tf_op jit(solution)/shard_map/ppermute | solution.py:300
  (16 other events, 139.9 us)

commit v8 on v7

--- a/solution.py
+++ b/solution.py
@@ -62,24 +62,18 @@
     out_ref[...] = out.astype(jnp.int32)
 
 
-def fill_kernel(index_ref, tiles_ref, first_ref, second_ref, first_filled, second_filled, sems):
-    copies = []
-    for k, (filled, out_ref, base) in enumerate(((first_filled, first_ref, 0), (second_filled, second_ref, BATCH))):
-        size = filled.shape[0] // COLS
-
-        def group(g, carry, filled=filled, size=size, base=base):
-            codes = [index_ref[g, base + j] for j in range(size)]
-            tiles = [tiles_ref[code // 2] for code in codes]
-            for j in range(size):
-                turned = jnp.concatenate([tiles[j][:, TILE:], tiles[j][:, :TILE]], axis=1)
-                filled[g * size + j] = jnp.where(codes[j] % 2 == 1, turned, tiles[j])
-            return carry
-
-        lax.fori_loop(0, COLS, group, 0)
-        copies.append(pltpu.make_async_copy(filled, out_ref, sems.at[k]))
-        copies[k].start()
-    for copy in copies:
-        copy.wait()
+def fill_kernel(base, index_ref, tiles_ref, out_ref):
+    size = out_ref.shape[0] // COLS
+
+    def group(g, carry):
+        codes = [index_ref[g, base + j] for j in range(size)]
+        tiles = [tiles_ref[code // 2] for code in codes]
+        for j in range(size):
+            turned = jnp.concatenate([tiles[j][:, TILE:], tiles[j][:, :TILE]], axis=1)
+            out_ref[g * size + j] = jnp.where(codes[j] % 2 == 1, turned, tiles[j])
+        return carry
+
+    lax.fori_loop(0, COLS, group, 0)
 
 
 def compact_kernel(index_ref, spill_ref, second_ref, some_ref, rest_ref):
@@ -388,23 +382,20 @@
         name="route",
     )(myself.reshape(1).astype(jnp.int32), eri_slot.reshape(-1, 128))
     vmem = pl.BlockSpec(memory_space=pltpu.VMEM)
-    outgoing = pl.pallas_call(
-        fill_kernel,
-        grid_spec=pltpu.PrefetchScalarGridSpec(
-            num_scalar_prefetch=1,
-            grid=(),
-            in_specs=[vmem],
-            out_specs=[pl.BlockSpec(memory_space=pltpu.HBM)] * 2,
-            scratch_shapes=[
-                pltpu.VMEM((FIRST, SUB, 128), jnp.bfloat16),
-                pltpu.VMEM((SECOND, SUB, 128), jnp.bfloat16),
-                pltpu.SemaphoreType.DMA((2,)),
-            ],
-        ),
-        out_shape=[jax.ShapeDtypeStruct((size, SUB, 128), jnp.bfloat16) for size in (FIRST, SECOND)],
-        compiler_params=pltpu.CompilerParams(vmem_limit_bytes=VMEM_GRANT),
-        name="fill",
-    )(send_index, eri_tiles.reshape(slots_dev, SUB, 128))
+    stored = eri_tiles.reshape(slots_dev, SUB, 128)
+
+    def fill(base, size):
+        return pl.pallas_call(
+            functools.partial(fill_kernel, base),
+            grid_spec=pltpu.PrefetchScalarGridSpec(
+                num_scalar_prefetch=1, grid=(), in_specs=[vmem], out_specs=vmem
+            ),
+            out_shape=jax.ShapeDtypeStruct((size, SUB, 128), jnp.bfloat16),
+            compiler_params=pltpu.CompilerParams(vmem_limit_bytes=VMEM_GRANT),
+            name="fill",
+        )(send_index, stored)
+
+    outgoing = fill(0, FIRST), fill(BATCH, SECOND)
 
     def send(part):
         part = part.reshape(COLS, -1, SUB, 128)
@@ -500,8 +491,9 @@
     from_up, from_down, swapped, even, odd, tile_index, misc, third = lax.optimization_barrier(
         (from_up, from_down, swapped, even, odd, tile_index, misc, third)
     )
-    tail_up = ahead("y", from_up[half : half + EXTRA // 2])
-    tail_down = behind("y", from_down[half + EXTRA // 2 :])
+    tails = from_up[half : half + EXTRA // 2], from_down[half + EXTRA // 2 :]
+    tails, from_up, from_down = lax.optimization_barrier((tails, from_up, from_down))
+    tail_up, tail_down = ahead("y", tails[0]), behind("y", tails[1])
     tail = jax.ShapeDtypeStruct((3 * EXTRA // 2, SUB, 128), jnp.bfloat16)
     (tail,) = whole_call(tail_kernel, "tail", [tail], some, tail_up, tail_down)
     parts = [first, up, down, from_up, from_down, some[: EXTRA // 2], tail]

time: 207 us -> 200 us (0.966)
  waiting for transfers between devices: 76.9 us -> 69.9 us
    ppermute x9, waiting for transfers between devices: 8.08 us -> 4 us  [behind(): return lax.ppermute(value, axis, [(i, (i + 3) % 4) for i in range(4)])]
    all_to_all x2, waiting for transfers between devices: 29.9 us -> 26.2 us  [send(): lax.all_to_all(part, ('x', 'z'), split_axis=0, concat_axis=0, tiled=True)]
    pallas_call x1 -> x2, Pallas kernels: 4.61 us -> 5.06 us  [fill(): pl.pallas_call(functools.partial(fill_kernel, base), grid_spec=pltpu.Pref...]
  transfers between devices with their start and end apart: 29 -> 29, of which waited for: 13 -> 12; matrix products, arithmetic and copies ran while one was open for 3% -> 3% of each run, Pallas kernels for 13% -> 15%
where the time goes in v8:
time: 200 us; the launch traced here: 198 us
  waiting for transfers between devices  69.9 us (35%)
  Pallas kernels  53.5 us (27%)
  starting transfers between devices  44 us (22%)
  between operations  14.5 us (7%)
  local copies, waits for them, and re-layouts  10.5 us (5%)
  other arithmetic  3.79 us (2%)
    ppermute x9, waiting for transfers between devices, ahead(): return lax.ppermute(value, axis, [(i, (i + 1) % 4) for i in range(4)])  33.2 us
    all_to_all x2, waiting for transfers between devices, send(): lax.all_to_all(part, ('x', 'z'), split_axis=0, concat_axis=0, tiled=True)  26.2 us
    pallas_call x3, Pallas kernels, product_call(): pl.pallas_call(functools.partial(product_kernel, hops), grid_spec=pltpu.P...  25 us
    ppermute x9, starting transfers between devices, behind(): return lax.ppermute(value, axis, [(i, (i + 3) % 4) for i in range(4)])  15.5 us
    all_to_all x2, starting transfers between devices, send(): lax.all_to_all(part, ('x', 'z'), split_axis=0, concat_axis=0, tiled=True)  14.4 us
    unnamed x23, local copies, waits for them, and re-layouts  8.11 us
    pallas_call x4, Pallas kernels, whole_call(): pl.pallas_call(body, in_specs=[pl.BlockSpec(memory_space=pltpu.SMEM)] * l...  6.72 us
    ppermute x9, starting transfers between devices, ahead(): return lax.ppermute(value, axis, [(i, (i + 1) % 4) for i in range(4)])  6.32 us
  transfers between devices with their start and end apart: 29, of which 12 were waited for; matrix products, arithmetic and copies ran while one was open for 3% of the time, Pallas kernels for 15%

profile of v8, /device:TPU:6, one launch (start us, length us, event | category | flops | bytes accessed | tf_op | source)
XLA Modules:
  0.0 198.1 jit_solution(17353643367285803506)
XLA Ops:
  6.5 2.4 %copy.13 = bf16[40,8,32,128]{3,2,1,0:T(8,128)(2,1)S(1)} copy(bf16[40,8,32,128]{3,1,2,0:T(8,128)(2,1)} %bitcast.27) | data formatting | bytes 5242880
  13.1 8.3 %all-to-all-start = ((bf16[16,8,32,128]{3,2,1,0:T(8,128)(2,1)}), bf16[16,8,32,128]{3,2,1,0:T(8,128)(2,1)}, u32[]{:S(2)}, u32[]{:S(2)}) async-start(bf16[16,8,32,128]{3,2,1,0:T(8,128)(2,1)} %bitcast.23), calls=%async_computation | async-start | bytes 2097152 | tf_op jit(solution)/shard_map/all_to_all | solution.py:402
  21.4 2.7 %fill.3 = bf16[192,32,128]{2,1,0:T(8,128)(2,1)S(1)} custom-call(s32[16,128]{1,0:T(8,128)S(1)} %route.1.index_ref, bf16[320,32,128]{2,1,0:T(8,128)(2,1)S(1)} %bitcast.20), custom_call_target="tpu_custom_call" | custom-call | tf_op jit(solution)/shard_map/fill/pallas_call | solution.py:388
  25.3 11.4 %all-to-all-done = bf16[16,8,32,128]{3,2,1,0:T(8,128)(2,1)} async-done(((bf16[16,8,32,128]{3,2,1,0:T(8,128)(2,1)}), bf16[16,8,32,128]{3,2,1,0:T(8,128)(2,1)}, u32[]{:S(2)}, u32[]{:S(2)}) %all-to-all-start) | async-done | bytes 1048608 | tf_op jit(solution)/shard_map/all_to_all | solution.py:402
  36.7 3.0 %collective-permute-start.1 = (bf16[128,32,128]{2,1,0:T(8,128)(2,1)}, bf16[128,32,128]{2,1,0:T(8,128)(2,1)S(1)}, u32[]{:S(2)}, u32[]{:S(2)}) collective-permute-start(bf16[128,32,128]{2,1,0:T(8,128)(2,1)} %bitcast.3.refs_0_), channel_id=1, source_target_pairs={{0,96},{32,0},{64,32},{96,64},{1,97},{33,1},{65,33},{97,65},{2,98}... | collective-permute-start | bytes 3145736 | tf_op jit(solution)/shard_map/ppermute | solution.py:298
  39.8 6.1 %all-to-all-start.1 = ((bf16[16,12,32,128]{3,2,1,0:T(8,128)(2,1)}), bf16[16,12,32,128]{3,2,1,0:T(8,128)(2,1)S(1)}, u32[]{:S(2)}, u32[]{:S(2)}) async-start(bf16[16,12,32,128]{3,2,1,0:T(8,128)(2,1)} %bitcast.22), calls=%async_computation.1 | async-start | bytes 3145728 | tf_op jit(solution)/shard_map/all_to_all | solution.py:402
  50.2 14.7 %all-to-all-done.1 = bf16[16,12,32,128]{3,2,1,0:T(8,128)(2,1)S(1)} async-done(((bf16[16,12,32,128]{3,2,1,0:T(8,128)(2,1)}), bf16[16,12,32,128]{3,2,1,0:T(8,128)(2,1)S(1)}, u32[]{:S(2)}, u32[]{:S(2)}) %all-to-all-start.1) | async-done | bytes 1572896 | tf_op jit(solution)/shard_map/all_to_all | solution.py:402
  66.5 3.2 %join.1 = (bf16[144,32,128]{2,1,0:T(8,128)(2,1)}, bf16[144,32,128]{2,1,0:T(8,128)(2,1)}) custom-call(bf16[128,32,128]{2,1,0:T(8,128)(2,1)} %collective-permute-done.up_ref.refs_1_, bf16[128,32,128]{2,1,0:T(8,128)(2,1)S(1)} %collective-permute-done.1.down_ref.refs_2_, bf16[80,32,128]{2,1,0:T(8,128)(2,1)S(1)} %get-tuple-element.80.some_ref), custom_call_target="tpu_custom_call" | custom-call | tf_op jit(solution)/shard_map/join/pallas_call | solution.py:436
  70.1 2.9 %collective-permute-start.3 = (bf16[144,32,128]{2,1,0:T(8,128)(2,1)}, bf16[144,32,128]{2,1,0:T(8,128)(2,1)}, u32[]{:S(2)}, u32[]{:S(2)}) collective-permute-start(bf16[144,32,128]{2,1,0:T(8,128)(2,1)} %get-tuple-element.83), channel_id=1, source_target_pairs={{0,96},{32,0},{64,32},{96,64},{1,97},{33,1},{65,33},{97,65},{2,98}... | collective-permute-start | bytes 3538952 | tf_op jit(solution)/shard_map/ppermute | solution.py:298
  75.9 5.7 %prep.1 = (bf16[1024,1024]{1,0:T(8,128)(2,1)S(1)}, bf16[1024,1024]{1,0:T(8,128)(2,1)S(1)}) custom-call(s32[16,32]{1,0:T(8,128)S(1)} %copy-done.8, bf16[1024,2048]{1,0:T(8,128)(2,1)S(1)} %copy-done.4), custom_call_target="tpu_custom_call" | custom-call | tf_op jit(solution)/shard_map/prep/pallas_call | solution.py:451
  86.9 9.7 %collective-permute-done.2.refs_3_ = bf16[144,32,128]{2,1,0:T(8,128)(2,1)} collective-permute-done((bf16[144,32,128]{2,1,0:T(8,128)(2,1)}, bf16[144,32,128]{2,1,0:T(8,128)(2,1)}, u32[]{:S(2)}, u32[]{:S(2)}) %collective-permute-start.2) | collective-permute-done | bytes 1179680 | tf_op jit(solution)/shard_map/ppermute | solution.py:294
  102.4 4.5 %collective-permute-done.7.up_ref = bf16[40,32,128]{2,1,0:T(8,128)(2,1)S(1)} collective-permute-done((bf16[40,32,128]{2,1,0:T(8,128)(2,1)S(1)}, bf16[40,32,128]{2,1,0:T(8,128)(2,1)S(1)}, u32[]{:S(2)}, u32[]{:S(2)}) %collective-permute-start.7) | collective-permute-done | bytes 327712 | tf_op jit(solution)/shard_map/ppermute | solution.py:294
  110.2 4.0 %collect.1.tiles = bf16[2561,32,128]{2,1,0:T(8,128)(2,1)S(1)} custom-call(s32[3]{0:T(128)S(1)} %pad_add_fusion.misc_ref, bf16[128,32,128]{2,1,0:T(8,128)(2,1)} %bitcast.3.refs_0_, bf16[128,32,128]{2,1,0:T(8,128)(2,1)} %collective-permute-done.up_ref.refs_1_, bf16[128,32,128]{2,1,0:T(8,128)(2,1)S(1)} %collective-permute-done.1.down_ref.refs_2_, ...), custom_call_target="tpu_custom_call" | custom-call | bytes 20971520 | tf_op jit(solution)/shard_map/collect/pallas_call | solution.py:208
  114.2 6.6 %far.1 = (s16[4,528,128]{2,1,0:T(8,128)(2,1)S(1)}, s16[4,528,128]{2,1,0:T(8,128)(2,1)S(1)}, s16[4,528,128]{2,1,0:T(8,128)(2,1)S(1)}, s16[4,528,128]{2,1,0:T(8,12...) custom-call(s32[2048]{0:T(1024)S(1)} %select_select_fusion.index_ref, ...), custom_call_target="tpu_custom_call", output_to_operand_aliasing={{4}: (2, {}), {5}: (3, {}), {6}: (4, {})} | custom-call | flops 4294967296 | bytes 20971520 | tf_op jit(solution)/shard_map/far/pallas_call | solution.py:273
  122.9 3.2 %collective-permute-start.16 = (s16[4,528,128]{2,1,0:T(8,128)(2,1)S(1)}, s16[4,528,128]{2,1,0:T(8,128)(2,1)S(1)}, u32[]{:S(2)}, u32[]{:S(2)}) collective-permute-start(s16[4,528,128]{2,1,0:T(8,128)(2,1)S(1)} %get-tuple-element.120), channel_id=1, source_target_pairs={{0,3},{1,0},{2,1},{3,2},{4,7},{5,4},{6,5},{7,6},{8,11},{9,8},{10,9... | collective-permute-start | bytes 1622024 | tf_op jit(solution)/shard_map/ppermute | solution.py:298
  126.1 12.3 %near.1 = (s16[2,4,528,128]{3,2,1,0:T(8,128)(2,1)S(1)}, s16[2,4,528,128]{3,2,1,0:T(8,128)(2,1)S(1)}, s16[2,4,528,128]{3,2,1,0:T(8,128)(2,1)S(1)}, s16[2,4,528,12...) custom-call(s32[2048]{0:T(1024)S(1)} %select_select_fusion.index_ref, ...), custom_call_target="tpu_custom_call", output_to_operand_aliasing={{4}: (2, {}), {5}: (3, {}), {6}: (4, {})} | custom-call | flops 8589934592 | bytes 20971520 | tf_op jit(solution)/shard_map/near/pallas_call | solution.py:273
  143.4 2.8 %collective-permute-start.20 = (s16[2,4,528,128]{3,2,1,0:T(8,128)(2,1)S(1)}, s16[2,4,528,128]{3,2,1,0:T(8,128)(2,1)S(1)}, u32[]{:S(2)}, u32[]{:S(2)}) collective-permute-start(s16[2,4,528,128]{3,2,1,0:T(8,128)(2,1)S(1)} %get-tuple-element.124), channel_id=1, source_target_pairs={{0,3},{1,0},{2,1},{3,2},{4,7},{5,4},{6,5},{7,6},{8,11},{9,8},{10,9... | collective-permute-start | bytes 3244040 | tf_op jit(solution)/shard_map/ppermute | solution.py:298
  146.2 6.0 %own.1 = (f32[4,1024,128]{2,1,0:T(8,128)S(1)}, f32[4,1024,128]{2,1,0:T(8,128)S(1)}) custom-call(s32[2048]{0:T(1024)S(1)} %select_select_fusion.index_ref, s32[3]{0:T(128)S(1)} %pad_add_fusion.misc_ref, bf16[1024,1024]{1,0:T(8,128)(2,1)S(1)} %get-tuple-element.108.even_ref, bf16[1024,1024]{1,0:T(8,128)(2,1)S(1)} %get-tuple-element.109.odd_ref, ...), custom_call_target="tpu_custom_call" | custom-call | flops 4294967296 | bytes 20971520 | tf_op jit(solution)/shard_map/own/pallas_call | solution.py:273
  152.2 13.5 %collective-permute-done.17.refs_0_ = s16[2,4,528,128]{3,2,1,0:T(8,128)(2,1)S(1)} collective-permute-done((s16[2,4,528,128]{3,2,1,0:T(8,128)(2,1)S(1)}, s16[2,4,528,128]{3,2,1,0:T(8,128)(2,1)S(1)}, u32[]{:S(2)}, u32[]{:S(2)}) %collective-permute-start.17) | collective-permute-done | bytes 1081376 | tf_op jit(solution)/shard_map/ppermute | solution.py:294
  165.7 2.9 %collective-permute-done.18.refs_1_ = s16[2,4,528,128]{3,2,1,0:T(8,128)(2,1)S(1)} collective-permute-done((s16[2,4,528,128]{3,2,1,0:T(8,128)(2,1)S(1)}, s16[2,4,528,128]{3,2,1,0:T(8,128)(2,1)S(1)}, u32[]{:S(2)}, u32[]{:S(2)}) %collective-permute-start.18) | collective-permute-done | bytes 1081376 | tf_op jit(solution)/shard_map/ppermute | solution.py:298
  168.6 2.8 %middle.1 = (s16[2,528,128]{2,1,0:T(8,128)(2,1)S(1)}, s16[2,528,128]{2,1,0:T(8,128)(2,1)S(1)}, s16[2,528,128]{2,1,0:T(8,128)(2,1)S(1)}, s16[2,528,128]{2,1,0:T(8...) custom-call(s32[3]{0:T(128)S(1)} %pad_add_fusion.misc_ref, ...), custom_call_target="tpu_custom_call" | custom-call | flops 111902720 | bytes 11190272 | tf_op jit(solution)/shard_map/middle/pallas_call | solution.py:326
  171.5 4.4 %collective-permute-start.22 = (s16[2,528,128]{2,1,0:T(8,128)(2,1)S(1)}, s16[2,528,128]{2,1,0:T(8,128)(2,1)S(1)}, u32[]{:S(2)}, u32[]{:S(2)}) collective-permute-start(s16[2,528,128]{2,1,0:T(8,128)(2,1)S(1)} %get-tuple-element.127), channel_id=1, source_target_pairs={{0,2},{1,3},{2,0},{3,1},{4,6},{5,7},{6,4},{7,5},{8,10},{9,11},{10,... | collective-permute-start | bytes 811016 | tf_op jit(solution)/shard_map/ppermute | solution.py:528
  178.9 3.2 %collective-permute-done.21.refs_0_ = s16[2,528,128]{2,1,0:T(8,128)(2,1)S(1)} collective-permute-done((s16[2,528,128]{2,1,0:T(8,128)(2,1)S(1)}, s16[2,528,128]{2,1,0:T(8,128)(2,1)S(1)}, u32[]{:S(2)}, u32[]{:S(2)}) %collective-permute-start.21) | collective-permute-done | bytes 270368 | tf_op jit(solution)/shard_map/ppermute | solution.py:294
  182.1 3.5 %collective-permute-done.22.refs_1_ = s16[2,528,128]{2,1,0:T(8,128)(2,1)S(1)} collective-permute-done((s16[2,528,128]{2,1,0:T(8,128)(2,1)S(1)}, s16[2,528,128]{2,1,0:T(8,128)(2,1)S(1)}, u32[]{:S(2)}, u32[]{:S(2)}) %collective-permute-start.22) | collective-permute-done | bytes 270368 | tf_op jit(solution)/shard_map/ppermute | solution.py:528
  (102 shorter events, 45.0 us)
Async XLA Ops:
  13.1 23.6 %all-to-all-start = ((bf16[16,8,32,128]{3,2,1,0:T(8,128)(2,1)}), bf16[16,8,32,128]{3,2,1,0:T(8,128)(2,1)}, u32[]{:S(2)}, u32[]{:S(2)}) async-start(bf16[16,8,32,128]{3,2,1,0:T(8,128)(2,1)} %bitcast.23), calls=%async_computation | async-start | bytes 2097152 | tf_op jit(solution)/shard_map/all_to_all | solution.py:402
  36.7 29.8 %collective-permute-start.1 = (bf16[128,32,128]{2,1,0:T(8,128)(2,1)}, bf16[128,32,128]{2,1,0:T(8,128)(2,1)S(1)}, u32[]{:S(2)}, u32[]{:S(2)}) collective-permute-start(bf16[128,32,128]{2,1,0:T(8,128)(2,1)} %bitcast.3.refs_0_), channel_id=1, source_target_pairs={{0,96},{32,0},{64,32},{96,64},{1,97},{33,1},{65,33},{97,65},{2,98}... | collective-permute-start | bytes 3145736 | tf_op jit(solution)/shard_map/ppermute | solution.py:298
  39.8 26.8 %collective-permute-start = (bf16[128,32,128]{2,1,0:T(8,128)(2,1)}, bf16[128,32,128]{2,1,0:T(8,128)(2,1)}, u32[]{:S(2)}, u32[]{:S(2)}) collective-permute-start(bf16[128,32,128]{2,1,0:T(8,128)(2,1)} %bitcast.3.refs_0_), channel_id=1, source_target_pairs={{0,32},{32,64},{64,96},{96,0},{1,33},{33,65},{65,97},{97,1},{2,34}... | collective-permute-start | bytes 3145736 | tf_op jit(solution)/shard_map/ppermute | solution.py:294
  39.8 25.2 %all-to-all-start.1 = ((bf16[16,12,32,128]{3,2,1,0:T(8,128)(2,1)}), bf16[16,12,32,128]{3,2,1,0:T(8,128)(2,1)S(1)}, u32[]{:S(2)}, u32[]{:S(2)}) async-start(bf16[16,12,32,128]{3,2,1,0:T(8,128)(2,1)} %bitcast.22), calls=%async_computation.1 | async-start | bytes 3145728 | tf_op jit(solution)/shard_map/all_to_all | solution.py:402
  69.7 26.8 %collective-permute-start.2 = (bf16[144,32,128]{2,1,0:T(8,128)(2,1)}, bf16[144,32,128]{2,1,0:T(8,128)(2,1)}, u32[]{:S(2)}, u32[]{:S(2)}) collective-permute-start(bf16[144,32,128]{2,1,0:T(8,128)(2,1)} %get-tuple-element.82), channel_id=1, source_target_pairs={{0,32},{32,64},{64,96},{96,0},{1,33},{33,65},{65,97},{97,1},{2,34}... | collective-permute-start | bytes 3538952 | tf_op jit(solution)/shard_map/ppermute | solution.py:294
  70.1 26.5 %collective-permute-start.3 = (bf16[144,32,128]{2,1,0:T(8,128)(2,1)}, bf16[144,32,128]{2,1,0:T(8,128)(2,1)}, u32[]{:S(2)}, u32[]{:S(2)}) collective-permute-start(bf16[144,32,128]{2,1,0:T(8,128)(2,1)} %get-tuple-element.83), channel_id=1, source_target_pairs={{0,96},{32,0},{64,32},{96,64},{1,97},{33,1},{65,33},{97,65},{2,98}... | collective-permute-start | bytes 3538952 | tf_op jit(solution)/shard_map/ppermute | solution.py:298
  73.0 13.8 %collective-permute-start.4 = (bf16[128,32,128]{2,1,0:T(8,128)(2,1)}, bf16[128,32,128]{2,1,0:T(8,128)(2,1)}, u32[]{:S(2)}, u32[]{:S(2)}) collective-permute-start(bf16[128,32,128]{2,1,0:T(8,128)(2,1)} %bitcast.3.refs_0_), channel_id=1, source_target_pairs={{0,16},{16,0},{1,17},{17,1},{2,18},{18,2},{3,19},{19,3},{4,20},{20... | collective-permute-start | bytes 3145736 | tf_op jit(solution)/shard_map/ppermute | solution.py:306
  73.0 13.8 %collective-permute-start.5 = (bf16[128,32,128]{2,1,0:T(8,128)(2,1)}, bf16[128,32,128]{2,1,0:T(8,128)(2,1)}, u32[]{:S(2)}, u32[]{:S(2)}) collective-permute-start(bf16[128,32,128]{2,1,0:T(8,128)(2,1)} %collective-permute-done.up_ref.refs_1_), channel_id=1, source_target_pairs={{0,16},{16,0},{1,17},{17,1},{2,18},{18,2},{3,19},{19,3},{4,20},{20... | collective-permute-start | bytes 3145736 | tf_op jit(solution)/shard_map/ppermute | solution.py:306
  73.5 13.3 %collective-permute-start.6 = (bf16[128,32,128]{2,1,0:T(8,128)(2,1)S(1)}, bf16[128,32,128]{2,1,0:T(8,128)(2,1)}, u32[]{:S(2)}, u32[]{:S(2)}) collective-permute-start(bf16[128,32,128]{2,1,0:T(8,128)(2,1)S(1)} %collective-permute-done.1.down_ref.refs_2_), channel_id=1, source_target_pairs={{0,16},{16,0},{1,17},{17,1},{2,18},{18,2},{3,19},{19,3},{4,20},{20... | collective-permute-start | bytes 3145736 | tf_op jit(solution)/shard_map/ppermute | solution.py:306
  98.6 8.4 %collective-permute-start.7 = (bf16[40,32,128]{2,1,0:T(8,128)(2,1)S(1)}, bf16[40,32,128]{2,1,0:T(8,128)(2,1)S(1)}, u32[]{:S(2)}, u32[]{:S(2)}) collective-permute-start(bf16[40,32,128]{2,1,0:T(8,128)(2,1)S(1)} %slice.9), channel_id=1, source_target_pairs={{0,32},{32,64},{64,96},{96,0},{1,33},{33,65},{65,97},{97,1},{2,34}... | collective-permute-start | bytes 983048 | tf_op jit(solution)/shard_map/ppermute | solution.py:294
  101.9 8.2 %collective-permute-start.9 = (bf16[144,32,128]{2,1,0:T(8,128)(2,1)}, bf16[144,32,128]{2,1,0:T(8,128)(2,1)S(1)}, u32[]{:S(2)}, u32[]{:S(2)}) collective-permute-start(bf16[144,32,128]{2,1,0:T(8,128)(2,1)} %collective-permute-done.2.refs_3_), channel_id=1, source_target_pairs={{0,16},{16,0},{1,17},{17,1},{2,18},{18,2},{3,19},{19,3},{4,20},{20... | collective-permute-start | bytes 3538952 | tf_op jit(solution)/shard_map/ppermute | solution.py:306
  120.8 17.7 %collective-permute-start.13 = (s16[4,528,128]{2,1,0:T(8,128)(2,1)S(1)}, s16[4,528,128]{2,1,0:T(8,128)(2,1)S(1)}, u32[]{:S(2)}, u32[]{:S(2)}) collective-permute-start(s16[4,528,128]{2,1,0:T(8,128)(2,1)S(1)} %get-tuple-element.115), channel_id=1, source_target_pairs={{0,4},{4,8},{8,12},{12,0},{1,5},{5,9},{9,13},{13,1},{2,6},{6,10},{... | collective-permute-start | bytes 1622024 | tf_op jit(solution)/shard_map/ppermute | solution.py:294
  121.7 16.8 %collective-permute-start.14 = (s16[4,528,128]{2,1,0:T(8,128)(2,1)S(1)}, s16[4,528,128]{2,1,0:T(8,128)(2,1)S(1)}, u32[]{:S(2)}, u32[]{:S(2)}) collective-permute-start(s16[4,528,128]{2,1,0:T(8,128)(2,1)S(1)} %get-tuple-element.116), channel_id=1, source_target_pairs={{0,12},{4,0},{8,4},{12,8},{1,13},{5,1},{9,5},{13,9},{2,14},{6,2},{... | collective-permute-start | bytes 1622024 | tf_op jit(solution)/shard_map/ppermute | solution.py:298
  122.9 15.6 %collective-permute-start.15 = (s16[4,528,128]{2,1,0:T(8,128)(2,1)S(1)}, s16[4,528,128]{2,1,0:T(8,128)(2,1)S(1)}, u32[]{:S(2)}, u32[]{:S(2)}) collective-permute-start(s16[4,528,128]{2,1,0:T(8,128)(2,1)S(1)} %get-tuple-element.119), channel_id=1, source_target_pairs={{0,1},{1,2},{2,3},{3,0},{4,5},{5,6},{6,7},{7,4},{8,9},{9,10},{10,1... | collective-permute-start | bytes 1622024 | tf_op jit(solution)/shard_map/ppermute | solution.py:294
  122.9 15.6 %collective-permute-start.16 = (s16[4,528,128]{2,1,0:T(8,128)(2,1)S(1)}, s16[4,528,128]{2,1,0:T(8,128)(2,1)S(1)}, u32[]{:S(2)}, u32[]{:S(2)}) collective-permute-start(s16[4,528,128]{2,1,0:T(8,128)(2,1)S(1)} %get-tuple-element.120), channel_id=1, source_target_pairs={{0,3},{1,0},{2,1},{3,2},{4,7},{5,4},{6,5},{7,6},{8,11},{9,8},{10,9... | collective-permute-start | bytes 1622024 | tf_op jit(solution)/shard_map/ppermute | solution.py:298
  140.8 24.8 %collective-permute-start.17 = (s16[2,4,528,128]{3,2,1,0:T(8,128)(2,1)S(1)}, s16[2,4,528,128]{3,2,1,0:T(8,128)(2,1)S(1)}, u32[]{:S(2)}, u32[]{:S(2)}) collective-permute-start(s16[2,4,528,128]{3,2,1,0:T(8,128)(2,1)S(1)} %get-tuple-element.121), channel_id=1, source_target_pairs={{0,4},{4,8},{8,12},{12,0},{1,5},{5,9},{9,13},{13,1},{2,6},{6,10},{... | collective-permute-start | bytes 3244040 | tf_op jit(solution)/shard_map/ppermute | solution.py:294
  142.9 25.7 %collective-permute-start.18 = (s16[2,4,528,128]{3,2,1,0:T(8,128)(2,1)S(1)}, s16[2,4,528,128]{3,2,1,0:T(8,128)(2,1)S(1)}, u32[]{:S(2)}, u32[]{:S(2)}) collective-permute-start(s16[2,4,528,128]{3,2,1,0:T(8,128)(2,1)S(1)} %get-tuple-element.122), channel_id=1, source_target_pairs={{0,12},{4,0},{8,4},{12,8},{1,13},{5,1},{9,5},{13,9},{2,14},{6,2},{... | collective-permute-start | bytes 3244040 | tf_op jit(solution)/shard_map/ppermute | solution.py:298
  142.9 25.7 %collective-permute-start.19 = (s16[2,4,528,128]{3,2,1,0:T(8,128)(2,1)S(1)}, s16[2,4,528,128]{3,2,1,0:T(8,128)(2,1)S(1)}, u32[]{:S(2)}, u32[]{:S(2)}) collective-permute-start(s16[2,4,528,128]{3,2,1,0:T(8,128)(2,1)S(1)} %get-tuple-element.123), channel_id=1, source_target_pairs={{0,1},{1,2},{2,3},{3,0},{4,5},{5,6},{6,7},{7,4},{8,9},{9,10},{10,1... | collective-permute-start | bytes 3244040 | tf_op jit(solution)/shard_map/ppermute | solution.py:294
  143.4 25.2 %collective-permute-start.20 = (s16[2,4,528,128]{3,2,1,0:T(8,128)(2,1)S(1)}, s16[2,4,528,128]{3,2,1,0:T(8,128)(2,1)S(1)}, u32[]{:S(2)}, u32[]{:S(2)}) collective-permute-start(s16[2,4,528,128]{3,2,1,0:T(8,128)(2,1)S(1)} %get-tuple-element.124), channel_id=1, source_target_pairs={{0,3},{1,0},{2,1},{3,2},{4,7},{5,4},{6,5},{7,6},{8,11},{9,8},{10,9... | collective-permute-start | bytes 3244040 | tf_op jit(solution)/shard_map/ppermute | solution.py:298
  171.4 10.6 %collective-permute-start.21 = (s16[2,528,128]{2,1,0:T(8,128)(2,1)S(1)}, s16[2,528,128]{2,1,0:T(8,128)(2,1)S(1)}, u32[]{:S(2)}, u32[]{:S(2)}) collective-permute-start(s16[2,528,128]{2,1,0:T(8,128)(2,1)S(1)} %get-tuple-element.126), channel_id=1, source_target_pairs={{0,1},{1,2},{2,3},{3,0},{4,5},{5,6},{6,7},{7,4},{8,9},{9,10},{10,1... | collective-permute-start | bytes 811016 | tf_op jit(solution)/shard_map/ppermute | solution.py:294
  171.5 14.0 %collective-permute-start.22 = (s16[2,528,128]{2,1,0:T(8,128)(2,1)S(1)}, s16[2,528,128]{2,1,0:T(8,128)(2,1)S(1)}, u32[]{:S(2)}, u32[]{:S(2)}) collective-permute-start(s16[2,528,128]{2,1,0:T(8,128)(2,1)S(1)} %get-tuple-element.127), channel_id=1, source_target_pairs={{0,2},{1,3},{2,0},{3,1},{4,6},{5,7},{6,4},{7,5},{8,10},{9,11},{10,... | collective-permute-start | bytes 811016 | tf_op jit(solution)/shard_map/ppermute | solution.py:528
  175.9 10.4 %collective-permute-start.23 = (s16[2,528,128]{2,1,0:T(8,128)(2,1)S(1)}, s16[2,528,128]{2,1,0:T(8,128)(2,1)S(1)}, u32[]{:S(2)}, u32[]{:S(2)}) collective-permute-start(s16[2,528,128]{2,1,0:T(8,128)(2,1)S(1)} %get-tuple-element.128), channel_id=1, source_target_pairs={{0,8},{4,12},{8,0},{12,4},{1,9},{5,13},{9,1},{13,5},{2,10},{6,14},... | collective-permute-start | bytes 811016 | tf_op jit(solution)/shard_map/ppermute | solution.py:529
  177.5 8.9 %collective-permute-start.24 = (s16[2,528,128]{2,1,0:T(8,128)(2,1)S(1)}, s16[2,528,128]{2,1,0:T(8,128)(2,1)S(1)}, u32[]{:S(2)}, u32[]{:S(2)}) collective-permute-start(s16[2,528,128]{2,1,0:T(8,128)(2,1)S(1)} %get-tuple-element.129), channel_id=1, source_target_pairs={{0,3},{1,0},{2,1},{3,2},{4,7},{5,4},{6,5},{7,6},{8,11},{9,8},{10,9... | collective-permute-start | bytes 811016 | tf_op jit(solution)/shard_map/ppermute | solution.py:298
  177.5 11.2 %collective-permute-start.25 = (s16[2,528,128]{2,1,0:T(8,128)(2,1)S(1)}, s16[2,528,128]{2,1,0:T(8,128)(2,1)S(1)}, u32[]{:S(2)}, u32[]{:S(2)}) collective-permute-start(s16[2,528,128]{2,1,0:T(8,128)(2,1)S(1)} %get-tuple-element.130), channel_id=1, source_target_pairs={{0,4},{4,8},{8,12},{12,0},{1,5},{5,9},{9,13},{13,1},{2,6},{6,10},{... | collective-permute-start | bytes 811016 | tf_op jit(solution)/shard_map/ppermute | solution.py:294
  (16 other events, 132.8 us)

commit v9 on v8

--- a/solution.py
+++ b/solution.py
@@ -31,7 +31,7 @@
 HALF = 512
 SHARE = 32
 PACKED = HALF + HALF // SHARE
-VMEM_GRANT = 10 * 1024 * 1024
+VMEM_GRANT = 6 * 1024 * 1024
 
 
 def route_kernel(slots_dev, me_ref, slot_ref, out_ref):
@@ -76,24 +76,7 @@
     lax.fori_loop(0, COLS, group, 0)
 
 
-def compact_kernel(index_ref, spill_ref, second_ref, some_ref, rest_ref):
-    def move(out_ref, base):
-        def body(i, carry):
-            tiles = [second_ref[index_ref[base + i * 16 + k]] for k in range(16)]
-            for k in range(16):
-                out_ref[i * 16 + k] = tiles[k]
-            return carry
-
-        lax.fori_loop(0, out_ref.shape[0] // 16, body, 0)
-
-    move(some_ref, 0)
-
-    @pl.when(spill_ref[0] > 0)
-    def _():
-        move(rest_ref, EXTRA)
-
-
-def join_kernel(up_ref, down_ref, some_ref, up_out, down_out, sems):
+def mix_kernel(index_ref, spill_ref, second_ref, up_ref, down_ref, some_ref, rest_ref, up_out, down_out, sems):
     half = FIRST // 2
     copies = [
         pltpu.make_async_copy(up_ref.at[pl.ds(0, half)], up_out.at[pl.ds(0, half)], sems.at[0]),
@@ -103,13 +86,25 @@
         copy.start()
 
     def body(i, carry):
-        tiles = [some_ref[i * 16 + k] for k in range(16)]
+        tiles = [second_ref[index_ref[i * 16 + k]] for k in range(16)]
         for k in range(16):
+            some_ref[i * 16 + k] = tiles[k]
             up_out[half + i * 16 + k] = tiles[k]
             down_out[half + i * 16 + k] = tiles[k]
         return carry
 
     lax.fori_loop(0, EXTRA // 16, body, 0)
+
+    @pl.when(spill_ref[0] > 0)
+    def _():
+        def body_rest(i, carry):
+            tiles = [second_ref[index_ref[EXTRA + i * 16 + k]] for k in range(16)]
+            for k in range(16):
+                rest_ref[i * 16 + k] = tiles[k]
+            return carry
+
+        lax.fori_loop(0, (SECOND - EXTRA) // 16, body_rest, 0)
+
     for copy in copies:
         copy.wait()
 
@@ -421,27 +416,22 @@
     source = jnp.arange(COLS, dtype=jnp.int32)[None, :] * (CAP - BATCH) + spot[:, None] - mine_start[None, :]
     source = jnp.sum(jnp.where(inside, source, 0), axis=1).astype(jnp.int32)
     spill = spill.astype(jnp.int32).reshape(1)
-    second, source, spill = lax.optimization_barrier((second, source, spill))
+    second, source, spill, up, down = lax.optimization_barrier((second, source, spill, up, down))
     half = FIRST // 2
-    some, rest = pl.pallas_call(
-        compact_kernel,
+    sizes = (EXTRA, SECOND - EXTRA, half + EXTRA, half + EXTRA)
+    some, rest, from_up, from_down = pl.pallas_call(
+        mix_kernel,
         grid_spec=pltpu.PrefetchScalarGridSpec(
-            num_scalar_prefetch=2, grid=(), in_specs=[vmem], out_specs=[vmem] * 2
+            num_scalar_prefetch=2,
+            grid=(),
+            in_specs=[vmem] * 3,
+            out_specs=[vmem] * 4,
+            scratch_shapes=[pltpu.SemaphoreType.DMA((2,))],
         ),
-        out_shape=[jax.ShapeDtypeStruct((size, SUB, 128), jnp.bfloat16) for size in (EXTRA, SECOND - EXTRA)],
+        out_shape=[jax.ShapeDtypeStruct((size, SUB, 128), jnp.bfloat16) for size in sizes],
         compiler_params=pltpu.CompilerParams(vmem_limit_bytes=VMEM_GRANT),
-        name="compact",
-    )(source, spill, second)
-    some, up, down = lax.optimization_barrier((some, up, down))
-    from_up, from_down = pl.pallas_call(
-        join_kernel,
-        in_specs=[vmem] * 3,
-        out_specs=[vmem] * 2,
-        out_shape=[jax.ShapeDtypeStruct((half + EXTRA, SUB, 128), jnp.bfloat16)] * 2,
-        scratch_shapes=[pltpu.SemaphoreType.DMA((2,))],
-        compiler_params=pltpu.CompilerParams(vmem_limit_bytes=VMEM_GRANT),
-        name="join",
-    )(up, down, some)
+        name="mix",
+    )(source, spill, second, up, down)
     wanted = lax.dynamic_slice_in_dim(eri_slot, group * GROUP, GROUP)
     from_up, up, down, amplitudes, wanted = lax.optimization_barrier((from_up, up, down, amplitudes, wanted))
     from_up, from_down = ahead("y", from_up), behind("y", from_down)

time: 200 us -> 200 us (level)
    all_to_all x2, waiting for transfers between devices: 26.2 us -> 12.2 us  [send(): lax.all_to_all(part, ('x', 'z'), split_axis=0, concat_axis=0, tiled=True)]
    ppermute x9, waiting for transfers between devices: 4 us -> 14.6 us  [behind(): return lax.ppermute(value, axis, [(i, (i + 3) % 4) for i in range(4)])]
    ppermute x9, waiting for transfers between devices: 33.2 us -> 36.7 us  [ahead(): return lax.ppermute(value, axis, [(i, (i + 1) % 4) for i in range(4)])]
    pallas_call x2 -> x1, Pallas kernels: 4.77 us -> 3.85 us  [shards(): pl.pallas_call(mix_kernel, grid_spec=pltpu.PrefetchScalarGridSpec(num_sca...]
  transfers between devices with their start and end apart: 29 -> 29, of which waited for: 12 -> 14; matrix products, arithmetic and copies ran while one was open for 3% -> 3% of each run, Pallas kernels for 15% -> 14%
where the time goes in v9:
time: 200 us; the launch traced here: 198 us
  waiting for transfers between devices  69.9 us (35%)
  Pallas kernels  52.6 us (26%)
  starting transfers between devices  43.9 us (22%)
  between operations  14.5 us (7%)
  local copies, waits for them, and re-layouts  11.3 us (6%)
  other arithmetic  3.79 us (2%)
    ppermute x9, waiting for transfers between devices, ahead(): return lax.ppermute(value, axis, [(i, (i + 1) % 4) for i in range(4)])  36.7 us
    pallas_call x3, Pallas kernels, product_call(): pl.pallas_call(functools.partial(product_kernel, hops), grid_spec=pltpu.P...  25 us
    ppermute x9, starting transfers between devices, behind(): return lax.ppermute(value, axis, [(i, (i + 3) % 4) for i in range(4)])  15.5 us
    ppermute x9, waiting for transfers between devices, behind(): return lax.ppermute(value, axis, [(i, (i + 3) % 4) for i in range(4)])  14.6 us
    all_to_all x2, starting transfers between devices, send(): lax.all_to_all(part, ('x', 'z'), split_axis=0, concat_axis=0, tiled=True)  14.4 us
    all_to_all x2, waiting for transfers between devices, send(): lax.all_to_all(part, ('x', 'z'), split_axis=0, concat_axis=0, tiled=True)  12.2 us
    unnamed x23, local copies, waits for them, and re-layouts  8.97 us
    pallas_call x4, Pallas kernels, whole_call(): pl.pallas_call(body, in_specs=[pl.BlockSpec(memory_space=pltpu.SMEM)] * l...  6.72 us
  transfers between devices with their start and end apart: 29, of which 14 were waited for; matrix products, arithmetic and copies ran while one was open for 3% of the time, Pallas kernels for 14%

profile of v9, /device:TPU:6, one launch (start us, length us, event | category | flops | bytes accessed | tf_op | source)
XLA Modules:
  0.0 198.0 jit_solution(140253407961762262)
XLA Ops:
  13.1 8.3 %all-to-all-start = ((bf16[16,8,32,128]{3,2,1,0:T(8,128)(2,1)}), bf16[16,8,32,128]{3,2,1,0:T(8,128)(2,1)}, u32[]{:S(2)}, u32[]{:S(2)}) async-start(bf16[16,8,32,128]{3,2,1,0:T(8,128)(2,1)} %bitcast.23), calls=%async_computation | async-start | bytes 2097152 | tf_op jit(solution)/shard_map/all_to_all | solution.py:397
  21.4 2.7 %fill.3 = bf16[192,32,128]{2,1,0:T(8,128)(2,1)S(1)} custom-call(s32[16,128]{1,0:T(8,128)S(1)} %route.1.index_ref, bf16[320,32,128]{2,1,0:T(8,128)(2,1)S(1)} %bitcast.20), custom_call_target="tpu_custom_call" | custom-call | tf_op jit(solution)/shard_map/fill/pallas_call | solution.py:383
  25.3 11.4 %all-to-all-done = bf16[16,8,32,128]{3,2,1,0:T(8,128)(2,1)} async-done(((bf16[16,8,32,128]{3,2,1,0:T(8,128)(2,1)}), bf16[16,8,32,128]{3,2,1,0:T(8,128)(2,1)}, u32[]{:S(2)}, u32[]{:S(2)}) %all-to-all-start) | async-done | bytes 1048608 | tf_op jit(solution)/shard_map/all_to_all | solution.py:397
  36.7 3.0 %collective-permute-start.1 = (bf16[128,32,128]{2,1,0:T(8,128)(2,1)}, bf16[128,32,128]{2,1,0:T(8,128)(2,1)S(1)}, u32[]{:S(2)}, u32[]{:S(2)}) collective-permute-start(bf16[128,32,128]{2,1,0:T(8,128)(2,1)} %bitcast.3.refs_0_), channel_id=1, source_target_pairs={{0,96},{32,0},{64,32},{96,64},{1,97},{33,1},{65,33},{97,65},{2,98}... | collective-permute-start | bytes 3145736 | tf_op jit(solution)/shard_map/ppermute | solution.py:293
  39.8 6.1 %all-to-all-start.1 = ((bf16[16,12,32,128]{3,2,1,0:T(8,128)(2,1)}), bf16[16,12,32,128]{3,2,1,0:T(8,128)(2,1)S(1)}, u32[]{:S(2)}, u32[]{:S(2)}) async-start(bf16[16,12,32,128]{3,2,1,0:T(8,128)(2,1)} %bitcast.22), calls=%async_computation.1 | async-start | bytes 3145728 | tf_op jit(solution)/shard_map/all_to_all | solution.py:397
  50.2 10.6 %collective-permute-done.1.down_ref.refs_2_ = bf16[128,32,128]{2,1,0:T(8,128)(2,1)S(1)} collective-permute-done((bf16[128,32,128]{2,1,0:T(8,128)(2,1)}, bf16[128,32,128]{2,1,0:T(8,128)(2,1)S(1)}, u32[]{:S(2)}, u32[]{:S(2)}) %collective-permute-start.1) | collective-permute-done | bytes 1048608 | tf_op jit(solution)/shard_map/ppermute | solution.py:293
  60.8 3.4 %collective-permute-done.up_ref.refs_1_ = bf16[128,32,128]{2,1,0:T(8,128)(2,1)} collective-permute-done((bf16[128,32,128]{2,1,0:T(8,128)(2,1)}, bf16[128,32,128]{2,1,0:T(8,128)(2,1)}, u32[]{:S(2)}, u32[]{:S(2)}) %collective-permute-start) | collective-permute-done | bytes 1048608 | tf_op jit(solution)/shard_map/ppermute | solution.py:289
  64.9 3.8 %mix.1 = (bf16[80,32,128]{2,1,0:T(8,128)(2,1)S(1)}, bf16[112,32,128]{2,1,0:T(8,128)(2,1)}, bf16[144,32,128]{2,1,0:T(8,128)(2,1)}, bf16[144,32,128]{2,1,0:T(8,128)(2,1)}) custom-call(s32[192]{0:T(256)S(1)} %select_reduce_fusion.2.index_ref, s32[1]{0:T(128)} %bitcast.9.spill_ref, bf16[192,32,128]{2,1,0:T(8,128)(2,1)S(1)} %bitcast.21, ...), custom_call_target="tpu_custom_call" | custom-call | tf_op jit(solution)/shard_map/mix/pallas_call | solution.py:422
  70.0 2.9 %collective-permute-start.3 = (bf16[144,32,128]{2,1,0:T(8,128)(2,1)}, bf16[144,32,128]{2,1,0:T(8,128)(2,1)}, u32[]{:S(2)}, u32[]{:S(2)}) collective-permute-start(bf16[144,32,128]{2,1,0:T(8,128)(2,1)} %get-tuple-element.80), channel_id=1, source_target_pairs={{0,96},{32,0},{64,32},{96,64},{1,97},{33,1},{65,33},{97,65},{2,98}... | collective-permute-start | bytes 3538952 | tf_op jit(solution)/shard_map/ppermute | solution.py:293
  75.8 5.7 %prep.1 = (bf16[1024,1024]{1,0:T(8,128)(2,1)S(1)}, bf16[1024,1024]{1,0:T(8,128)(2,1)S(1)}) custom-call(s32[16,32]{1,0:T(8,128)S(1)} %copy-done.8, bf16[1024,2048]{1,0:T(8,128)(2,1)S(1)} %copy-done.4), custom_call_target="tpu_custom_call" | custom-call | tf_op jit(solution)/shard_map/prep/pallas_call | solution.py:441
  86.7 9.7 %collective-permute-done.2.refs_3_ = bf16[144,32,128]{2,1,0:T(8,128)(2,1)} collective-permute-done((bf16[144,32,128]{2,1,0:T(8,128)(2,1)}, bf16[144,32,128]{2,1,0:T(8,128)(2,1)}, u32[]{:S(2)}, u32[]{:S(2)}) %collective-permute-start.2) | collective-permute-done | bytes 1179680 | tf_op jit(solution)/shard_map/ppermute | solution.py:289
  102.2 4.5 %collective-permute-done.7.up_ref = bf16[40,32,128]{2,1,0:T(8,128)(2,1)S(1)} collective-permute-done((bf16[40,32,128]{2,1,0:T(8,128)(2,1)S(1)}, bf16[40,32,128]{2,1,0:T(8,128)(2,1)S(1)}, u32[]{:S(2)}, u32[]{:S(2)}) %collective-permute-start.7) | collective-permute-done | bytes 327712 | tf_op jit(solution)/shard_map/ppermute | solution.py:289
  110.0 4.0 %collect.1.tiles = bf16[2561,32,128]{2,1,0:T(8,128)(2,1)S(1)} custom-call(s32[3]{0:T(128)S(1)} %pad_add_fusion.misc_ref, bf16[128,32,128]{2,1,0:T(8,128)(2,1)} %bitcast.3.refs_0_, bf16[128,32,128]{2,1,0:T(8,128)(2,1)} %collective-permute-done.up_ref.refs_1_, bf16[128,32,128]{2,1,0:T(8,128)(2,1)S(1)} %collective-permute-done.1.down_ref.refs_2_, ...), custom_call_target="tpu_custom_call" | custom-call | bytes 20971520 | tf_op jit(solution)/shard_map/collect/pallas_call | solution.py:203
  114.0 6.6 %far.1 = (s16[4,528,128]{2,1,0:T(8,128)(2,1)S(1)}, s16[4,528,128]{2,1,0:T(8,128)(2,1)S(1)}, s16[4,528,128]{2,1,0:T(8,128)(2,1)S(1)}, s16[4,528,128]{2,1,0:T(8,12...) custom-call(s32[2048]{0:T(1024)S(1)} %select_select_fusion.index_ref, ...), custom_call_target="tpu_custom_call", output_to_operand_aliasing={{4}: (2, {}), {5}: (3, {}), {6}: (4, {})} | custom-call | flops 4294967296 | bytes 20971520 | tf_op jit(solution)/shard_map/far/pallas_call | solution.py:268
  122.8 3.2 %collective-permute-start.16 = (s16[4,528,128]{2,1,0:T(8,128)(2,1)S(1)}, s16[4,528,128]{2,1,0:T(8,128)(2,1)S(1)}, u32[]{:S(2)}, u32[]{:S(2)}) collective-permute-start(s16[4,528,128]{2,1,0:T(8,128)(2,1)S(1)} %get-tuple-element.118), channel_id=1, source_target_pairs={{0,3},{1,0},{2,1},{3,2},{4,7},{5,4},{6,5},{7,6},{8,11},{9,8},{10,9... | collective-permute-start | bytes 1622024 | tf_op jit(solution)/shard_map/ppermute | solution.py:293
  126.0 12.3 %near.1 = (s16[2,4,528,128]{3,2,1,0:T(8,128)(2,1)S(1)}, s16[2,4,528,128]{3,2,1,0:T(8,128)(2,1)S(1)}, s16[2,4,528,128]{3,2,1,0:T(8,128)(2,1)S(1)}, s16[2,4,528,12...) custom-call(s32[2048]{0:T(1024)S(1)} %select_select_fusion.index_ref, ...), custom_call_target="tpu_custom_call", output_to_operand_aliasing={{4}: (2, {}), {5}: (3, {}), {6}: (4, {})} | custom-call | flops 8589934592 | bytes 20971520 | tf_op jit(solution)/shard_map/near/pallas_call | solution.py:268
  143.2 2.8 %collective-permute-start.20 = (s16[2,4,528,128]{3,2,1,0:T(8,128)(2,1)S(1)}, s16[2,4,528,128]{3,2,1,0:T(8,128)(2,1)S(1)}, u32[]{:S(2)}, u32[]{:S(2)}) collective-permute-start(s16[2,4,528,128]{3,2,1,0:T(8,128)(2,1)S(1)} %get-tuple-element.122), channel_id=1, source_target_pairs={{0,3},{1,0},{2,1},{3,2},{4,7},{5,4},{6,5},{7,6},{8,11},{9,8},{10,9... | collective-permute-start | bytes 3244040 | tf_op jit(solution)/shard_map/ppermute | solution.py:293
  146.0 6.0 %own.1 = (f32[4,1024,128]{2,1,0:T(8,128)S(1)}, f32[4,1024,128]{2,1,0:T(8,128)S(1)}) custom-call(s32[2048]{0:T(1024)S(1)} %select_select_fusion.index_ref, s32[3]{0:T(128)S(1)} %pad_add_fusion.misc_ref, bf16[1024,1024]{1,0:T(8,128)(2,1)S(1)} %get-tuple-element.106.even_ref, bf16[1024,1024]{1,0:T(8,128)(2,1)S(1)} %get-tuple-element.107.odd_ref, ...), custom_call_target="tpu_custom_call" | custom-call | flops 4294967296 | bytes 20971520 | tf_op jit(solution)/shard_map/own/pallas_call | solution.py:268
  152.0 13.5 %collective-permute-done.17.refs_0_ = s16[2,4,528,128]{3,2,1,0:T(8,128)(2,1)S(1)} collective-permute-done((s16[2,4,528,128]{3,2,1,0:T(8,128)(2,1)S(1)}, s16[2,4,528,128]{3,2,1,0:T(8,128)(2,1)S(1)}, u32[]{:S(2)}, u32[]{:S(2)}) %collective-permute-start.17) | collective-permute-done | bytes 1081376 | tf_op jit(solution)/shard_map/ppermute | solution.py:289
  165.5 2.9 %collective-permute-done.18.refs_1_ = s16[2,4,528,128]{3,2,1,0:T(8,128)(2,1)S(1)} collective-permute-done((s16[2,4,528,128]{3,2,1,0:T(8,128)(2,1)S(1)}, s16[2,4,528,128]{3,2,1,0:T(8,128)(2,1)S(1)}, u32[]{:S(2)}, u32[]{:S(2)}) %collective-permute-start.18) | collective-permute-done | bytes 1081376 | tf_op jit(solution)/shard_map/ppermute | solution.py:293
  168.5 2.8 %middle.1 = (s16[2,528,128]{2,1,0:T(8,128)(2,1)S(1)}, s16[2,528,128]{2,1,0:T(8,128)(2,1)S(1)}, s16[2,528,128]{2,1,0:T(8,128)(2,1)S(1)}, s16[2,528,128]{2,1,0:T(8...) custom-call(s32[3]{0:T(128)S(1)} %pad_add_fusion.misc_ref, ...), custom_call_target="tpu_custom_call" | custom-call | flops 111902720 | bytes 11190272 | tf_op jit(solution)/shard_map/middle/pallas_call | solution.py:321
  171.4 4.4 %collective-permute-start.22 = (s16[2,528,128]{2,1,0:T(8,128)(2,1)S(1)}, s16[2,528,128]{2,1,0:T(8,128)(2,1)S(1)}, u32[]{:S(2)}, u32[]{:S(2)}) collective-permute-start(s16[2,528,128]{2,1,0:T(8,128)(2,1)S(1)} %get-tuple-element.125), channel_id=1, source_target_pairs={{0,2},{1,3},{2,0},{3,1},{4,6},{5,7},{6,4},{7,5},{8,10},{9,11},{10,... | collective-permute-start | bytes 811016 | tf_op jit(solution)/shard_map/ppermute | solution.py:518
  178.7 3.2 %collective-permute-done.21.refs_0_ = s16[2,528,128]{2,1,0:T(8,128)(2,1)S(1)} collective-permute-done((s16[2,528,128]{2,1,0:T(8,128)(2,1)S(1)}, s16[2,528,128]{2,1,0:T(8,128)(2,1)S(1)}, u32[]{:S(2)}, u32[]{:S(2)}) %collective-permute-start.21) | collective-permute-done | bytes 270368 | tf_op jit(solution)/shard_map/ppermute | solution.py:289
  181.9 3.5 %collective-permute-done.22.refs_1_ = s16[2,528,128]{2,1,0:T(8,128)(2,1)S(1)} collective-permute-done((s16[2,528,128]{2,1,0:T(8,128)(2,1)S(1)}, s16[2,528,128]{2,1,0:T(8,128)(2,1)S(1)}, u32[]{:S(2)}, u32[]{:S(2)}) %collective-permute-start.22) | collective-permute-done | bytes 270368 | tf_op jit(solution)/shard_map/ppermute | solution.py:518
  (101 shorter events, 47.2 us)
Async XLA Ops:
  13.1 23.6 %all-to-all-start = ((bf16[16,8,32,128]{3,2,1,0:T(8,128)(2,1)}), bf16[16,8,32,128]{3,2,1,0:T(8,128)(2,1)}, u32[]{:S(2)}, u32[]{:S(2)}) async-start(bf16[16,8,32,128]{3,2,1,0:T(8,128)(2,1)} %bitcast.23), calls=%async_computation | async-start | bytes 2097152 | tf_op jit(solution)/shard_map/all_to_all | solution.py:397
  36.7 24.1 %collective-permute-start.1 = (bf16[128,32,128]{2,1,0:T(8,128)(2,1)}, bf16[128,32,128]{2,1,0:T(8,128)(2,1)S(1)}, u32[]{:S(2)}, u32[]{:S(2)}) collective-permute-start(bf16[128,32,128]{2,1,0:T(8,128)(2,1)} %bitcast.3.refs_0_), channel_id=1, source_target_pairs={{0,96},{32,0},{64,32},{96,64},{1,97},{33,1},{65,33},{97,65},{2,98}... | collective-permute-start | bytes 3145736 | tf_op jit(solution)/shard_map/ppermute | solution.py:293
  39.8 24.5 %collective-permute-start = (bf16[128,32,128]{2,1,0:T(8,128)(2,1)}, bf16[128,32,128]{2,1,0:T(8,128)(2,1)}, u32[]{:S(2)}, u32[]{:S(2)}) collective-permute-start(bf16[128,32,128]{2,1,0:T(8,128)(2,1)} %bitcast.3.refs_0_), channel_id=1, source_target_pairs={{0,32},{32,64},{64,96},{96,0},{1,33},{33,65},{65,97},{97,1},{2,34}... | collective-permute-start | bytes 3145736 | tf_op jit(solution)/shard_map/ppermute | solution.py:289
  39.8 25.2 %all-to-all-start.1 = ((bf16[16,12,32,128]{3,2,1,0:T(8,128)(2,1)}), bf16[16,12,32,128]{3,2,1,0:T(8,128)(2,1)S(1)}, u32[]{:S(2)}, u32[]{:S(2)}) async-start(bf16[16,12,32,128]{3,2,1,0:T(8,128)(2,1)} %bitcast.22), calls=%async_computation.1 | async-start | bytes 3145728 | tf_op jit(solution)/shard_map/all_to_all | solution.py:397
  69.7 26.8 %collective-permute-start.2 = (bf16[144,32,128]{2,1,0:T(8,128)(2,1)}, bf16[144,32,128]{2,1,0:T(8,128)(2,1)}, u32[]{:S(2)}, u32[]{:S(2)}) collective-permute-start(bf16[144,32,128]{2,1,0:T(8,128)(2,1)} %get-tuple-element.79), channel_id=1, source_target_pairs={{0,32},{32,64},{64,96},{96,0},{1,33},{33,65},{65,97},{97,1},{2,34}... | collective-permute-start | bytes 3538952 | tf_op jit(solution)/shard_map/ppermute | solution.py:289
  70.0 26.5 %collective-permute-start.3 = (bf16[144,32,128]{2,1,0:T(8,128)(2,1)}, bf16[144,32,128]{2,1,0:T(8,128)(2,1)}, u32[]{:S(2)}, u32[]{:S(2)}) collective-permute-start(bf16[144,32,128]{2,1,0:T(8,128)(2,1)} %get-tuple-element.80), channel_id=1, source_target_pairs={{0,96},{32,0},{64,32},{96,64},{1,97},{33,1},{65,33},{97,65},{2,98}... | collective-permute-start | bytes 3538952 | tf_op jit(solution)/shard_map/ppermute | solution.py:293
  72.9 13.8 %collective-permute-start.4 = (bf16[128,32,128]{2,1,0:T(8,128)(2,1)}, bf16[128,32,128]{2,1,0:T(8,128)(2,1)}, u32[]{:S(2)}, u32[]{:S(2)}) collective-permute-start(bf16[128,32,128]{2,1,0:T(8,128)(2,1)} %bitcast.3.refs_0_), channel_id=1, source_target_pairs={{0,16},{16,0},{1,17},{17,1},{2,18},{18,2},{3,19},{19,3},{4,20},{20... | collective-permute-start | bytes 3145736 | tf_op jit(solution)/shard_map/ppermute | solution.py:301
  72.9 13.8 %collective-permute-start.5 = (bf16[128,32,128]{2,1,0:T(8,128)(2,1)}, bf16[128,32,128]{2,1,0:T(8,128)(2,1)}, u32[]{:S(2)}, u32[]{:S(2)}) collective-permute-start(bf16[128,32,128]{2,1,0:T(8,128)(2,1)} %collective-permute-done.up_ref.refs_1_), channel_id=1, source_target_pairs={{0,16},{16,0},{1,17},{17,1},{2,18},{18,2},{3,19},{19,3},{4,20},{20... | collective-permute-start | bytes 3145736 | tf_op jit(solution)/shard_map/ppermute | solution.py:301
  73.4 13.3 %collective-permute-start.6 = (bf16[128,32,128]{2,1,0:T(8,128)(2,1)S(1)}, bf16[128,32,128]{2,1,0:T(8,128)(2,1)}, u32[]{:S(2)}, u32[]{:S(2)}) collective-permute-start(bf16[128,32,128]{2,1,0:T(8,128)(2,1)S(1)} %collective-permute-done.1.down_ref.refs_2_), channel_id=1, source_target_pairs={{0,16},{16,0},{1,17},{17,1},{2,18},{18,2},{3,19},{19,3},{4,20},{20... | collective-permute-start | bytes 3145736 | tf_op jit(solution)/shard_map/ppermute | solution.py:301
  98.4 8.4 %collective-permute-start.7 = (bf16[40,32,128]{2,1,0:T(8,128)(2,1)S(1)}, bf16[40,32,128]{2,1,0:T(8,128)(2,1)S(1)}, u32[]{:S(2)}, u32[]{:S(2)}) collective-permute-start(bf16[40,32,128]{2,1,0:T(8,128)(2,1)S(1)} %slice.9), channel_id=1, source_target_pairs={{0,32},{32,64},{64,96},{96,0},{1,33},{33,65},{65,97},{97,1},{2,34}... | collective-permute-start | bytes 983048 | tf_op jit(solution)/shard_map/ppermute | solution.py:289
  101.7 8.2 %collective-permute-start.9 = (bf16[144,32,128]{2,1,0:T(8,128)(2,1)}, bf16[144,32,128]{2,1,0:T(8,128)(2,1)S(1)}, u32[]{:S(2)}, u32[]{:S(2)}) collective-permute-start(bf16[144,32,128]{2,1,0:T(8,128)(2,1)} %collective-permute-done.2.refs_3_), channel_id=1, source_target_pairs={{0,16},{16,0},{1,17},{17,1},{2,18},{18,2},{3,19},{19,3},{4,20},{20... | collective-permute-start | bytes 3538952 | tf_op jit(solution)/shard_map/ppermute | solution.py:301
  120.7 17.7 %collective-permute-start.13 = (s16[4,528,128]{2,1,0:T(8,128)(2,1)S(1)}, s16[4,528,128]{2,1,0:T(8,128)(2,1)S(1)}, u32[]{:S(2)}, u32[]{:S(2)}) collective-permute-start(s16[4,528,128]{2,1,0:T(8,128)(2,1)S(1)} %get-tuple-element.113), channel_id=1, source_target_pairs={{0,4},{4,8},{8,12},{12,0},{1,5},{5,9},{9,13},{13,1},{2,6},{6,10},{... | collective-permute-start | bytes 1622024 | tf_op jit(solution)/shard_map/ppermute | solution.py:289
  121.5 16.8 %collective-permute-start.14 = (s16[4,528,128]{2,1,0:T(8,128)(2,1)S(1)}, s16[4,528,128]{2,1,0:T(8,128)(2,1)S(1)}, u32[]{:S(2)}, u32[]{:S(2)}) collective-permute-start(s16[4,528,128]{2,1,0:T(8,128)(2,1)S(1)} %get-tuple-element.114), channel_id=1, source_target_pairs={{0,12},{4,0},{8,4},{12,8},{1,13},{5,1},{9,5},{13,9},{2,14},{6,2},{... | collective-permute-start | bytes 1622024 | tf_op jit(solution)/shard_map/ppermute | solution.py:293
  122.8 15.6 %collective-permute-start.15 = (s16[4,528,128]{2,1,0:T(8,128)(2,1)S(1)}, s16[4,528,128]{2,1,0:T(8,128)(2,1)S(1)}, u32[]{:S(2)}, u32[]{:S(2)}) collective-permute-start(s16[4,528,128]{2,1,0:T(8,128)(2,1)S(1)} %get-tuple-element.117), channel_id=1, source_target_pairs={{0,1},{1,2},{2,3},{3,0},{4,5},{5,6},{6,7},{7,4},{8,9},{9,10},{10,1... | collective-permute-start | bytes 1622024 | tf_op jit(solution)/shard_map/ppermute | solution.py:289
  122.8 15.6 %collective-permute-start.16 = (s16[4,528,128]{2,1,0:T(8,128)(2,1)S(1)}, s16[4,528,128]{2,1,0:T(8,128)(2,1)S(1)}, u32[]{:S(2)}, u32[]{:S(2)}) collective-permute-start(s16[4,528,128]{2,1,0:T(8,128)(2,1)S(1)} %get-tuple-element.118), channel_id=1, source_target_pairs={{0,3},{1,0},{2,1},{3,2},{4,7},{5,4},{6,5},{7,6},{8,11},{9,8},{10,9... | collective-permute-start | bytes 1622024 | tf_op jit(solution)/shard_map/ppermute | solution.py:293
  140.7 24.9 %collective-permute-start.17 = (s16[2,4,528,128]{3,2,1,0:T(8,128)(2,1)S(1)}, s16[2,4,528,128]{3,2,1,0:T(8,128)(2,1)S(1)}, u32[]{:S(2)}, u32[]{:S(2)}) collective-permute-start(s16[2,4,528,128]{3,2,1,0:T(8,128)(2,1)S(1)} %get-tuple-element.119), channel_id=1, source_target_pairs={{0,4},{4,8},{8,12},{12,0},{1,5},{5,9},{9,13},{13,1},{2,6},{6,10},{... | collective-permute-start | bytes 3244040 | tf_op jit(solution)/shard_map/ppermute | solution.py:289
  142.7 25.7 %collective-permute-start.18 = (s16[2,4,528,128]{3,2,1,0:T(8,128)(2,1)S(1)}, s16[2,4,528,128]{3,2,1,0:T(8,128)(2,1)S(1)}, u32[]{:S(2)}, u32[]{:S(2)}) collective-permute-start(s16[2,4,528,128]{3,2,1,0:T(8,128)(2,1)S(1)} %get-tuple-element.120), channel_id=1, source_target_pairs={{0,12},{4,0},{8,4},{12,8},{1,13},{5,1},{9,5},{13,9},{2,14},{6,2},{... | collective-permute-start | bytes 3244040 | tf_op jit(solution)/shard_map/ppermute | solution.py:293
  142.8 25.7 %collective-permute-start.19 = (s16[2,4,528,128]{3,2,1,0:T(8,128)(2,1)S(1)}, s16[2,4,528,128]{3,2,1,0:T(8,128)(2,1)S(1)}, u32[]{:S(2)}, u32[]{:S(2)}) collective-permute-start(s16[2,4,528,128]{3,2,1,0:T(8,128)(2,1)S(1)} %get-tuple-element.121), channel_id=1, source_target_pairs={{0,1},{1,2},{2,3},{3,0},{4,5},{5,6},{6,7},{7,4},{8,9},{9,10},{10,1... | collective-permute-start | bytes 3244040 | tf_op jit(solution)/shard_map/ppermute | solution.py:289
  143.2 25.2 %collective-permute-start.20 = (s16[2,4,528,128]{3,2,1,0:T(8,128)(2,1)S(1)}, s16[2,4,528,128]{3,2,1,0:T(8,128)(2,1)S(1)}, u32[]{:S(2)}, u32[]{:S(2)}) collective-permute-start(s16[2,4,528,128]{3,2,1,0:T(8,128)(2,1)S(1)} %get-tuple-element.122), channel_id=1, source_target_pairs={{0,3},{1,0},{2,1},{3,2},{4,7},{5,4},{6,5},{7,6},{8,11},{9,8},{10,9... | collective-permute-start | bytes 3244040 | tf_op jit(solution)/shard_map/ppermute | solution.py:293
  171.3 10.6 %collective-permute-start.21 = (s16[2,528,128]{2,1,0:T(8,128)(2,1)S(1)}, s16[2,528,128]{2,1,0:T(8,128)(2,1)S(1)}, u32[]{:S(2)}, u32[]{:S(2)}) collective-permute-start(s16[2,528,128]{2,1,0:T(8,128)(2,1)S(1)} %get-tuple-element.124), channel_id=1, source_target_pairs={{0,1},{1,2},{2,3},{3,0},{4,5},{5,6},{6,7},{7,4},{8,9},{9,10},{10,1... | collective-permute-start | bytes 811016 | tf_op jit(solution)/shard_map/ppermute | solution.py:289
  171.4 14.1 %collective-permute-start.22 = (s16[2,528,128]{2,1,0:T(8,128)(2,1)S(1)}, s16[2,528,128]{2,1,0:T(8,128)(2,1)S(1)}, u32[]{:S(2)}, u32[]{:S(2)}) collective-permute-start(s16[2,528,128]{2,1,0:T(8,128)(2,1)S(1)} %get-tuple-element.125), channel_id=1, source_target_pairs={{0,2},{1,3},{2,0},{3,1},{4,6},{5,7},{6,4},{7,5},{8,10},{9,11},{10,... | collective-permute-start | bytes 811016 | tf_op jit(solution)/shard_map/ppermute | solution.py:518
  175.8 10.4 %collective-permute-start.23 = (s16[2,528,128]{2,1,0:T(8,128)(2,1)S(1)}, s16[2,528,128]{2,1,0:T(8,128)(2,1)S(1)}, u32[]{:S(2)}, u32[]{:S(2)}) collective-permute-start(s16[2,528,128]{2,1,0:T(8,128)(2,1)S(1)} %get-tuple-element.126), channel_id=1, source_target_pairs={{0,8},{4,12},{8,0},{12,4},{1,9},{5,13},{9,1},{13,5},{2,10},{6,14},... | collective-permute-start | bytes 811016 | tf_op jit(solution)/shard_map/ppermute | solution.py:519
  177.3 8.9 %collective-permute-start.24 = (s16[2,528,128]{2,1,0:T(8,128)(2,1)S(1)}, s16[2,528,128]{2,1,0:T(8,128)(2,1)S(1)}, u32[]{:S(2)}, u32[]{:S(2)}) collective-permute-start(s16[2,528,128]{2,1,0:T(8,128)(2,1)S(1)} %get-tuple-element.127), channel_id=1, source_target_pairs={{0,3},{1,0},{2,1},{3,2},{4,7},{5,4},{6,5},{7,6},{8,11},{9,8},{10,9... | collective-permute-start | bytes 811016 | tf_op jit(solution)/shard_map/ppermute | solution.py:293
  177.3 11.2 %collective-permute-start.25 = (s16[2,528,128]{2,1,0:T(8,128)(2,1)S(1)}, s16[2,528,128]{2,1,0:T(8,128)(2,1)S(1)}, u32[]{:S(2)}, u32[]{:S(2)}) collective-permute-start(s16[2,528,128]{2,1,0:T(8,128)(2,1)S(1)} %get-tuple-element.128), channel_id=1, source_target_pairs={{0,4},{4,8},{8,12},{12,0},{1,5},{5,9},{9,13},{13,1},{2,6},{6,10},{... | collective-permute-start | bytes 811016 | tf_op jit(solution)/shard_map/ppermute | solution.py:289
  (16 other events, 145.9 us)
